TPU v7x, 32 devices: a whole 2x2x4 slice. The times are simulated.
32 devices in a mesh: slab: 4 (over z), grp: 8 (over y, x, core).
Axes of the slice: x: 2, y: 2, z: 4, core: 2. Of those that a mesh axis runs over, the one named last changes fastest.
Arguments:
- coords: float32 [3, 262144], P(None, ('slab', 'grp')), may hold values from -1 to 1
- charges: float32 [262144], P(('slab', 'grp')), may hold values from -1.5 to 1.5
- multipoles: float32 [121, 16384], P(None, ('slab', 'grp')), may hold values from -6 to 6
- operators: float32 [8, 121, 121], replicated, may hold values from -0.5 to 0.5
- send_list: int32 [32, 128], P(('slab', 'grp')), may hold values from 0 to 511
- near_list: int32 [16384, 8], P(('slab', 'grp')), may hold values from 0 to 1535
- m2l_source: int32 [32, 4096], P(('slab', 'grp')), may hold values from 0 to 127
- m2l_target: int32 [32, 4096], P(('slab', 'grp')), may hold values from 0 to 512, as said below
- m2l_operator: int32 [32, 4096], P(('slab', 'grp')), may hold values from 0 to 7
Outputs:
- local_exp: float32 [121, 16384], P(None, ('slab', 'grp'))
- near_potential: float32 [262144], P(('slab', 'grp'))
Inputs may be any that keep to these rules, and one draw needn't show every extreme that they name: `m2l_target`: entries past a block's count of used slots hold 512, an empty slot; the first block uses all 4096 slots.
All inputs are finite; a program needn't handle non-finite values.
Results may differ from a plain program's by a relative error of at most 0.00011.
Values sent between devices are 32-bit elements; how exact they have to be, the bound alone decides.
No kernel may reach another device: no remote copies, remote signals or barrier semaphores. Data moves between devices by JAX's collectives and lax.ppermute only.
A program may use at most 64 MiB of HBM per device.

v0:
```python
import jax
import jax.numpy as jnp
from jax import lax
from jax.sharding import PartitionSpec as P

SOFT2 = 0.0625


def padded(cells, sides, width):
    for axis, dim in sides:
        count = lax.axis_size(axis)
        ends = count - 1
        head = lax.slice_in_dim(cells, 0, width, axis=dim)
        tail = lax.slice_in_dim(cells, cells.shape[dim] - width, cells.shape[dim], axis=dim)
        cells = jnp.concatenate(
            [
                lax.ppermute(tail, axis, [(i, (i + 1) % count) for i in range(ends)]),
                cells,
                lax.ppermute(head, axis, [((i + 1) % count, i) for i in range(ends)]),
            ],
            axis=dim,
        )
    return cells


def shards(
    coords,
    charges,
    multipoles,
    operators,
    send_list,
    near_list,
    m2l_source,
    m2l_target,
    m2l_operator,
):
    ncoef = multipoles.shape[0]
    leaves = multipoles.shape[1]
    npoints = charges.shape[0]
    per_leaf = npoints // leaves
    near_count = near_list.shape[1]
    stacked = jnp.concatenate([coords, charges[None, :]], axis=0)
    window = padded(stacked, (("slab", 1),), npoints)
    window_rows = jnp.transpose(window.reshape(4, 3 * leaves, per_leaf), (1, 0, 2)).reshape(
        3 * leaves, 4 * per_leaf
    )
    selector = (
        near_list.reshape(-1)[:, None] == jnp.arange(3 * leaves, dtype=jnp.int32)[None, :]
    ).astype(jnp.float32)
    picked = jnp.dot(selector, window_rows, precision=lax.Precision.HIGHEST)
    picked = picked.reshape(leaves, near_count, 4, per_leaf)
    sources = jnp.transpose(picked, (2, 0, 1, 3)).reshape(4, leaves, near_count * per_leaf)
    targets = jnp.transpose(stacked.reshape(4, leaves, per_leaf), (0, 2, 1))
    dx = targets[0][:, :, None] - sources[0][None]
    dy = targets[1][:, :, None] - sources[1][None]
    dz = targets[2][:, :, None] - sources[2][None]
    inverse = 1.0 / jnp.sqrt(dx * dx + dy * dy + dz * dz + SOFT2)
    potential = jnp.sum(inverse * sources[3][None], axis=2)
    near_potential = potential.T.reshape(npoints)
    outgoing = jnp.take(multipoles, send_list[0], axis=1)
    received = lax.all_to_all(outgoing, "grp", split_axis=1, concat_axis=1, tiled=True)
    columns_in = received.shape[1]
    op_count = operators.shape[0]
    table = jnp.einsum("ocd,de->coe", operators, received, precision=lax.Precision.HIGHEST)
    table = table.reshape(ncoef, op_count * columns_in)
    entry_index = m2l_operator[0] * columns_in + m2l_source[0]
    entry_columns = jnp.take(table, entry_index, axis=1)
    target_table = (m2l_target[0][:, None] == jnp.arange(leaves, dtype=jnp.int32)[None, :]).astype(
        jnp.float32
    )
    local_exp = jnp.dot(entry_columns, target_table, precision=lax.Precision.HIGHEST)
    return (local_exp, near_potential)


def solution(mesh):
    return jax.shard_map(
        shards,
        mesh=mesh,
        in_specs=(
            P(None, ("slab", "grp")),
            P(("slab", "grp")),
            P(None, ("slab", "grp")),
            P(),
            P(("slab", "grp"), None),
            P(("slab", "grp"), None),
            P(("slab", "grp"), None),
            P(("slab", "grp"), None),
            P(("slab", "grp"), None),
        ),
        out_specs=(P(None, ("slab", "grp")), P(("slab", "grp"))),
        check_vma=False,
    )
```

profile of v0, /device:TPU:0, one launch (start us, length us, event | category | flops | bytes accessed | tf_op | source)
XLA Modules:
  0.0 62.7 jit_solution(3552161837293061211)
XLA Ops:
  0.7 1.0 %pad_maximum_fusion.1 = f32[4,8192]{1,0:T(4,128)S(1)} fusion(f32[1,8192]{1,0:T(1,128)} %bitcast.59, f32[3,8192]{1,0:T(4,128)} %param.9), kind=kLoop, calls=%fused_computation.19 | loop fusion | flops 32768 | bytes 262144 | tf_op jit(solution)/shard_map/concatenate | solution.py:42
  1.7 4.9 %collective-permute-start = (f32[4,8192]{1,0:T(4,128)S(1)}, f32[4,8192]{1,0:T(4,128)S(1)}, u32[]{:S(2)}, u32[]{:S(2)}) collective-permute-start(f32[4,8192]{1,0:T(4,128)S(1)} %pad_maximum_fusion.1), channel_id=1, source_target_pairs={{0,8},{8,16},{16,24},{1,9},{9,17},{17,25},{2,10},{10,18},{18,26},{... | collective-permute-start | bytes 393224 | tf_op jit(solution)/shard_map/ppermute | solution.py:17
  6.7 1.3 %collective-permute-start.1 = (f32[4,8192]{1,0:T(4,128)S(1)}, f32[4,8192]{1,0:T(4,128)S(1)}, u32[]{:S(2)}, u32[]{:S(2)}) collective-permute-start(f32[4,8192]{1,0:T(4,128)S(1)} %pad_maximum_fusion.1), channel_id=1, source_target_pairs={{8,0},{16,8},{24,16},{9,1},{17,9},{25,17},{10,2},{18,10},{26,18},{... | collective-permute-start | bytes 393224 | tf_op jit(solution)/shard_map/ppermute | solution.py:19
  8.0 1.1 %copy.49 = f32[121,512]{0,1:T(8,128)S(1)} copy(f32[121,512]{1,0:T(8,128)} %param.11) | data formatting | bytes 495616 | tf_op args[2]
  9.0 0.7 %fusion.15 = s32[128]{0:T(128)S(1)} fusion(s32[1,128]{1,0:T(1,128)} %param.13), kind=kLoop, calls=%fused_computation.33 | loop fusion | flops 384 | bytes 1024 | tf_op jit(solution)/shard_map/jit(_take)/jit(_where)/select_n | solution.py:60
  9.7 0.5 broadcast.111
  10.2 1.3 %reduce.3 = s32[128]{0:T(128)S(1)} reduce(s32[1,128]{1,0:T(1,128)} %param.13, s32[]{:T(128)} %broadcast.111), dimensions={0}, to_apply=%param.13.reduce_sub_computation.3 | reduce | bytes 1028 | tf_op args[4]
  11.5 0.1 squeeze.7
  11.6 0.6 %gather_fusion = f32[128,121]{1,0:T(8,128)S(1)} fusion(f32[121,512]{0,1:T(8,128)S(1)} %copy.49, s32[1024]{0:T(1024)S(1)} %pad_clamp_fusion), kind=kCustom, calls=%fused_computation | custom fusion | bytes 124416 | tf_op jit(solution)/shard_map/jit(_take)/gather | solution.py:60
  12.3 0.7 %broadcast_select_fusion = f32[121,8,16]{0,2,1:T(8,128)} fusion(f32[121,8,16]{0,2,1:T(8,128)S(1)} %bitcast.62, pred[8,16]{1,0:T(8,128)(4,1)S(1)} %compare_and_fusion.1), kind=kLoop, calls=%fused_computation.25 | loop fusion | flops 15488 | bytes 124032 | tf_op jit(solution)/shard_map/jit(_take)/select_n | solution.py:60
  13.0 3.7 %all-to-all-start = ((f32[121,8,16]{0,2,1:T(8,128)}), f32[121,8,16]{0,2,1:T(8,128)S(1)}, u32[]{:S(2)}, u32[]{:S(2)}) async-start(f32[121,8,16]{0,2,1:T(8,128)} %broadcast_select_fusion), calls=%async_computation | async-start | bytes 131072 | tf_op jit(solution)/shard_map/all_to_all | solution.py:61
  16.7 1.2 %concatenate.13 = f32[3,512,16]{2,1,0:T(8,128)S(1)} reshape(f32[3,8192]{1,0:T(4,128)} %param.9) | data formatting | bytes 196608 | tf_op jit(solution)/shard_map/concatenate | solution.py:42
  17.9 0.9 %concatenate.14 = f32[1,512,16]{2,1,0:T(8,128)S(1)} reshape(f32[8192]{0:T(1024)} %param.10) | data formatting | bytes 65536 | tf_op jit(solution)/shard_map/concatenate | solution.py:42
  18.8 0.2 copy.51
  19.0 0.1 copy.52
  19.2 0.6 %slice_bitcast_fusion.2 = (f32[16,512]{1,0:T(8,128)}, f32[16,512]{1,0:T(8,128)}, f32[16,512]{1,0:T(8,128)}) fusion(f32[4,16,512]{2,1,0:T(8,128)S(1)} %maximum_bitcast_fusion), kind=kLoop, calls=%fused_computation.24 | loop fusion | bytes 196608 | tf_op jit(solution)/shard_map/sub | solution.py:54
  19.9 1.9 %all-to-all-done = f32[121,8,16]{0,2,1:T(8,128)S(1)} async-done(((f32[121,8,16]{0,2,1:T(8,128)}), f32[121,8,16]{0,2,1:T(8,128)S(1)}, u32[]{:S(2)}, u32[]{:S(2)}) %all-to-all-start) | async-done | bytes 61984 | tf_op jit(solution)/shard_map/all_to_all | solution.py:61
  21.7 0.7 %fusion.12 = f32[128,8,121]{2,0,1:T(8,128)S(1)} fusion(f32[121,128,1]{0,1,2:T(8,128)S(1)} %bitcast.61, f32[8,121,121]{2,0,1:T(8,128)S(1)} %copy-done), kind=kOutput, calls=%fused_computation.14 | convolution fusion | flops 179908608 | bytes 1026080 | tf_op jit(solution)/shard_map/ocd,de->coe/dot_general | solution.py:64
  22.4 10.8 %gather_fusion.1 = f32[4096,121]{1,0:T(8,128)S(1)} fusion(f32[121,1024]{0,1:T(8,128)S(1)} %bitcast.53, s32[4096]{0:T(1024)S(1)} %broadcast_clamp_fusion), kind=kCustom, calls=%fused_computation.1 | custom fusion | bytes 3981312 | tf_op jit(solution)/shard_map/jit(_take)/gather | solution.py:67
  33.2 4.4 %fusion.4 = f32[121,512]{1,0:T(8,128)} fusion(s32[4096]{0:T(1024)S(1)} %bitcast.66, f32[4096,121]{1,0:T(8,128)S(1)} %gather_fusion.1, pred[4096]{0:T(1024)(128)(4,1)S(1)} %compare_and_fusion), kind=kOutput, calls=%fused_computation.7 | convolution fusion | flops 3047657472 | bytes 2250752 | tf_op jit(solution)/shard_map/dot_general | solution.py:71
  37.7 0.1 pad_maximum_fusion
  37.8 2.7 %reshape.143 = f32[4,1536,16]{2,1,0:T(8,128)} reshape(f32[4,24576]{1,0:T(4,128)S(1)} %pad_maximum_fusion) | data formatting | bytes 786432 | tf_op jit(solution)/shard_map/reshape | solution.py:44
  40.5 2.3 %copy.53 = f32[1536,4,16]{0,2,1:T(8,128)S(1)} copy(f32[1536,4,16]{2,0,1:T(8,128)} %bitcast.54) | data formatting | bytes 786432 | tf_op jit(solution)/shard_map/transpose | solution.py:44
  42.9 13.4 %fusion.7 = f32[4,512,8,16]{1,3,0,2:T(8,128)S(1)} fusion(s32[512,8]{0,1:T(8,128)S(1)} %copy-done.9, f32[1536,4,16]{0,2,1:T(8,128)S(1)} %copy.53), kind=kOutput, calls=%fused_computation.11 | convolution fusion | flops 4838129664 | bytes 1458176 | tf_op jit(solution)/shard_map/dot_general | solution.py:50
  56.3 0.1 fusion.17
  56.4 0.1 copy.54
  56.6 0.1 copy.55
  56.7 0.1 copy.56
  56.9 0.1 copy.57
  57.1 4.7 %multiply_reduce_fusion = f32[16,512]{1,0:T(8,128)S(1)} fusion(f32[512,128]{1,0:T(8,128)S(1)} %copy.57, f32[512,128]{1,0:T(8,128)S(1)} %copy.56, f32[16,512]{1,0:T(8,128)S(1)} %copy-done.4, f32[512,128]{1,0:T(8,128)S(1)} %copy.55, f32[16,512]{1,0:T(8,128)S(1)} %copy-done.5, f32[512,128]{1,0:T(8,128)S(1)} %copy.54, f32[16,512]{1,0:T(8,128)S(1)} %copy-done.3), kind=kLoop, calls=%fused_computation.8 | loop fusion | flops 11526144 | bytes 1179648 | tf_op jit(solution)/shard_map/reduce_sum | solution.py:58
  61.8 0.1 copy.58
  62.0 0.8 %reshape.145 = f32[8192]{0:T(1024)} reshape(f32[512,16]{1,0:T(8,128)S(1)} %copy.58) | data formatting | bytes 65536 | tf_op jit(solution)/shard_map/reshape | solution.py:59
  (28 shorter events, 0.2 us)
Async XLA Ops:
  0.6 21.1 %copy-start = (f32[8,121,121]{2,0,1:T(8,128)S(1)}, f32[8,121,121]{2,0,1:T(8,128)}, u32[]{:S(2)}) copy-start(f32[8,121,121]{2,0,1:T(8,128)} %param.12) | copy-start | bytes 1405540
  0.6 19.1 %copy-start.6 = (s32[1,4096]{1,0:T(1,128)S(1)}, s32[1,4096]{1,0:T(1,128)}, u32[]{:S(2)}) copy-start(s32[1,4096]{1,0:T(1,128)} %param.15) | copy-start | bytes 49156
  0.7 19.1 %copy-start.7 = (s32[1,4096]{1,0:T(1,128)S(1)}, s32[1,4096]{1,0:T(1,128)}, u32[]{:S(2)}) copy-start(s32[1,4096]{1,0:T(1,128)} %param.17) | copy-start | bytes 49156
  1.7 35.9 %collective-permute-start = (f32[4,8192]{1,0:T(4,128)S(1)}, f32[4,8192]{1,0:T(4,128)S(1)}, u32[]{:S(2)}, u32[]{:S(2)}) collective-permute-start(f32[4,8192]{1,0:T(4,128)S(1)} %pad_maximum_fusion.1), channel_id=1, source_target_pairs={{0,8},{8,16},{16,24},{1,9},{9,17},{17,25},{2,10},{10,18},{18,26},{... | collective-permute-start | bytes 393224 | tf_op jit(solution)/shard_map/ppermute | solution.py:17
  6.7 31.0 %collective-permute-start.1 = (f32[4,8192]{1,0:T(4,128)S(1)}, f32[4,8192]{1,0:T(4,128)S(1)}, u32[]{:S(2)}, u32[]{:S(2)}) collective-permute-start(f32[4,8192]{1,0:T(4,128)S(1)} %pad_maximum_fusion.1), channel_id=1, source_target_pairs={{8,0},{16,8},{24,16},{9,1},{17,9},{25,17},{10,2},{18,10},{26,18},{... | collective-permute-start | bytes 393224 | tf_op jit(solution)/shard_map/ppermute | solution.py:19
  13.0 8.7 %all-to-all-start = ((f32[121,8,16]{0,2,1:T(8,128)}), f32[121,8,16]{0,2,1:T(8,128)S(1)}, u32[]{:S(2)}, u32[]{:S(2)}) async-start(f32[121,8,16]{0,2,1:T(8,128)} %broadcast_select_fusion), calls=%async_computation | async-start | bytes 131072 | tf_op jit(solution)/shard_map/all_to_all | solution.py:61
  22.4 10.8 %copy-start.8 = (s32[1,4096]{1,0:T(1,128)S(1)}, s32[1,4096]{1,0:T(1,128)}, u32[]{:S(2)}) copy-start(s32[1,4096]{1,0:T(1,128)} %param.16) | copy-start | bytes 49156
  33.2 4.4 %copy-start.1 = (f32[3,8192]{1,0:T(4,128)S(1)}, f32[3,8192]{1,0:T(4,128)}, u32[]{:S(2)}) copy-start(f32[3,8192]{1,0:T(4,128)} %param.9) | copy-start | bytes 294916
  33.2 4.4 %copy-start.2 = (f32[8192]{0:T(1024)S(1)}, f32[8192]{0:T(1024)}, u32[]{:S(2)}) copy-start(f32[8192]{0:T(1024)} %param.10) | copy-start | bytes 98308
  37.8 5.1 %copy-start.9 = (s32[512,8]{0,1:T(8,128)S(1)}, s32[512,8]{0,1:T(8,128)}, u32[]{:S(2)}) copy-start(s32[512,8]{0,1:T(8,128)} %param.14) | copy-start | bytes 49156
  56.3 0.8 %copy-start.3 = (f32[16,512]{1,0:T(8,128)S(1)}, f32[16,512]{1,0:T(8,128)}, u32[]{:S(2)}) copy-start(f32[16,512]{1,0:T(8,128)} %get-tuple-element.8) | copy-start | bytes 98308
  56.3 0.8 %copy-start.4 = (f32[16,512]{1,0:T(8,128)S(1)}, f32[16,512]{1,0:T(8,128)}, u32[]{:S(2)}) copy-start(f32[16,512]{1,0:T(8,128)} %get-tuple-element.9) | copy-start | bytes 98308
  56.3 0.8 %copy-start.5 = (f32[16,512]{1,0:T(8,128)S(1)}, f32[16,512]{1,0:T(8,128)}, u32[]{:S(2)}) copy-start(f32[16,512]{1,0:T(8,128)} %get-tuple-element.10) | copy-start | bytes 98308
where the time goes:
time: 63.2 us; the launch traced here: 62.7 us
  local copies, waits for them, and re-layouts  22.8 us (36%)
  matrix products  18.5 us (29%)
  starting transfers between devices  9.95 us (16%)
  other arithmetic  8.67 us (14%)
  waiting for transfers between devices  1.88 us (3%)
  between operations  0.91 us (1%)
    dot_general x1, matrix products, shards(): picked = jnp.dot(selector, window_rows, precision=lax.Precision.HIGHEST)  13.4 us
    gather x1, local copies, waits for them, and re-layouts, shards(): entry_columns = jnp.take(table, entry_index, axis=1)  10.8 us
    ppermute x1, starting transfers between devices, padded(): lax.ppermute(tail, axis, [(i, (i + 1) % count) for i in range(ends)])  4.94 us
    reduce_sum x1, other arithmetic, shards(): potential = jnp.sum(inverse * sources[3][None], axis=2)  4.74 us
    dot_general x1, matrix products, shards(): jnp.dot(entry_columns, target_table, precision=lax.Precision.HIGHEST)  4.4 us
    all_to_all x1, starting transfers between devices, shards(): lax.all_to_all(outgoing, 'grp', split_axis=1, concat_axis=1, tiled=True)  3.72 us
    reshape x1, local copies, waits for them, and re-layouts, shards(): window.reshape(4, 3 * leaves, per_leaf)  2.73 us
    concatenate x4, local copies, waits for them, and re-layouts, shards(): stacked = jnp.concatenate([coords, charges[None, :]], axis=0)  2.4 us
  transfers between devices with their start and end apart: 3, of which 1 were waited for; matrix products, arithmetic and copies ran while one was open for 38% of the time, Pallas kernels for 0%

commit v1 on v0

v1 whole, which is shorter than its diff:
```python
import functools

import jax
import jax.numpy as jnp
from jax import lax
from jax.experimental import pallas as pl
from jax.experimental.pallas import tpu as pltpu
from jax.sharding import PartitionSpec as P

SOFT2 = 0.0625
LANES = 128
VMEM = pl.BlockSpec(memory_space=pltpu.VMEM)
ANY = pl.BlockSpec(memory_space=pl.ANY)
PARAMS = pltpu.CompilerParams(vmem_limit_bytes=48 * 1024 * 1024)
WIDE = pltpu.CompilerParams(vmem_limit_bytes=64 * 1024 * 1024)


def lane_gather(x, idx):
    return jnp.take_along_axis(x, idx, axis=1, mode="promise_in_bounds")


def prep_kernel(coords_hbm, charges_hbm, multipoles_hbm, send_hbm, table_ref, out_ref, coords_ref, charges_ref, multipoles_ref, send_ref, sems):
    pairs = (
        (coords_hbm, coords_ref),
        (charges_hbm, charges_ref),
        (send_hbm, send_ref),
        (multipoles_hbm, multipoles_ref),
    )
    copies = [pltpu.make_async_copy(src, dst, sems.at[i]) for i, (src, dst) in enumerate(pairs)]
    for copy in copies:
        copy.start()
    copies[0].wait()
    copies[1].wait()
    for c in range(4):
        rows = charges_ref[...] if c == 3 else coords_ref[:, c, :]
        cols = rows.T
        for pair in range(4):
            a = cols[32 * pair : 32 * pair + 16, :]
            b = cols[32 * pair + 16 : 32 * pair + 32, :]
            table_ref[16 * c : 16 * c + 16, LANES * pair : LANES * (pair + 1)] = jnp.concatenate([a, b], axis=1)
    copies[2].wait()
    copies[3].wait()
    ncoef, leaves = multipoles_ref.shape
    for sb in range(send_ref.shape[1] // LANES):
        send = send_ref[:, LANES * sb : LANES * (sb + 1)]
        lane = send & (LANES - 1)
        group = send >> 7
        idx = jnp.broadcast_to(lane, (ncoef, LANES))
        picked = jnp.zeros((ncoef, LANES), jnp.float32)
        for g in range(leaves // LANES):
            got = lane_gather(multipoles_ref[:, LANES * g : LANES * (g + 1)], idx)
            picked = jnp.where(group == g, got, picked)
        out_ref[LANES * sb : LANES * (sb + 1), :] = picked.T


def count_kernel(source_ref, target_ref, operator_ref, low_ref, high_ref, flag_ref, acc_ref, *, sources, leaves, chunk):
    nrows = acc_ref.shape[1]
    entries = source_ref.shape[1]
    base = pl.program_id(0) * nrows
    half = entries // 2
    for h in range(2):
        for k in range(half // chunk):
            at = pl.ds(h * half + k * chunk, chunk)
            op = operator_ref[:, at]
            code = (op >> 1) * sources + source_ref[:, at] - base
            weight = jnp.where((op & 1) == 1, 4096.0, 1.0)
            a = jnp.where(lax.broadcasted_iota(jnp.int32, (nrows, chunk), 0) == code, weight, 0.0).astype(jnp.bfloat16)
            b = jnp.where(
                lax.broadcasted_iota(jnp.int32, (leaves, chunk), 0) == target_ref[:, at], 1.0, 0.0
            ).astype(jnp.bfloat16)
            part = lax.dot_general(a, b, (((1,), (1,)), ((), ())), preferred_element_type=jnp.float32)
            if k == 0:
                acc_ref[h] = part
            else:
                acc_ref[h] += part
    first, second = acc_ref[0], acc_ref[1]
    odd_first = jnp.floor(first * (1.0 / 4096.0))
    odd_second = jnp.floor(second * (1.0 / 4096.0))
    odd = odd_first + odd_second
    even = (first + second) - 4096.0 * odd
    top = jnp.zeros((), jnp.float32)
    for i, count in enumerate((even, odd)):
        high = 256.0 * jnp.floor(count * (1.0 / 256.0))
        low_ref[i] = (count - high).astype(jnp.bfloat16)
        high_ref[i] = high.astype(jnp.bfloat16)
        top = jnp.maximum(top, jnp.max(high))
    flag_ref[0, 0, 0] = (top > 0.0).astype(jnp.int32)


def split(x):
    hi = x.astype(jnp.bfloat16)
    return hi, (x - hi.astype(jnp.float32)).astype(jnp.bfloat16)


def far_kernel(flag_ref, operators_ref, gathered_hbm, low_ref, high_ref, out_ref, received_ref, table_ref, split_ref, sems, *, ops):
    ncoef, leaves = out_ref.shape
    peers, sources, _ = gathered_hbm.shape
    cap = sources // peers
    start = pl.multiple_of(lax.axis_index("grp") * cap, cap)
    copies = [
        pltpu.make_async_copy(
            gathered_hbm.at[p, pl.ds(start, cap), :], received_ref.at[pl.ds(cap * p, cap), :], sems.at[p]
        )
        for p in range(peers)
    ]
    for copy in copies:
        copy.start()
    for copy in copies:
        copy.wait()
    blocks = sources // LANES
    for k in range(blocks):
        table_ref[k] = lax.dot_general(
            operators_ref[...],
            received_ref[LANES * k : LANES * (k + 1), :],
            (((1,), (1,)), ((), ())),
            precision=lax.Precision.HIGHEST,
            preferred_element_type=jnp.float32,
        )
    split_ref[...] = jnp.zeros_like(split_ref)
    for op in range(ops):
        for k in range(blocks):
            lane = ((op % 2) * (ops // 2) + op // 2) * sources + LANES * k
            hi, lo = split(table_ref[k, pl.ds(op, ncoef, stride=ops), :])
            split_ref[:ncoef, lane : lane + LANES] = hi
            split_ref[LANES : LANES + ncoef, lane : lane + LANES] = lo

    def product(counts_ref):
        both = jnp.dot(split_ref[...], counts_ref[...], preferred_element_type=jnp.float32)
        return both[:ncoef, :] + both[LANES : LANES + ncoef, :]

    out_ref[...] = product(low_ref)
    flagged = flag_ref[0, 0, 0]
    for i in range(1, flag_ref.shape[0]):
        flagged = flagged | flag_ref[i, 0, 0]

    @pl.when(flagged > 0)
    def _():
        out_ref[...] += product(high_ref)


def near_kernel(gathered_hbm, own_ref, list_ref, out_ref, left_ref, right_ref, picked_ref, place_ref, pot_ref, sems):
    pts = 16
    slabs = gathered_hbm.shape[0]
    me = lax.axis_index("slab")
    sides = ((left_ref, me > 0, jnp.maximum(me - 1, 0)), (right_ref, me < slabs - 1, jnp.minimum(me + 1, slabs - 1)))
    copies = [pltpu.make_async_copy(gathered_hbm.at[at], ref, sems.at[i]) for i, (ref, _, at) in enumerate(sides)]
    for copy in copies:
        copy.start()
    near, leaves = list_ref.shape
    groups = leaves // LANES
    lane = lax.broadcasted_iota(jnp.int32, (near, LANES), 1)
    for g in range(groups):
        idx = 8 * (lane & 15) + 2 * g + (lane >> 6)
        part = (lane & 63) >> 4
        row = jnp.zeros((near, LANES), jnp.int32)
        for s in range(groups):
            row = jnp.where(part == s, lane_gather(list_ref[:, LANES * s : LANES * (s + 1)], idx), row)
        place_ref[g] = ((row >> 9) << 9) + ((row & 7) << 6) + ((row >> 3) & 63)
    for copy, (ref, inside, _) in zip(copies, sides):
        copy.wait()

        @pl.when(jnp.logical_not(inside))
        def _(ref=ref):
            ref[...] = jnp.zeros_like(ref)

    windows = (left_ref, own_ref, right_ref)
    rows = 4 * pts

    def step(i, carry):
        g = i // near
        n = i % near
        place = jnp.broadcast_to(place_ref[g, pl.ds(n, 1), :], (8, LANES))
        idx = place & (LANES - 1)
        group = place >> 7
        picked = [jnp.zeros((8, LANES), jnp.float32) for _ in range(rows // 8)]
        for s in range(3 * groups):
            here = group == s
            for r in range(rows // 8):
                source = windows[s // groups][8 * r : 8 * r + 8, LANES * (s % groups) : LANES * (s % groups + 1)]
                picked[r] = jnp.where(here, lane_gather(source, idx), picked[r])
        for r in range(rows // 8):
            picked_ref[8 * r : 8 * r + 8, :] = picked[r]
        at = pl.ds(pl.multiple_of(g * LANES, LANES), LANES)
        tx, ty, tz = (own_ref[pts * c : pts * (c + 1), at] for c in range(3))
        acc = jnp.where(n == 0, 0.0, pot_ref[g])
        for p in range(pts):
            sx, sy, sz, q = (picked_ref[pts * c + p : pts * c + p + 1, :] for c in range(4))
            dx, dy, dz = tx - sx, ty - sy, tz - sz
            acc += q * lax.rsqrt(dx * dx + dy * dy + (dz * dz + SOFT2))
        pot_ref[g] = acc
        return carry

    lax.fori_loop(0, groups * near, step, 0)
    half = LANES // 2
    pieces = []
    for g in range(groups):
        pot = pot_ref[g]
        pieces += [pot[:, :half], pot[:, half:]]
    out_ref[...] = jnp.concatenate(pieces, axis=0).T


def shards(
    coords,
    charges,
    multipoles,
    operators,
    send_list,
    near_list,
    m2l_source,
    m2l_target,
    m2l_operator,
):
    ncoef, leaves = multipoles.shape
    npoints = charges.shape[0]
    near = near_list.shape[1]
    entries = m2l_source.shape[1]
    ops = operators.shape[0]
    sources = send_list.shape[1]
    f32 = jnp.float32

    tiles = npoints // LANES
    coords3 = jnp.transpose(coords.reshape(3, tiles, LANES), (1, 0, 2))
    table, outgoing = pl.pallas_call(
        prep_kernel,
        name="prep",
        out_shape=(
            jax.ShapeDtypeStruct((64, leaves), f32),
            jax.ShapeDtypeStruct((sources, ncoef), f32),
        ),
        in_specs=[ANY] * 4,
        out_specs=(VMEM, VMEM),
        scratch_shapes=[
            pltpu.VMEM((tiles, 3, LANES), f32),
            pltpu.VMEM((tiles, LANES), f32),
            pltpu.VMEM((ncoef, leaves), f32),
            pltpu.VMEM((1, sources), jnp.int32),
            pltpu.SemaphoreType.DMA((4,)),
        ],
        compiler_params=WIDE,
    )(coords3, charges.reshape(tiles, LANES), multipoles, send_list)
    gathered = lax.all_gather(outgoing, "grp")
    window = lax.all_gather(table, "slab")

    nrows = ops // 2 * sources
    block = min(nrows, 512)
    low, high, flag = pl.pallas_call(
        functools.partial(count_kernel, sources=sources, leaves=leaves, chunk=512),
        name="counts",
        grid=(nrows // block,),
        out_shape=(
            jax.ShapeDtypeStruct((2, nrows, leaves), jnp.bfloat16),
            jax.ShapeDtypeStruct((2, nrows, leaves), jnp.bfloat16),
            jax.ShapeDtypeStruct((nrows // block, 1, 1), jnp.int32),
        ),
        in_specs=[pl.BlockSpec((1, entries), lambda i: (0, 0))] * 3,
        out_specs=(
            pl.BlockSpec((2, block, leaves), lambda i: (0, i, 0)),
            pl.BlockSpec((2, block, leaves), lambda i: (0, i, 0)),
            pl.BlockSpec((1, 1, 1), lambda i: (i, 0, 0), memory_space=pltpu.SMEM),
        ),
        scratch_shapes=[pltpu.VMEM((2, block, leaves), f32)],
        compiler_params=PARAMS,
    )(m2l_source, m2l_target, m2l_operator)

    local_exp = pl.pallas_call(
        functools.partial(far_kernel, ops=ops),
        name="far",
        out_shape=jax.ShapeDtypeStruct((ncoef, leaves), f32),
        in_specs=[pl.BlockSpec(memory_space=pltpu.SMEM), VMEM, ANY, VMEM, VMEM],
        out_specs=VMEM,
        scratch_shapes=[
            pltpu.VMEM((sources, ncoef), f32),
            pltpu.VMEM((sources // LANES, ncoef * ops, LANES), f32),
            pltpu.VMEM((2 * LANES, ops * sources), jnp.bfloat16),
            pltpu.SemaphoreType.DMA((gathered.shape[0],)),
        ],
        compiler_params=PARAMS,
    )(flag, jnp.transpose(operators, (1, 0, 2)).reshape(ncoef * ops, ncoef), gathered, low.reshape(ops * sources, leaves), high.reshape(ops * sources, leaves))

    near_potential = pl.pallas_call(
        near_kernel,
        name="near",
        out_shape=jax.ShapeDtypeStruct((tiles, LANES), f32),
        in_specs=[ANY, VMEM, VMEM],
        out_specs=VMEM,
        scratch_shapes=[
            pltpu.VMEM((64, leaves), f32),
            pltpu.VMEM((64, leaves), f32),
            pltpu.VMEM((64, LANES), f32),
            pltpu.VMEM((leaves // LANES, near, LANES), jnp.int32),
            pltpu.VMEM((leaves // LANES, 16, LANES), f32),
            pltpu.SemaphoreType.DMA((2,)),
        ],
        compiler_params=PARAMS,
    )(window, table, near_list.T)
    return (local_exp, near_potential.reshape(npoints))


def solution(mesh):
    both = ("slab", "grp")
    return jax.shard_map(
        shards,
        mesh=mesh,
        in_specs=(
            P(None, both),
            P(both),
            P(None, both),
            P(),
            P(both, None),
            P(both, None),
            P(both, None),
            P(both, None),
            P(both, None),
        ),
        out_specs=(P(None, both), P(both)),
        check_vma=False,
    )
```

time: 63.2 us -> 46.6 us (0.74)
  blocking collectives: 0 us -> 28.2 us
  local copies, waits for them, and re-layouts: 22.8 us -> 0.03 us
  matrix products: 18.5 us -> 0 us
  Pallas kernels: 0 us -> 17.4 us
  starting transfers between devices: 9.95 us -> 0 us
  other arithmetic: 8.67 us -> 0 us
  waiting for transfers between devices: 1.88 us -> 0 us
    all_gather x0 -> x2, blocking collectives: none -> 28.2 us  [the longest x1 16.5 us: shards(): window = lax.all_gather(table, 'slab')]
    dot_general x3 -> x0, matrix products: 18.5 us -> none  [the longest x1 13.4 us: shards(): picked = jnp.dot(selector, window_rows, precision=lax.Precision.HIGHEST)]
    pallas_call x0 -> x4, Pallas kernels: none -> 17.4 us  [the longest x1 8.49 us: shards(): pl.pallas_call(near_kernel, name='near', out_shape=jax.ShapeDtypeStruct((...]
    gather x2 -> x0, local copies, waits for them, and re-layouts: 11.4 us -> none  [the longest x1 10.8 us: shards(): entry_columns = jnp.take(table, entry_index, axis=1)]
    ppermute x2 -> x0, starting transfers between devices: 6.23 us -> none  [the longest x1 4.94 us: padded(): lax.ppermute(tail, axis, [(i, (i + 1) % count) for i in range(ends)])]
    reduce_sum x1 -> x0, other arithmetic: 4.74 us -> none  [shards(): potential = jnp.sum(inverse * sources[3][None], axis=2)]
    all_to_all x1 -> x0, starting transfers between devices: 3.72 us -> none  [shards(): lax.all_to_all(outgoing, 'grp', split_axis=1, concat_axis=1, tiled=True)]
    reshape x2 -> x0, local copies, waits for them, and re-layouts: 3.48 us -> none  [the longest x1 2.73 us: shards(): window.reshape(4, 3 * leaves, per_leaf)]
  transfers between devices with their start and end apart: 3 -> 0, of which waited for: 1 -> 0; matrix products, arithmetic and copies ran while one was open for 38% -> 0% of each run, Pallas kernels for 0% -> 0%
where the time goes in v1:
time: 46.6 us; the launch traced here: 46.3 us
  blocking collectives  28.2 us (61%)
  Pallas kernels  17.4 us (37%)
  between operations  0.72 us (2%)
    all_gather x1, blocking collectives, shards(): window = lax.all_gather(table, 'slab')  16.5 us
    all_gather x1, blocking collectives, shards(): gathered = lax.all_gather(outgoing, 'grp')  11.7 us
    pallas_call x1, Pallas kernels, shards(): pl.pallas_call(near_kernel, name='near', out_shape=jax.ShapeDtypeStruct((...  8.49 us
    pallas_call x1, Pallas kernels, shards(): pl.pallas_call(functools.partial(count_kernel, sources=sources, leaves=le...  3.49 us
    pallas_call x1, Pallas kernels, shards(): pl.pallas_call(functools.partial(far_kernel, ops=ops), name='far', out_sh...  3.37 us
    pallas_call x1, Pallas kernels, shards(): pl.pallas_call(prep_kernel, name='prep', out_shape=(jax.ShapeDtypeStruct(...  2.01 us

profile of v1, /device:TPU:0, one launch (start us, length us, event | category | flops | bytes accessed | tf_op | source)
XLA Modules:
  0.0 46.3 jit_solution(4977140376221219719)
XLA Ops:
  0.6 2.0 %prep.1 = (f32[64,512]{1,0:T(8,128)}, f32[128,121]{1,0:T(8,128)}) custom-call(f32[64,3,128]{2,1,0:T(4,128)} %bitcast.19, f32[64,128]{1,0:T(8,128)} %bitcast.21, f32[121,512]{1,0:T(8,128)} %multipoles_hbm.1, s32[1,128]{1,0:T(1,128)} %send_hbm.1), custom_call_target="tpu_custom_call" | custom-call | tf_op jit(solution)/shard_map/prep/pallas_call | solution.py:223
  2.6 0.0 copy-start
  2.7 11.7 %all-gather = f32[1024,121]{1,0:T(8,128)S(1)} all-gather(f32[128,121]{1,0:T(8,128)} %get-tuple-element.8), channel_id=2, replica_groups=mesh['slab'=4,'grp'=8] {'grp'}, dimensions={0}, use_global_device_ids=true | all-gather | bytes 557568 | tf_op jit(solution)/shard_map/all_gather | solution.py:241
  14.4 0.0 copy-done
  14.4 0.0 copy-start.2
  14.4 16.5 %all-gather.1 = f32[256,512]{1,0:T(8,128)S(1)} all-gather(f32[64,512]{1,0:T(8,128)S(1)} %copy-done), channel_id=3, replica_groups=mesh['slab'=4,'grp'=8] {'slab'}, dimensions={0}, use_global_device_ids=true | all-gather | bytes 655360 | tf_op jit(solution)/shard_map/all_gather | solution.py:242
  30.9 0.0 copy-start.1
  30.9 0.0 copy-done.2
  30.9 0.0 copy-start.3
  30.9 0.0 copy-start.4
  30.9 0.0 copy-start.5
  30.9 8.5 %near.1 = f32[64,128]{1,0:T(8,128)} custom-call(f32[4,64,512]{2,1,0:T(8,128)S(1)} %bitcast.13, f32[64,512]{1,0:T(8,128)S(1)} %copy-done, s32[8,512]{1,0:T(8,128)S(1)} %bitcast.18), custom_call_target="tpu_custom_call" | custom-call | tf_op jit(solution)/shard_map/near/pallas_call | solution.py:280
  39.4 0.0 copy-done.3
  39.4 0.0 copy-done.4
  39.4 0.0 copy-done.5
  39.5 3.5 %counts.1 = (bf16[2,512,512]{2,1,0:T(8,128)(2,1)S(1)}, bf16[2,512,512]{2,1,0:T(8,128)(2,1)S(1)}, s32[1,1,1]{2,1,0:T(1,128)}) custom-call(s32[1,4096]{1,0:T(1,128)S(1)} %copy-done.3, s32[1,4096]{1,0:T(1,128)S(1)} %copy-done.4, s32[1,4096]{1,0:T(1,128)S(1)} %copy-done.5), custom_call_target="tpu_custom_call" | custom-call | tf_op jit(solution)/shard_map/counts/pallas_call | solution.py:246
  43.0 0.0 copy-done.1
  43.0 3.4 %far.1 = f32[121,512]{1,0:T(8,128)} custom-call(s32[1,1,1]{2,1,0:T(1,128)} %get-tuple-element.7.flag_ref, f32[968,121]{1,0:T(8,128)S(1)} %bitcast.17, f32[8,128,121]{2,1,0:T(8,128)S(1)} %bitcast.14, bf16[1024,512]{1,0:T(8,128)(2,1)S(1)} %bitcast.15, bf16[1024,512]{1,0:T(8,128)(2,1)S(1)} %bitcast.16), custom_call_target="tpu_custom_call" | custom-call | tf_op jit(solution)/shard_map/far/pallas_call | solution.py:265
Async XLA Ops:
  2.6 11.8 %copy-start = (f32[64,512]{1,0:T(8,128)S(1)}, f32[64,512]{1,0:T(8,128)}, u32[]{:S(2)}) copy-start(f32[64,512]{1,0:T(8,128)} %get-tuple-element.11.own_ref) | copy-start | bytes 393220
  14.4 16.5 %copy-start.2 = (s32[512,8]{0,1:T(8,128)S(1)}, s32[512,8]{0,1:T(8,128)}, u32[]{:S(2)}) copy-start(s32[512,8]{0,1:T(8,128)} %param.14) | copy-start | bytes 49156
  30.9 12.1 %copy-start.1 = (f32[8,121,121]{2,0,1:T(8,128)S(1)}, f32[8,121,121]{2,0,1:T(8,128)}, u32[]{:S(2)}) copy-start(f32[8,121,121]{2,0,1:T(8,128)} %param.12) | copy-start | bytes 1405540
  30.9 8.5 %copy-start.3 = (s32[1,4096]{1,0:T(1,128)S(1)}, s32[1,4096]{1,0:T(1,128)}, u32[]{:S(2)}) copy-start(s32[1,4096]{1,0:T(1,128)} %source_ref.1) | copy-start | bytes 49156
  30.9 8.5 %copy-start.4 = (s32[1,4096]{1,0:T(1,128)S(1)}, s32[1,4096]{1,0:T(1,128)}, u32[]{:S(2)}) copy-start(s32[1,4096]{1,0:T(1,128)} %target_ref.1) | copy-start | bytes 49156
  30.9 8.5 %copy-start.5 = (s32[1,4096]{1,0:T(1,128)S(1)}, s32[1,4096]{1,0:T(1,128)}, u32[]{:S(2)}) copy-start(s32[1,4096]{1,0:T(1,128)} %operator_ref.1) | copy-start | bytes 49156

commit v2 on v1

v2 whole, which is shorter than its diff:
```python
import functools

import jax
import jax.numpy as jnp
from jax import lax
from jax.experimental import pallas as pl
from jax.experimental.pallas import tpu as pltpu
from jax.sharding import PartitionSpec as P

SOFT2 = 0.0625
LANES = 128
PTS = 16
VMEM = pl.BlockSpec(memory_space=pltpu.VMEM)
ANY = pl.BlockSpec(memory_space=pl.ANY)
PARAMS = pltpu.CompilerParams(vmem_limit_bytes=48 * 1024 * 1024)
WIDE = pltpu.CompilerParams(vmem_limit_bytes=64 * 1024 * 1024)
NT = (((1,), (1,)), ((), ()))


def lane_gather(x, idx):
    return jnp.take_along_axis(x, idx, axis=1, mode="promise_in_bounds")


def split(x):
    hi = x.astype(jnp.bfloat16)
    return hi, (x - hi.astype(jnp.float32)).astype(jnp.bfloat16)


def pad_lanes(x):
    return jnp.concatenate([x, jnp.zeros((x.shape[0], LANES - x.shape[1]), x.dtype)], axis=1)


def prep_kernel(
    coords_hbm, charges_hbm, multipoles_hbm, send_hbm, table_ref, out_ref,
    coords_ref, charges_ref, multipoles_ref, send_ref, sems,
):
    pairs = (
        (coords_hbm, coords_ref),
        (charges_hbm, charges_ref),
        (send_hbm, send_ref),
        (multipoles_hbm, multipoles_ref),
    )
    copies = [pltpu.make_async_copy(src, dst, sems.at[i]) for i, (src, dst) in enumerate(pairs)]
    for copy in copies:
        copy.start()
    copies[0].wait()
    copies[1].wait()
    for c in range(4):
        rows = charges_ref[...] if c == 3 else coords_ref[:, c, :]
        cols = rows.T
        for pair in range(4):
            a = cols[32 * pair : 32 * pair + 16, :]
            b = cols[32 * pair + 16 : 32 * pair + 32, :]
            table_ref[16 * c : 16 * c + 16, LANES * pair : LANES * (pair + 1)] = jnp.concatenate([a, b], axis=1)
    copies[2].wait()
    copies[3].wait()
    ncoef, leaves = multipoles_ref.shape
    for sb in range(send_ref.shape[1] // LANES):
        send = send_ref[:, LANES * sb : LANES * (sb + 1)]
        lane = send & (LANES - 1)
        group = send >> 7
        idx = jnp.broadcast_to(lane, (ncoef, LANES))
        picked = jnp.zeros((ncoef, LANES), jnp.float32)
        for g in range(leaves // LANES):
            got = lane_gather(multipoles_ref[:, LANES * g : LANES * (g + 1)], idx)
            picked = jnp.where(group == g, got, picked)
        out_ref[LANES * sb : LANES * (sb + 1), :] = picked.T


def counts_kernel(
    source_ref, target_ref, operator_ref, operators_ref, low_ref, high_ref, flag_ref, parts_ref,
    acc_ref, wide_ref, *, sources, leaves, chunk, ops,
):
    nrows = acc_ref.shape[1]
    entries = source_ref.shape[1]
    base = pl.program_id(0) * nrows
    half = entries // 2
    for h in range(2):
        for k in range(half // chunk):
            at = pl.ds(h * half + k * chunk, chunk)
            op = operator_ref[:, at]
            code = (op >> 1) * sources + source_ref[:, at] - base
            weight = jnp.where((op & 1) == 1, 4096.0, 1.0)
            a = jnp.where(lax.broadcasted_iota(jnp.int32, (nrows, chunk), 0) == code, weight, 0.0).astype(jnp.bfloat16)
            b = jnp.where(
                lax.broadcasted_iota(jnp.int32, (leaves, chunk), 0) == target_ref[:, at], 1.0, 0.0
            ).astype(jnp.bfloat16)
            part = lax.dot_general(a, b, NT, preferred_element_type=jnp.float32)
            if k == 0:
                acc_ref[h] = part
            else:
                acc_ref[h] += part
    first, second = acc_ref[0], acc_ref[1]
    odd_first = jnp.floor(first * (1.0 / 4096.0))
    odd_second = jnp.floor(second * (1.0 / 4096.0))
    odd = odd_first + odd_second
    even = (first + second) - 4096.0 * odd
    top = jnp.zeros((), jnp.float32)
    for i, count in enumerate((even, odd)):
        high = 256.0 * jnp.floor(count * (1.0 / 256.0))
        low_ref[i] = (count - high).astype(jnp.bfloat16)
        high_ref[i] = high.astype(jnp.bfloat16)
        top = jnp.maximum(top, jnp.max(high))
    flag_ref[0, 0, 0] = (top > 0.0).astype(jnp.int32)

    @pl.when(pl.program_id(0) == 0)
    def _():
        ncoef = operators_ref.shape[1]
        wide_ref[...] = pad_lanes(operators_ref[...])
        for op in range(ops):
            row = ((op % 2) * (ops // 2) + op // 2) * LANES
            matrix = wide_ref[pl.ds(op, ncoef, stride=ops), :]
            matrix = jnp.concatenate([matrix, jnp.zeros((LANES - ncoef, LANES), jnp.float32)], axis=0)
            hi, lo = split(matrix)
            parts_ref[row : row + LANES, :LANES] = hi
            parts_ref[row : row + LANES, LANES:] = lo


def far_kernel(flag_ref, parts_ref, received_ref, low_ref, high_ref, out_ref, split_ref, *, ops):
    ncoef, leaves = out_ref.shape
    sources = received_ref.shape[0]
    hi, lo = split(pad_lanes(received_ref[...]))
    table = lax.dot_general(
        parts_ref[...], jnp.concatenate([hi, hi], axis=1), NT, preferred_element_type=jnp.float32
    ) + lax.dot_general(parts_ref[:, :LANES], lo, NT, preferred_element_type=jnp.float32)
    for k in range(ops):
        hi, lo = split(table[LANES * k : LANES * (k + 1), :])
        split_ref[:LANES, sources * k : sources * (k + 1)] = hi
        split_ref[LANES:, sources * k : sources * (k + 1)] = lo

    def product(counts_ref):
        both = jnp.dot(split_ref[...], counts_ref[...], preferred_element_type=jnp.float32)
        return both[:ncoef, :] + both[LANES : LANES + ncoef, :]

    out_ref[...] = product(low_ref)
    flagged = flag_ref[0, 0, 0]
    for i in range(1, flag_ref.shape[0]):
        flagged = flagged | flag_ref[i, 0, 0]

    @pl.when(flagged > 0)
    def _():
        out_ref[...] += product(high_ref)


def near_kernel(second_ref, own_ref, first_ref, list_ref, out_ref, picked_ref, place_ref, pot_ref):
    near, leaves = list_ref.shape
    groups = leaves // LANES
    even = lax.axis_index("slab") % 2 == 0
    lane = lax.broadcasted_iota(jnp.int32, (near, LANES), 1)
    for g in range(groups):
        idx = 8 * (lane & 15) + 2 * g + (lane >> 6)
        part = (lane & 63) >> 4
        row = jnp.zeros((near, LANES), jnp.int32)
        for s in range(groups):
            row = jnp.where(part == s, lane_gather(list_ref[:, LANES * s : LANES * (s + 1)], idx), row)
        block = row >> 9
        block = jnp.where(even, 2 - block, block)
        place_ref[g] = (block << 9) + ((row & 7) << 6) + ((row >> 3) & 63)
    windows = (first_ref, own_ref, second_ref)
    rows = 4 * PTS

    def step(g, carry):
        at = pl.ds(pl.multiple_of(g * LANES, LANES), LANES)
        tx, ty, tz = (own_ref[PTS * c : PTS * (c + 1), at] for c in range(3))
        acc = jnp.zeros((PTS, LANES), jnp.float32)
        for n in range(near):
            place = jnp.broadcast_to(place_ref[g, n : n + 1, :], (8, LANES))
            idx = place & (LANES - 1)
            group = place >> 7
            picked = [jnp.zeros((8, LANES), jnp.float32) for _ in range(rows // 8)]
            for s in range(3 * groups):
                here = group == s
                for r in range(rows // 8):
                    source = windows[s // groups][8 * r : 8 * r + 8, LANES * (s % groups) : LANES * (s % groups + 1)]
                    picked[r] = jnp.where(here, lane_gather(source, idx), picked[r])
            for r in range(rows // 8):
                picked_ref[n, 8 * r : 8 * r + 8, :] = picked[r]
            for p in range(PTS):
                sx, sy, sz, q = (picked_ref[n, PTS * c + p : PTS * c + p + 1, :] for c in range(4))
                dx, dy, dz = tx - sx, ty - sy, tz - sz
                acc += q * lax.rsqrt(dx * dx + dy * dy + (dz * dz + SOFT2))
        pot_ref[g] = acc
        return carry

    lax.fori_loop(0, groups, step, 0)
    half = LANES // 2
    pieces = []
    for g in range(groups):
        pot = pot_ref[g]
        pieces += [pot[:, :half], pot[:, half:]]
    out_ref[...] = jnp.concatenate(pieces, axis=0).T


def shards(
    coords,
    charges,
    multipoles,
    operators,
    send_list,
    near_list,
    m2l_source,
    m2l_target,
    m2l_operator,
):
    ncoef, leaves = multipoles.shape
    npoints = charges.shape[0]
    near = near_list.shape[1]
    entries = m2l_source.shape[1]
    ops = operators.shape[0]
    sources = send_list.shape[1]
    peers = lax.axis_size("grp")
    f32, bf16 = jnp.float32, jnp.bfloat16

    tiles = npoints // LANES
    coords3 = jnp.transpose(coords.reshape(3, tiles, LANES), (1, 0, 2))
    table, outgoing = pl.pallas_call(
        prep_kernel,
        name="prep",
        out_shape=(
            jax.ShapeDtypeStruct((4 * PTS, leaves), f32),
            jax.ShapeDtypeStruct((sources, ncoef), f32),
        ),
        in_specs=[ANY] * 4,
        out_specs=(VMEM, VMEM),
        scratch_shapes=[
            pltpu.VMEM((tiles, 3, LANES), f32),
            pltpu.VMEM((tiles, LANES), f32),
            pltpu.VMEM((ncoef, leaves), f32),
            pltpu.VMEM((1, sources), jnp.int32),
            pltpu.SemaphoreType.DMA((4,)),
        ],
        compiler_params=WIDE,
    )(coords3, charges.reshape(tiles, LANES), multipoles, send_list)
    received = lax.all_to_all(
        outgoing.reshape(peers, sources // peers, ncoef), "grp", split_axis=0, concat_axis=0, tiled=True
    ).reshape(sources, ncoef)
    slabs = lax.axis_size("slab")

    def exchange(start):
        ties = [(i, i + 1) for i in range(start, slabs - 1, 2)]
        return lax.ppermute(table, "slab", ties + [(b, a) for a, b in ties])

    first = exchange(0)
    second = exchange(1)

    nrows = ops // 2 * sources
    block = min(nrows, 512)
    low, high, flag, parts = pl.pallas_call(
        functools.partial(counts_kernel, sources=sources, leaves=leaves, chunk=512, ops=ops),
        name="counts",
        grid=(nrows // block,),
        out_shape=(
            jax.ShapeDtypeStruct((2, nrows, leaves), bf16),
            jax.ShapeDtypeStruct((2, nrows, leaves), bf16),
            jax.ShapeDtypeStruct((nrows // block, 1, 1), jnp.int32),
            jax.ShapeDtypeStruct((ops * LANES, 2 * LANES), bf16),
        ),
        in_specs=[pl.BlockSpec((1, entries), lambda i: (0, 0))] * 3
        + [pl.BlockSpec((ncoef * ops, ncoef), lambda i: (0, 0))],
        out_specs=(
            pl.BlockSpec((2, block, leaves), lambda i: (0, i, 0)),
            pl.BlockSpec((2, block, leaves), lambda i: (0, i, 0)),
            pl.BlockSpec((1, 1, 1), lambda i: (i, 0, 0), memory_space=pltpu.SMEM),
            pl.BlockSpec((ops * LANES, 2 * LANES), lambda i: (0, 0)),
        ),
        scratch_shapes=[pltpu.VMEM((2, block, leaves), f32), pltpu.VMEM((ncoef * ops, LANES), f32)],
        compiler_params=PARAMS,
    )(m2l_source, m2l_target, m2l_operator, jnp.transpose(operators, (1, 0, 2)).reshape(ncoef * ops, ncoef))

    local_exp = pl.pallas_call(
        functools.partial(far_kernel, ops=ops),
        name="far",
        out_shape=jax.ShapeDtypeStruct((ncoef, leaves), f32),
        in_specs=[pl.BlockSpec(memory_space=pltpu.SMEM)] + [VMEM] * 4,
        out_specs=VMEM,
        scratch_shapes=[pltpu.VMEM((2 * LANES, ops * sources), bf16)],
        compiler_params=PARAMS,
    )(flag, parts, received, low.reshape(ops * sources, leaves), high.reshape(ops * sources, leaves))

    near_potential = pl.pallas_call(
        near_kernel,
        name="near",
        out_shape=jax.ShapeDtypeStruct((tiles, LANES), f32),
        in_specs=[VMEM] * 4,
        out_specs=VMEM,
        scratch_shapes=[
            pltpu.VMEM((near, 4 * PTS, LANES), f32),
            pltpu.VMEM((leaves // LANES, near, LANES), jnp.int32),
            pltpu.VMEM((leaves // LANES, PTS, LANES), f32),
        ],
        compiler_params=PARAMS,
    )(second, table, first, near_list.T)
    return (local_exp, near_potential.reshape(npoints))


def solution(mesh):
    both = ("slab", "grp")
    return jax.shard_map(
        shards,
        mesh=mesh,
        in_specs=(
            P(None, both),
            P(both),
            P(None, both),
            P(),
            P(both, None),
            P(both, None),
            P(both, None),
            P(both, None),
            P(both, None),
        ),
        out_specs=(P(None, both), P(both)),
        check_vma=False,
    )
```

time: 46.6 us -> 24.3 us (0.52)
  the two profiles are of different devices: /device:TPU:0 before, /device:TPU:11 now
where the time goes in v2:
time: 24.3 us; the launch traced here: 24 us
  Pallas kernels  12.4 us (51%)
  starting transfers between devices  9.83 us (40%)
  local copies, waits for them, and re-layouts  1.06 us (4%)
  between operations  0.74 us (3%)
    all_to_all x1, starting transfers between devices, shards(): lax.all_to_all(outgoing.reshape(peers, sources // peers, ncoef), 'grp', s...  5.27 us
    pallas_call x1, Pallas kernels, shards(): pl.pallas_call(near_kernel, name='near', out_shape=jax.ShapeDtypeStruct((...  4.72 us
    ppermute x2, starting transfers between devices, exchange(): return lax.ppermute(table, 'slab', ties + [(b, a) for a, b in ties])  4.55 us
    pallas_call x1, Pallas kernels, shards(): pl.pallas_call(functools.partial(counts_kernel, sources=sources, leaves=l...  3.49 us
    pallas_call x1, Pallas kernels, shards(): pl.pallas_call(functools.partial(far_kernel, ops=ops), name='far', out_sh...  2.14 us
    pallas_call x1, Pallas kernels, shards(): pl.pallas_call(prep_kernel, name='prep', out_shape=(jax.ShapeDtypeStruct(...  2.02 us
    unnamed x12, local copies, waits for them, and re-layouts  1.06 us
  transfers between devices with their start and end apart: 3, of which 0 were waited for; matrix products, arithmetic and copies ran while one was open for 0% of the time, Pallas kernels for 23%

profile of v2, /device:TPU:11, one launch (start us, length us, event | category | flops | bytes accessed | tf_op | source)
XLA Modules:
  0.0 24.0 jit_solution(16278102689071853355)
XLA Ops:
  0.6 2.0 %prep.1 = (f32[64,512]{1,0:T(8,128)}, f32[128,121]{1,0:T(8,128)}) custom-call(f32[64,3,128]{2,1,0:T(4,128)} %bitcast.18, f32[64,128]{1,0:T(8,128)} %bitcast.21, f32[121,512]{1,0:T(8,128)} %multipoles_hbm.1, s32[1,128]{1,0:T(1,128)} %send_hbm.1), custom_call_target="tpu_custom_call" | custom-call | tf_op jit(solution)/shard_map/prep/pallas_call | solution.py:216
  2.7 0.2 collective-permute-start.1
  2.9 4.3 %collective-permute-start = (f32[64,512]{1,0:T(8,128)}, f32[64,512]{1,0:T(8,128)S(1)}, u32[]{:S(2)}, u32[]{:S(2)}) collective-permute-start(f32[64,512]{1,0:T(8,128)} %get-tuple-element.13.own_ref), channel_id=1, source_target_pairs={{8,16},{16,8},{9,17},{17,9},{10,18},{18,10},{11,19},{19,11},{12,20... | collective-permute-start | bytes 393224 | tf_op jit(solution)/shard_map/ppermute | solution.py:241
  7.2 0.0 copy-start.3
  7.2 0.0 copy-start.4
  7.2 0.0 copy-start.5
  7.3 5.3 %all-to-all-start = ((f32[8,16,121]{2,1,0:T(8,128)}), f32[8,16,121]{2,1,0:T(8,128)S(1)}, u32[]{:S(2)}, u32[]{:S(2)}) async-start(f32[8,16,121]{2,1,0:T(8,128)} %bitcast.19), calls=%async_computation | async-start | bytes 131072 | tf_op jit(solution)/shard_map/all_to_all | solution.py:234
  12.5 0.0 copy-done.3
  12.5 0.0 copy-done.4
  12.5 0.0 copy-done.5
  12.5 0.0 copy-start
  12.6 1.0 %copy-done = f32[8,121,121]{2,0,1:T(8,128)S(1)} copy-done((f32[8,121,121]{2,0,1:T(8,128)S(1)}, f32[8,121,121]{2,0,1:T(8,128)}, u32[]{:S(2)}) %copy-start) | copy-done | bytes 468536
  13.6 3.5 %counts.1 = (bf16[2,512,512]{2,1,0:T(8,128)(2,1)S(1)}, bf16[2,512,512]{2,1,0:T(8,128)(2,1)S(1)}, s32[1,1,1]{2,1,0:T(1,128)}, bf16[1024,256]{1,0:T(8,128)(2,1)S(1)}) custom-call(s32[1,4096]{1,0:T(1,128)S(1)} %copy-done.3, s32[1,4096]{1,0:T(1,128)S(1)} %copy-done.4, s32[1,4096]{1,0:T(1,128)S(1)} %copy-done.5, f32[968,121]{1,0:T(8,128)S(1)} %bitcast.15), custom_call_target="tpu_custom_call" | custom-call | tf_op jit(solution)/shard_map/counts/pallas_call | solution.py:248
  17.1 0.0 all-to-all-done
  17.1 0.0 copy-start.1
  17.1 0.0 copy-start.2
  17.1 2.1 %far.1 = f32[121,512]{1,0:T(8,128)} custom-call(s32[1,1,1]{2,1,0:T(1,128)} %get-tuple-element.8.flag_ref, bf16[1024,256]{1,0:T(8,128)(2,1)S(1)} %get-tuple-element.9.parts_ref, f32[128,121]{1,0:T(8,128)S(1)} %bitcast.16, bf16[1024,512]{1,0:T(8,128)(2,1)S(1)} %bitcast.13, bf16[1024,512]{1,0:T(8,128)(2,1)S(1)} %bitcast.14), custom_call_target="tpu_custom_call" | custom-call | tf_op jit(solution)/shard_map/far/pallas_call | solution.py:270
  19.3 0.0 collective-permute-done.1.first_ref
  19.3 0.0 collective-permute-done.second_ref
  19.3 0.0 copy-done.1
  19.3 0.0 copy-done.2
  19.3 4.7 %near.1 = f32[64,128]{1,0:T(8,128)} custom-call(f32[64,512]{1,0:T(8,128)S(1)} %collective-permute-done.second_ref, f32[64,512]{1,0:T(8,128)S(1)} %copy-done.1, f32[64,512]{1,0:T(8,128)S(1)} %collective-permute-done.1.first_ref, s32[8,512]{1,0:T(8,128)S(1)} %bitcast.17), custom_call_target="tpu_custom_call" | custom-call | tf_op jit(solution)/shard_map/near/pallas_call | solution.py:280
Async XLA Ops:
  2.7 16.6 %collective-permute-start.1 = (f32[64,512]{1,0:T(8,128)}, f32[64,512]{1,0:T(8,128)S(1)}, u32[]{:S(2)}, u32[]{:S(2)}) collective-permute-start(f32[64,512]{1,0:T(8,128)} %get-tuple-element.13.own_ref), channel_id=1, source_target_pairs={{0,8},{16,24},{8,0},{24,16},{1,9},{17,25},{9,1},{25,17},{2,10},{18... | collective-permute-start | bytes 393224 | tf_op jit(solution)/shard_map/ppermute | solution.py:241
  2.9 16.4 %collective-permute-start = (f32[64,512]{1,0:T(8,128)}, f32[64,512]{1,0:T(8,128)S(1)}, u32[]{:S(2)}, u32[]{:S(2)}) collective-permute-start(f32[64,512]{1,0:T(8,128)} %get-tuple-element.13.own_ref), channel_id=1, source_target_pairs={{8,16},{16,8},{9,17},{17,9},{10,18},{18,10},{11,19},{19,11},{12,20... | collective-permute-start | bytes 393224 | tf_op jit(solution)/shard_map/ppermute | solution.py:241
  7.2 5.3 %copy-start.3 = (s32[1,4096]{1,0:T(1,128)S(1)}, s32[1,4096]{1,0:T(1,128)}, u32[]{:S(2)}) copy-start(s32[1,4096]{1,0:T(1,128)} %source_ref.1) | copy-start | bytes 49156
  7.2 5.3 %copy-start.4 = (s32[1,4096]{1,0:T(1,128)S(1)}, s32[1,4096]{1,0:T(1,128)}, u32[]{:S(2)}) copy-start(s32[1,4096]{1,0:T(1,128)} %target_ref.1) | copy-start | bytes 49156
  7.2 5.3 %copy-start.5 = (s32[1,4096]{1,0:T(1,128)S(1)}, s32[1,4096]{1,0:T(1,128)}, u32[]{:S(2)}) copy-start(s32[1,4096]{1,0:T(1,128)} %operator_ref.1) | copy-start | bytes 49156
  7.3 9.8 %all-to-all-start = ((f32[8,16,121]{2,1,0:T(8,128)}), f32[8,16,121]{2,1,0:T(8,128)S(1)}, u32[]{:S(2)}, u32[]{:S(2)}) async-start(f32[8,16,121]{2,1,0:T(8,128)} %bitcast.19), calls=%async_computation | async-start | bytes 131072 | tf_op jit(solution)/shard_map/all_to_all | solution.py:234
  12.5 1.0 %copy-start = (f32[8,121,121]{2,0,1:T(8,128)S(1)}, f32[8,121,121]{2,0,1:T(8,128)}, u32[]{:S(2)}) copy-start(f32[8,121,121]{2,0,1:T(8,128)} %param.12) | copy-start | bytes 1405540
  17.1 2.2 %copy-start.1 = (f32[64,512]{1,0:T(8,128)S(1)}, f32[64,512]{1,0:T(8,128)}, u32[]{:S(2)}) copy-start(f32[64,512]{1,0:T(8,128)} %get-tuple-element.13.own_ref) | copy-start | bytes 393220
  17.1 2.2 %copy-start.2 = (s32[512,8]{0,1:T(8,128)S(1)}, s32[512,8]{0,1:T(8,128)}, u32[]{:S(2)}) copy-start(s32[512,8]{0,1:T(8,128)} %param.14) | copy-start | bytes 49156

commit v3 on v2

v3 whole, which is shorter than its diff:
```python
import functools

import jax
import jax.numpy as jnp
from jax import lax
from jax.experimental import pallas as pl
from jax.experimental.pallas import tpu as pltpu
from jax.sharding import PartitionSpec as P

SOFT2 = 0.0625
LANES = 128
PTS = 16
SCALE = 2.0**20
MARK = jnp.bfloat16
VMEM = pl.BlockSpec(memory_space=pltpu.VMEM)
ANY = pl.BlockSpec(memory_space=pl.ANY)
PARAMS = pltpu.CompilerParams(vmem_limit_bytes=24 * 1024 * 1024)
NT = (((1,), (1,)), ((), ()))


def lane_gather(x, idx):
    return jnp.take_along_axis(x, idx, axis=1, mode="promise_in_bounds")


def split(x):
    hi = x.astype(jnp.bfloat16)
    return hi, (x - hi.astype(jnp.float32)).astype(jnp.bfloat16)


def pad_lanes(x):
    return jnp.concatenate([x, jnp.zeros((x.shape[0], LANES - x.shape[1]), x.dtype)], axis=1)


def prep_kernel(coords_hbm, charges_hbm, multipoles_hbm, send_hbm, *refs, others):
    sources, refs = refs[:others], refs[others:]
    (table_ref, table_hbm, out_ref, *targets), refs = refs[: others + 3], refs[others + 3 :]
    coords_ref, charges_ref, multipoles_ref, send_ref, sems = refs
    pairs = (
        (coords_hbm, coords_ref),
        (charges_hbm, charges_ref),
        (send_hbm, send_ref),
        (multipoles_hbm, multipoles_ref),
        *zip(sources, targets),
    )
    copies = [pltpu.make_async_copy(src, dst, sems.at[i]) for i, (src, dst) in enumerate(pairs)]
    for copy in copies:
        copy.start()
    copies[0].wait()
    copies[1].wait()
    for c in range(4):
        rows = charges_ref[...] if c == 3 else coords_ref[:, c, :]
        cols = rows.T
        for pair in range(4):
            a = cols[32 * pair : 32 * pair + 16, :]
            b = cols[32 * pair + 16 : 32 * pair + 32, :]
            table_ref[16 * c : 16 * c + 16, LANES * pair : LANES * (pair + 1)] = jnp.concatenate([a, b], axis=1)
    whole = pltpu.make_async_copy(table_ref, table_hbm, sems.at[len(copies)])
    whole.start()
    copies[2].wait()
    copies[3].wait()
    ncoef, leaves = multipoles_ref.shape
    for sb in range(send_ref.shape[1] // LANES):
        send = send_ref[:, LANES * sb : LANES * (sb + 1)]
        lane = send & (LANES - 1)
        group = send >> 7
        idx = jnp.broadcast_to(lane, (ncoef, LANES))
        picked = jnp.zeros((ncoef, LANES), jnp.float32)
        for g in range(leaves // LANES):
            got = lane_gather(multipoles_ref[:, LANES * g : LANES * (g + 1)], idx)
            picked = jnp.where(group == g, got, picked)
        out_ref[LANES * sb : LANES * (sb + 1), :] = picked.T
    for copy in copies[4:]:
        copy.wait()
    whole.wait()


def decode(acc):
    odd = jnp.floor(acc * (1.0 / 8192.0))
    return acc - 8192.0 * odd, odd + 2048.0


def near_kernel(
    second_ref, own_ref, first_ref, list_ref, source_ref, target_ref, operator_ref, operators_ref,
    near_ref, low_ref, acc_ref, peak_ref, parts_ref,
    packed_ref, picked_ref, place_ref, pot_ref, wide_ref, a_ref, b_ref, *, ops, sources,
):
    near, leaves = list_ref.shape
    ncoef = operators_ref.shape[1]
    nrows = acc_ref.shape[0]
    block, chunk = a_ref.shape
    groups = leaves // LANES
    each = ops // groups
    f32, bf16 = jnp.float32, jnp.bfloat16
    even = lax.axis_index("slab") % 2 == 0
    lane = lax.broadcasted_iota(jnp.int32, (near, LANES), 1)
    for g in range(groups):
        idx = 8 * (lane & 15) + 2 * g + (lane >> 6)
        part = (lane & 63) >> 4
        row = jnp.zeros((near, LANES), jnp.int32)
        for s in range(groups):
            row = jnp.where(part == s, lane_gather(list_ref[:, LANES * s : LANES * (s + 1)], idx), row)
        side = row >> 9
        side = jnp.where(even, 2 - side, side)
        place_ref[g] = (side << 9) + ((row & 7) << 6) + ((row >> 3) & 63)
    wide_ref[...] = pad_lanes(operators_ref[...])
    acc_ref[...] = jnp.full(acc_ref.shape, -(2.0**24), f32)
    iota = lax.broadcasted_iota(jnp.int32, (max(block, leaves), LANES), 0).astype(jnp.int16).reshape(-1, 16, LANES)
    zero = jnp.zeros((1, 16, LANES), bf16)
    one = jnp.ones((1, 16, LANES), bf16)

    def spread(row, dtype):
        return jnp.broadcast_to(row, (16, LANES)).astype(dtype)[None]

    def columns(ref, g, c):
        return ref[:, pl.ds(pl.multiple_of(g * chunk + c * LANES, LANES), LANES)]

    def mark_codes(g, k):
        for c in range(chunk // LANES):
            op = columns(operator_ref, g, c)
            code = spread((op >> 1) * sources + columns(source_ref, g, c) - block * k, jnp.int16)
            weight = spread(jnp.where((op & 1) == 1, 8192.0, 1.0), bf16)
            marks = jnp.where(iota[: block // 16] == code, weight, zero).reshape(block, LANES)
            a_ref[:, LANES * c : LANES * (c + 1)] = marks.astype(MARK)

    def mark_leaves(g, h):
        size = leaves // 2
        for c in range(chunk // LANES):
            leaf = spread(columns(target_ref, g, c) - size * h, jnp.int16)
            marks = jnp.where(iota[: size // 16] == leaf, one, zero).reshape(size, LANES)
            b_ref[size * h : size * (h + 1), LANES * c : LANES * (c + 1)] = marks.astype(MARK)

    def count(k, h):
        to = (slice(block * k, block * (k + 1)), slice(leaves // 2 * h, leaves // 2 * (h + 1)))
        acc_ref[to] += lax.dot_general(a_ref[...], b_ref[to[1], :], NT, preferred_element_type=f32)

    def cut(g):
        for j in range(each):
            place = each * g + j
            op = 2 * lax.rem(place, ops // 2) + lax.div(place, ops // 2)
            matrix = wide_ref[pl.ds(op, ncoef, stride=ops), :]
            matrix = jnp.concatenate([matrix, jnp.zeros((LANES - ncoef, LANES), f32)], axis=0)
            hi, lo = split(matrix)
            parts_ref[pl.ds(pl.multiple_of(place * LANES, LANES), LANES), :] = jnp.concatenate([hi, lo], axis=1)

    for g in range(groups):
        cut(g)
    for k, ref in enumerate((first_ref, own_ref, second_ref)):
        x, y, z = (
            jnp.clip(jnp.floor(ref[PTS * c : PTS * (c + 1), :] * SCALE + 0.5), -SCALE, SCALE - 1.0).astype(jnp.int32)
            for c in range(3)
        )
        packed_ref[:PTS, leaves * k : leaves * (k + 1)] = (x << 11) | ((y >> 10) & 2047)
        packed_ref[PTS:, leaves * k : leaves * (k + 1)] = (z << 11) | (y & 1023)

    def gather(place):
        idx = place & (LANES - 1)
        group = place >> 7
        words = [jnp.zeros((8, LANES), jnp.int32) for _ in range(2 * PTS // 8)]
        charge = [jnp.zeros((8, LANES), f32) for _ in range(PTS // 8)]
        for s in range(3 * groups):
            here = group == s
            window = (first_ref, own_ref, second_ref)[s // groups]
            at = slice(LANES * (s % groups), LANES * (s % groups + 1))
            for r in range(2 * PTS // 8):
                got = lane_gather(packed_ref[8 * r : 8 * r + 8, LANES * s : LANES * (s + 1)], idx)
                words[r] = jnp.where(here, got, words[r])
            for r in range(PTS // 8):
                got = lane_gather(window[3 * PTS + 8 * r : 3 * PTS + 8 * r + 8, at], idx)
                charge[r] = jnp.where(here, got, charge[r])
        return words, charge

    def step(g, carry):
        for k in range(1, nrows // block):
            mark_codes(g, k)
            for h in range(2):
                mark_leaves(g, h)
                count(k, h)
        mark_codes(g, 0)
        at = pl.ds(pl.multiple_of(g * LANES, LANES), LANES)
        tx, ty, tz = (own_ref[PTS * c : PTS * (c + 1), at] * SCALE for c in range(3))
        square = tx * tx + ty * ty + (tz * tz + SOFT2 * SCALE * SCALE)
        tx, ty, tz = -2.0 * tx, -2.0 * ty, -2.0 * tz
        acc = jnp.zeros((PTS, LANES), f32)
        for n in range(near):
            if n % (near // 2) == 0:
                mark_leaves(g, n // (near // 2))
                count(0, n // (near // 2))
            words, charge = gather(jnp.broadcast_to(place_ref[g, n : n + 1, :], (8, LANES)))
            for r in range(PTS // 8):
                first, second = words[r], words[PTS // 8 + r]
                x = (first >> 11).astype(f32)
                y = (((first << 21) >> 11) | (second & 1023)).astype(f32)
                z = (second >> 11).astype(f32)
                for k, row in enumerate((x, y, z, charge[r], x * x + y * y + z * z)):
                    picked_ref[n, PTS * k + 8 * r : PTS * k + 8 * r + 8, :] = row
            for p in range(PTS):
                sx, sy, sz, q, far = (picked_ref[n, PTS * c + p : PTS * c + p + 1, :] for c in range(5))
                acc += q * lax.rsqrt((square + far) + tx * sx + (ty * sy + tz * sz))
        pot_ref[g] = acc * SCALE
        return carry

    lax.fori_loop(0, groups, step, 0)
    half = LANES // 2
    pieces = []
    for g in range(groups):
        pot = pot_ref[g]
        pieces += [pot[:, :half], pot[:, half:]]
    near_ref[...] = jnp.concatenate(pieces, axis=0).T
    count_even, count_odd = decode(acc_ref[...])
    low_ref[:nrows, :] = count_even.astype(bf16)
    low_ref[nrows:, :] = count_odd.astype(bf16)
    peak_ref[...] = jnp.max(jnp.maximum(count_even, count_odd).reshape(-1, 8, leaves), axis=0)


def far_kernel(peak_ref, parts_ref, received_ref, low_ref, acc_ref, out_ref, split_ref, *, ops):
    ncoef, leaves = out_ref.shape
    sources = received_ref.shape[0]
    nrows = acc_ref.shape[0]
    hi, lo = split(pad_lanes(received_ref[...]))
    table = lax.dot_general(
        parts_ref[...], jnp.concatenate([hi, hi], axis=1), NT, preferred_element_type=jnp.float32
    ) + lax.dot_general(parts_ref[:, :LANES], lo, NT, preferred_element_type=jnp.float32)
    for k in range(ops):
        hi, lo = split(table[LANES * k : LANES * (k + 1), :])
        split_ref[:LANES, sources * k : sources * (k + 1)] = hi
        split_ref[LANES:, sources * k : sources * (k + 1)] = lo
    both = jnp.dot(split_ref[...], low_ref[...], preferred_element_type=jnp.float32)
    out_ref[...] = both[:ncoef, :] + both[LANES : LANES + ncoef, :]

    @pl.when(jnp.max(peak_ref[...]) > 256.0)
    def _():
        for i, counts in enumerate(decode(acc_ref[...])):
            at = slice(nrows * i, nrows * (i + 1))
            missing = (counts - low_ref[at, :].astype(jnp.float32)).astype(jnp.bfloat16)
            both = jnp.dot(split_ref[:, at], missing, preferred_element_type=jnp.float32)
            out_ref[...] += both[:ncoef, :] + both[LANES : LANES + ncoef, :]


def shards(
    coords,
    charges,
    multipoles,
    operators,
    send_list,
    near_list,
    m2l_source,
    m2l_target,
    m2l_operator,
):
    ncoef, leaves = multipoles.shape
    npoints = charges.shape[0]
    near = near_list.shape[1]
    entries = m2l_source.shape[1]
    ops = operators.shape[0]
    sources = send_list.shape[1]
    peers = lax.axis_size("grp")
    f32, bf16 = jnp.float32, jnp.bfloat16

    tiles = npoints // LANES
    points = (jnp.transpose(coords.reshape(3, tiles, LANES), (1, 0, 2)), charges.reshape(tiles, LANES))
    others = (
        near_list.T,
        m2l_source,
        m2l_target,
        m2l_operator,
        jnp.transpose(operators, (1, 0, 2)).reshape(ncoef * ops, ncoef),
    )
    table, sent, outgoing, near_list, m2l_source, m2l_target, m2l_operator, operators = pl.pallas_call(
        functools.partial(prep_kernel, others=len(others)),
        name="prep",
        out_shape=(
            pltpu.VMEM((4 * PTS, leaves), f32),
            pltpu.HBM((4 * PTS, leaves), f32),
            pltpu.VMEM((sources, ncoef), f32),
            *(pltpu.VMEM(x.shape, x.dtype) for x in others),
        ),
        in_specs=[ANY] * (4 + len(others)),
        out_specs=(VMEM, ANY, VMEM) + (VMEM,) * len(others),
        scratch_shapes=[
            pltpu.VMEM((tiles, 3, LANES), f32),
            pltpu.VMEM((tiles, LANES), f32),
            pltpu.VMEM((ncoef, leaves), f32),
            pltpu.VMEM((1, sources), jnp.int32),
            pltpu.SemaphoreType.DMA((5 + len(others),)),
        ],
        compiler_params=PARAMS,
    )(*(pltpu.with_memory_space_constraint(x, pltpu.HBM) for x in (*points, multipoles, send_list, *others)))
    received = lax.all_to_all(
        outgoing.reshape(peers, sources // peers, ncoef), "grp", split_axis=0, concat_axis=0, tiled=True
    ).reshape(sources, ncoef)
    slabs = lax.axis_size("slab")

    def exchange(start):
        ties = [(i, i + 1) for i in range(start, slabs - 1, 2)]
        return lax.ppermute(sent, "slab", ties + [(b, a) for a, b in ties])

    first = exchange(0)
    second = exchange(1)

    nrows = ops // 2 * sources
    block = min(nrows, 512)
    groups = leaves // LANES
    chunk = entries // groups
    near_potential, low, acc, peak, parts = pl.pallas_call(
        functools.partial(near_kernel, ops=ops, sources=sources),
        name="near_counts",
        out_shape=(
            jax.ShapeDtypeStruct((tiles, LANES), f32),
            pltpu.VMEM((2 * nrows, leaves), bf16),
            pltpu.VMEM((nrows, leaves), f32),
            pltpu.VMEM((8, leaves), f32),
            pltpu.VMEM((ops * LANES, 2 * LANES), bf16),
        ),
        in_specs=[VMEM] * 8,
        out_specs=(VMEM,) * 5,
        scratch_shapes=[
            pltpu.VMEM((2 * PTS, 3 * leaves), jnp.int32),
            pltpu.VMEM((near, 5 * PTS, LANES), f32),
            pltpu.VMEM((groups, near, LANES), jnp.int32),
            pltpu.VMEM((groups, PTS, LANES), f32),
            pltpu.VMEM((ncoef * ops, LANES), f32),
            pltpu.VMEM((block, chunk), MARK),
            pltpu.VMEM((leaves, chunk), MARK),
        ],
        compiler_params=PARAMS,
    )(second, table, first, near_list, m2l_source, m2l_target, m2l_operator, operators)

    local_exp = pl.pallas_call(
        functools.partial(far_kernel, ops=ops),
        name="far",
        out_shape=jax.ShapeDtypeStruct((ncoef, leaves), f32),
        in_specs=[VMEM] * 5,
        out_specs=VMEM,
        scratch_shapes=[pltpu.VMEM((2 * LANES, ops * sources), bf16)],
        compiler_params=PARAMS,
    )(peak, parts, received, low, acc)
    return (local_exp, near_potential.reshape(npoints))


def solution(mesh):
    both = ("slab", "grp")
    return jax.shard_map(
        shards,
        mesh=mesh,
        in_specs=(
            P(None, both),
            P(both),
            P(None, both),
            P(),
            P(both, None),
            P(both, None),
            P(both, None),
            P(both, None),
            P(both, None),
        ),
        out_specs=(P(None, both), P(both)),
        check_vma=False,
    )
```

time: 24.3 us -> 22.1 us (0.909)
  Pallas kernels: 12.4 us -> 9.97 us
  local copies, waits for them, and re-layouts: 1.06 us -> 1.55 us
    pallas_call x3 -> x2, Pallas kernels: 10.2 us -> 8.51 us  [the longest x1 6 us: shards(): pl.pallas_call(functools.partial(near_kernel, ops=ops, sources=sources),...]
    pallas_call x1, Pallas kernels: 2.14 us -> 1.46 us  [shards(): pl.pallas_call(functools.partial(far_kernel, ops=ops), name='far', out_sh...]
    unnamed x12 -> x4, local copies, waits for them, and re-layouts: 1.06 us -> 1.55 us
  transfers between devices with their start and end apart: 3 -> 3, of which waited for: 0 -> 0; matrix products, arithmetic and copies ran while one was open for 0% -> 0% of each run, Pallas kernels for 23% -> 27%
where the time goes in v3:
time: 22.1 us; the launch traced here: 21.9 us
  Pallas kernels  9.97 us (45%)
  starting transfers between devices  9.69 us (44%)
  local copies, waits for them, and re-layouts  1.55 us (7%)
  between operations  0.66 us (3%)
    pallas_call x1, Pallas kernels, shards(): pl.pallas_call(functools.partial(near_kernel, ops=ops, sources=sources),...  6 us
    all_to_all x1, starting transfers between devices, shards(): lax.all_to_all(outgoing.reshape(peers, sources // peers, ncoef), 'grp', s...  5.14 us
    ppermute x2, starting transfers between devices, exchange(): return lax.ppermute(sent, 'slab', ties + [(b, a) for a, b in ties])  4.55 us
    pallas_call x1, Pallas kernels, shards(): pl.pallas_call(functools.partial(prep_kernel, others=len(others)), name='...  2.51 us
    unnamed x4, local copies, waits for them, and re-layouts  1.55 us
    pallas_call x1, Pallas kernels, shards(): pl.pallas_call(functools.partial(far_kernel, ops=ops), name='far', out_sh...  1.46 us
  transfers between devices with their start and end apart: 3, of which 0 were waited for; matrix products, arithmetic and copies ran while one was open for 0% of the time, Pallas kernels for 27%

profile of v3, /device:TPU:11, one launch (start us, length us, event | category | flops | bytes accessed | tf_op | source)
XLA Modules:
  0.0 21.9 jit_solution(8601368632320135085)
XLA Ops:
  0.6 2.5 %prep.1 = (f32[64,512]{1,0:T(8,128)S(1)}, f32[64,512]{1,0:T(8,128)}, f32[128,121]{1,0:T(8,128)}, s32[8,512]{1,0:T(8,128)S(1)}, s32[1,4096]{1,0:T(1,128)S(1)}, /*...) custom-call(f32[64,3,128]{2,1,0:T(4,128)} %bitcast.13, f32[64,128]{1,0:T(8,128)} %bitcast.14, ...), custom_call_target="tpu_custom_call" | custom-call | tf_op jit(solution)/shard_map/prep/pallas_call | solution.py:268
  3.1 0.2 %collective-permute-start.1 = (f32[64,512]{1,0:T(8,128)}, f32[64,512]{1,0:T(8,128)S(1)}, u32[]{:S(2)}, u32[]{:S(2)}) collective-permute-start(f32[64,512]{1,0:T(8,128)} %get-tuple-element.15), channel_id=1, source_target_pairs={{0,8},{16,24},{8,0},{24,16},{1,9},{17,25},{9,1},{25,17},{2,10},{18... | collective-permute-start | bytes 393224 | tf_op jit(solution)/shard_map/ppermute | solution.py:295
  3.4 4.3 %collective-permute-start = (f32[64,512]{1,0:T(8,128)}, f32[64,512]{1,0:T(8,128)S(1)}, u32[]{:S(2)}, u32[]{:S(2)}) collective-permute-start(f32[64,512]{1,0:T(8,128)} %get-tuple-element.15), channel_id=1, source_target_pairs={{8,16},{16,8},{9,17},{17,9},{10,18},{18,10},{11,19},{19,11},{12,20... | collective-permute-start | bytes 393224 | tf_op jit(solution)/shard_map/ppermute | solution.py:295
  7.7 5.1 %all-to-all-start = ((f32[8,16,121]{2,1,0:T(8,128)}), f32[8,16,121]{2,1,0:T(8,128)S(1)}, u32[]{:S(2)}, u32[]{:S(2)}) async-start(f32[8,16,121]{2,1,0:T(8,128)} %bitcast.6), calls=%async_computation | async-start | bytes 131072 | tf_op jit(solution)/shard_map/all_to_all | solution.py:288
  12.8 0.0 collective-permute-done.1.first_ref
  12.9 0.0 collective-permute-done.second_ref
  12.9 0.0 copy-start
  12.9 0.6 %copy-done = f32[64,512]{1,0:T(8,128)} copy-done((f32[64,512]{1,0:T(8,128)}, f32[64,512]{1,0:T(8,128)S(1)}, u32[]{:S(2)}) %copy-start) | copy-done | bytes 131096
  13.5 0.0 copy-start.1
  13.5 0.9 %copy-done.1 = f32[64,512]{1,0:T(8,128)S(1)} copy-done((f32[64,512]{1,0:T(8,128)S(1)}, f32[64,512]{1,0:T(8,128)}, u32[]{:S(2)}) %copy-start.1) | copy-done | bytes 131096
  14.4 6.0 %near_counts.1 = (f32[64,128]{1,0:T(8,128)}, bf16[1024,512]{1,0:T(8,128)(2,1)S(1)}, f32[512,512]{1,0:T(8,128)S(1)}, f32[8,512]{1,0:T(8,128)S(1)}, bf16[1024,256]{1,0:T(8,128)(2,1)S(1)}) custom-call(f32[64,512]{1,0:T(8,128)S(1)} %copy-done.1, f32[64,512]{1,0:T(8,128)S(1)} %get-tuple-element.16.own_ref, f32[64,512]{1,0:T(8,128)S(1)} %collective-permute-done.1.first_ref, ...), custom_call_target="tpu_custom_call" | custom-call | tf_op jit(solution)/shard_map/near_counts/pallas_call | solution.py:304
  20.4 0.0 all-to-all-done
  20.4 1.5 %far.1 = f32[121,512]{1,0:T(8,128)} custom-call(f32[8,512]{1,0:T(8,128)S(1)} %get-tuple-element.22.peak_ref, bf16[1024,256]{1,0:T(8,128)(2,1)S(1)} %get-tuple-element.23.parts_ref, f32[128,121]{1,0:T(8,128)S(1)} %bitcast.11, bf16[1024,512]{1,0:T(8,128)(2,1)S(1)} %get-tuple-element.25.low_ref, f32[512,512]{1,0:T(8,128)S(1)} %get-tuple-element.26.acc_ref), custom_call_target="tpu_custom_call" | custom-call | tf_op jit(solution)/shard_map/far/pallas_call | solution.py:328
Async XLA Ops:
  3.1 9.7 %collective-permute-start.1 = (f32[64,512]{1,0:T(8,128)}, f32[64,512]{1,0:T(8,128)S(1)}, u32[]{:S(2)}, u32[]{:S(2)}) collective-permute-start(f32[64,512]{1,0:T(8,128)} %get-tuple-element.15), channel_id=1, source_target_pairs={{0,8},{16,24},{8,0},{24,16},{1,9},{17,25},{9,1},{25,17},{2,10},{18... | collective-permute-start | bytes 393224 | tf_op jit(solution)/shard_map/ppermute | solution.py:295
  3.4 9.5 %collective-permute-start = (f32[64,512]{1,0:T(8,128)}, f32[64,512]{1,0:T(8,128)S(1)}, u32[]{:S(2)}, u32[]{:S(2)}) collective-permute-start(f32[64,512]{1,0:T(8,128)} %get-tuple-element.15), channel_id=1, source_target_pairs={{8,16},{16,8},{9,17},{17,9},{10,18},{18,10},{11,19},{19,11},{12,20... | collective-permute-start | bytes 393224 | tf_op jit(solution)/shard_map/ppermute | solution.py:295
  7.7 12.7 %all-to-all-start = ((f32[8,16,121]{2,1,0:T(8,128)}), f32[8,16,121]{2,1,0:T(8,128)S(1)}, u32[]{:S(2)}, u32[]{:S(2)}) async-start(f32[8,16,121]{2,1,0:T(8,128)} %bitcast.6), calls=%async_computation | async-start | bytes 131072 | tf_op jit(solution)/shard_map/all_to_all | solution.py:288
  12.9 0.7 %copy-start = (f32[64,512]{1,0:T(8,128)}, f32[64,512]{1,0:T(8,128)S(1)}, u32[]{:S(2)}) copy-start(f32[64,512]{1,0:T(8,128)S(1)} %collective-permute-done.second_ref) | copy-start | bytes 393220
  13.5 0.9 %copy-start.1 = (f32[64,512]{1,0:T(8,128)S(1)}, f32[64,512]{1,0:T(8,128)}, u32[]{:S(2)}) copy-start(f32[64,512]{1,0:T(8,128)} %copy-done) | copy-start | bytes 393220

commit v4 on v3

v4 whole, which is shorter than its diff:
```python
import functools

import jax
import jax.numpy as jnp
from jax import lax
from jax.experimental import pallas as pl
from jax.experimental.pallas import tpu as pltpu
from jax.sharding import PartitionSpec as P

SOFT2 = 0.0625
LANES = 128
PTS = 16
SCALE = 2.0**20
VMEM = pl.BlockSpec(memory_space=pltpu.VMEM)
ANY = pl.BlockSpec(memory_space=pl.ANY)
PARAMS = pltpu.CompilerParams(vmem_limit_bytes=48 * 1024 * 1024)
NT = (((1,), (1,)), ((), ()))


def lane_gather(x, idx):
    return jnp.take_along_axis(x, idx, axis=1, mode="promise_in_bounds")


def split(x):
    hi = x.astype(jnp.bfloat16)
    return hi, (x - hi.astype(jnp.float32)).astype(jnp.bfloat16)


def pad_lanes(x):
    return jnp.concatenate([x, jnp.zeros((x.shape[0], LANES - x.shape[1]), x.dtype)], axis=1)


def prep_kernel(coords_hbm, charges_hbm, multipoles_hbm, send_hbm, *refs, others):
    sources, refs = refs[:others], refs[others:]
    (table_ref, out_ref, *targets), refs = refs[: others + 2], refs[others + 2 :]
    coords_ref, charges_ref, multipoles_ref, send_ref, sems = refs
    pairs = (
        (coords_hbm, coords_ref),
        (charges_hbm, charges_ref),
        (send_hbm, send_ref),
        (multipoles_hbm, multipoles_ref),
        *zip(sources, targets),
    )
    copies = [pltpu.make_async_copy(src, dst, sems.at[i]) for i, (src, dst) in enumerate(pairs)]
    for copy in copies:
        copy.start()
    copies[0].wait()
    copies[1].wait()
    for c in range(4):
        rows = charges_ref[...] if c == 3 else coords_ref[:, c, :]
        cols = rows.T
        for pair in range(4):
            a = cols[32 * pair : 32 * pair + 16, :]
            b = cols[32 * pair + 16 : 32 * pair + 32, :]
            table_ref[16 * c : 16 * c + 16, LANES * pair : LANES * (pair + 1)] = jnp.concatenate([a, b], axis=1)
    copies[2].wait()
    copies[3].wait()
    ncoef, leaves = multipoles_ref.shape
    for sb in range(send_ref.shape[1] // LANES):
        send = send_ref[:, LANES * sb : LANES * (sb + 1)]
        lane = send & (LANES - 1)
        group = send >> 7
        idx = jnp.broadcast_to(lane, (ncoef, LANES))
        picked = jnp.zeros((ncoef, LANES), jnp.float32)
        for g in range(leaves // LANES):
            got = lane_gather(multipoles_ref[:, LANES * g : LANES * (g + 1)], idx)
            picked = jnp.where(group == g, got, picked)
        out_ref[LANES * sb : LANES * (sb + 1), :] = picked.T
    for copy in copies[4:]:
        copy.wait()


def cut_kernel(list_ref, operators_ref, place_ref, parts_ref, wide_ref, *, ops):
    near, leaves = list_ref.shape
    ncoef = operators_ref.shape[1]
    groups = leaves // LANES
    even = lax.axis_index("slab") % 2 == 0
    lane = lax.broadcasted_iota(jnp.int32, (near, LANES), 1)
    for g in range(groups):
        idx = 8 * (lane & 15) + 2 * g + (lane >> 6)
        part = (lane & 63) >> 4
        row = jnp.zeros((near, LANES), jnp.int32)
        for s in range(groups):
            row = jnp.where(part == s, lane_gather(list_ref[:, LANES * s : LANES * (s + 1)], idx), row)
        side = row >> 9
        side = jnp.where(even, 2 - side, side)
        place_ref[g] = (side << 9) + ((row & 7) << 6) + ((row >> 3) & 63)
    wide_ref[...] = pad_lanes(operators_ref[...])
    for op in range(ops):
        matrix = wide_ref[pl.ds(op, ncoef, stride=ops), :]
        matrix = jnp.concatenate([matrix, jnp.zeros((LANES - ncoef, LANES), jnp.float32)], axis=0)
        hi, lo = split(matrix)
        parts_ref[LANES * spot(op, ops) : LANES * (spot(op, ops) + 1), :] = jnp.concatenate([hi, lo], axis=1)


def spot(op, ops):
    return (op % 4) * (ops // 4) + op // 4


def near_kernel(
    second_ref, own_ref, first_ref, place_ref, source_ref, target_ref, operator_ref,
    near_ref, low_ref, rest_ref, inexact_ref,
    packed_ref, picked_ref, pot_ref, acc_ref, pair_ref, a_ref, b_ref, *, ops, sources,
):
    groups, near, _ = place_ref.shape
    leaves = own_ref.shape[1]
    block, chunk = a_ref.shape
    codes = acc_ref.shape[1]
    f32, bf16 = jnp.float32, jnp.bfloat16
    iota = lax.broadcasted_iota(jnp.int32, (max(block, leaves), LANES), 0).astype(jnp.int16).reshape(-1, 16, LANES)
    zero = jnp.zeros((1, 16, LANES), bf16)
    one = jnp.ones((1, 16, LANES), bf16)

    def spread(row, dtype):
        return jnp.broadcast_to(row, (16, LANES)).astype(dtype)[None]

    def columns(ref, g, c):
        return ref[:, pl.ds(pl.multiple_of(g * chunk + c * LANES, LANES), LANES)]

    def mark_leaves(g):
        for c in range(chunk // LANES):
            leaf = spread(columns(target_ref, g, c), jnp.int16)
            marks = jnp.where(iota[: leaves // 16] == leaf, one, zero).reshape(leaves, LANES)
            b_ref[:, LANES * c : LANES * (c + 1)] = marks

    def mark_codes(g, first, size, shift, weigh):
        for c in range(chunk // LANES):
            op = columns(operator_ref, g, c)
            code = spread((op >> shift) * sources + columns(source_ref, g, c) - first, jnp.int16)
            marks = jnp.where(iota[: size // 16] == code, spread(weigh(op), bf16), zero).reshape(size, LANES)
            a_ref[:size, LANES * c : LANES * (c + 1)] = marks

    def products(size):
        return lax.dot_general(b_ref[...], a_ref[:size, :], NT, preferred_element_type=f32)

    def digit_weight(op):
        last = op & 3
        return jnp.where(last == 0, 1.0, jnp.where(last == 1, 64.0, jnp.where(last == 2, 4096.0, 2.0**18)))

    def count(g):
        mark_leaves(g)
        for first in range(0, codes, block):
            size = min(block, codes - first)
            mark_codes(g, first, size, 2, digit_weight)
            acc_ref[:, first : first + size] += products(size)

    acc_ref[...] = jnp.zeros_like(acc_ref)
    for k, ref in enumerate((first_ref, own_ref, second_ref)):
        x, y, z = (
            jnp.clip(jnp.floor(ref[PTS * c : PTS * (c + 1), :] * SCALE + 0.5), -SCALE, SCALE - 1.0).astype(jnp.int32)
            for c in range(3)
        )
        packed_ref[:PTS, leaves * k : leaves * (k + 1)] = (x << 11) | ((y >> 10) & 2047)
        packed_ref[PTS:, leaves * k : leaves * (k + 1)] = (z << 11) | (y & 1023)

    def gather(place):
        idx = place & (LANES - 1)
        group = place >> 7
        words = [jnp.zeros((8, LANES), jnp.int32) for _ in range(2 * PTS // 8)]
        charge = [jnp.zeros((8, LANES), f32) for _ in range(PTS // 8)]
        for s in range(3 * groups):
            here = group == s
            window = (first_ref, own_ref, second_ref)[s // groups]
            at = slice(LANES * (s % groups), LANES * (s % groups + 1))
            for r in range(2 * PTS // 8):
                got = lane_gather(packed_ref[8 * r : 8 * r + 8, LANES * s : LANES * (s + 1)], idx)
                words[r] = jnp.where(here, got, words[r])
            for r in range(PTS // 8):
                got = lane_gather(window[3 * PTS + 8 * r : 3 * PTS + 8 * r + 8, at], idx)
                charge[r] = jnp.where(here, got, charge[r])
        return words, charge

    def step(g, carry):
        count(g)
        at = pl.ds(pl.multiple_of(g * LANES, LANES), LANES)
        tx, ty, tz = (own_ref[PTS * c : PTS * (c + 1), at] * SCALE for c in range(3))
        square = tx * tx + ty * ty + (tz * tz + SOFT2 * SCALE * SCALE)
        tx, ty, tz = -2.0 * tx, -2.0 * ty, -2.0 * tz
        acc = jnp.zeros((PTS, LANES), f32)
        for n in range(near):
            words, charge = gather(jnp.broadcast_to(place_ref[g, n : n + 1, :], (8, LANES)))
            for r in range(PTS // 8):
                first, second = words[r], words[PTS // 8 + r]
                x = (first >> 11).astype(f32)
                y = (((first << 21) >> 11) | (second & 1023)).astype(f32)
                z = (second >> 11).astype(f32)
                for k, row in enumerate((x, y, z, charge[r], x * x + y * y + z * z)):
                    picked_ref[n, PTS * k + 8 * r : PTS * k + 8 * r + 8, :] = row
            for p in range(PTS):
                sx, sy, sz, q, far = (picked_ref[n, PTS * c + p : PTS * c + p + 1, :] for c in range(5))
                acc += q * lax.rsqrt((square + far) + tx * sx + (ty * sy + tz * sz))
        pot_ref[g] = acc * SCALE
        return carry

    lax.fori_loop(0, groups, step, 0)
    half = LANES // 2
    pieces = []
    for g in range(groups):
        pot = pot_ref[g]
        pieces += [pot[:, :half], pot[:, half:]]
    near_ref[...] = jnp.concatenate(pieces, axis=0).T

    value = acc_ref[...]
    total = jnp.zeros_like(value)
    left = value
    for digit in range(4):
        above = jnp.floor(left * (1.0 / 64.0))
        here = left - 64.0 * above
        low_ref[:, codes * digit : codes * (digit + 1)] = here.astype(bf16)
        total += here
        left = above
    total = jnp.where(value < 2.0**24, total, -(2.0**30))
    used = jnp.sum(jnp.where(target_ref[...] < leaves, 1.0, 0.0))
    carried = jnp.sum(total) != used
    inexact_ref[...] = jnp.zeros_like(inexact_ref)

    @pl.when(carried)
    def _():
        pairs = ops // 2 * sources
        for first in range(0, pairs, block):
            size = min(block, pairs - first)
            pair_ref[:, :size] = jnp.full((leaves, size), -(2.0**24), f32)

            def more(g, carry):
                mark_leaves(g)
                mark_codes(g, first, size, 1, lambda op: jnp.where((op & 1) == 1, 8192.0, 1.0))
                pair_ref[:, :size] += products(size)
                return carry

            lax.fori_loop(0, groups, more, 0)
            for lane in range(first, first + size, LANES):
                value = pair_ref[:, lane - first : lane - first + LANES]
                odd = jnp.floor(value * (1.0 / 8192.0))
                for parity, count in enumerate((value - 8192.0 * odd, odd + 2048.0)):
                    to = spot(2 * (lane // sources) + parity, ops) * sources + lane % sources
                    kept = count.astype(bf16)
                    low_ref[:, to : to + LANES] = kept
                    rest_ref[:, to : to + LANES] = (count - kept.astype(f32)).astype(bf16)
        inexact_ref[...] = jnp.ones_like(inexact_ref)


def far_kernel(inexact_ref, parts_ref, received_ref, low_ref, rest_ref, out_ref, split_ref, *, ops):
    ncoef, leaves = out_ref.shape
    sources = received_ref.shape[0]
    hi, lo = split(pad_lanes(received_ref[...]))
    table = lax.dot_general(
        parts_ref[...], jnp.concatenate([hi, hi], axis=1), NT, preferred_element_type=jnp.float32
    ) + lax.dot_general(parts_ref[:, :LANES], lo, NT, preferred_element_type=jnp.float32)
    for k in range(ops):
        hi, lo = split(table[LANES * k : LANES * (k + 1), :])
        split_ref[:LANES, sources * k : sources * (k + 1)] = hi
        split_ref[LANES:, sources * k : sources * (k + 1)] = lo

    def product(counts):
        both = lax.dot_general(split_ref[...], counts, NT, preferred_element_type=jnp.float32)
        return both[:ncoef, :] + both[LANES : LANES + ncoef, :]

    out_ref[...] = product(low_ref[...])

    @pl.when(jnp.max(inexact_ref[...]) > 0.0)
    def _():
        out_ref[...] += product(rest_ref[...])


def shards(
    coords,
    charges,
    multipoles,
    operators,
    send_list,
    near_list,
    m2l_source,
    m2l_target,
    m2l_operator,
):
    ncoef, leaves = multipoles.shape
    npoints = charges.shape[0]
    near = near_list.shape[1]
    entries = m2l_source.shape[1]
    ops = operators.shape[0]
    sources = send_list.shape[1]
    peers = lax.axis_size("grp")
    f32, bf16 = jnp.float32, jnp.bfloat16

    tiles = npoints // LANES
    points = (jnp.transpose(coords.reshape(3, tiles, LANES), (1, 0, 2)), charges.reshape(tiles, LANES))
    others = (
        near_list.T,
        m2l_source,
        m2l_target,
        m2l_operator,
        jnp.transpose(operators, (1, 0, 2)).reshape(ncoef * ops, ncoef),
    )
    table, outgoing, near_list, m2l_source, m2l_target, m2l_operator, operators = pl.pallas_call(
        functools.partial(prep_kernel, others=len(others)),
        name="prep",
        out_shape=(
            pltpu.VMEM((4 * PTS, leaves), f32),
            pltpu.VMEM((sources, ncoef), f32),
            *(pltpu.VMEM(x.shape, x.dtype) for x in others),
        ),
        in_specs=[ANY] * (4 + len(others)),
        out_specs=(VMEM,) * (2 + len(others)),
        scratch_shapes=[
            pltpu.VMEM((tiles, 3, LANES), f32),
            pltpu.VMEM((tiles, LANES), f32),
            pltpu.VMEM((ncoef, leaves), f32),
            pltpu.VMEM((1, sources), jnp.int32),
            pltpu.SemaphoreType.DMA((4 + len(others),)),
        ],
        compiler_params=PARAMS,
    )(*(pltpu.with_memory_space_constraint(x, pltpu.HBM) for x in (*points, multipoles, send_list, *others)))
    received = lax.all_to_all(
        outgoing.reshape(peers, sources // peers, ncoef), "grp", split_axis=0, concat_axis=0, tiled=True
    ).reshape(sources, ncoef)
    slabs = lax.axis_size("slab")

    def exchange(start):
        ties = [(i, i + 1) for i in range(start, slabs - 1, 2)]
        return lax.ppermute(table, "slab", ties + [(b, a) for a, b in ties])

    first = exchange(0)
    second = exchange(1)

    codes = ops // 4 * sources
    block = min(2 * codes, 512)
    groups = leaves // LANES
    chunk = entries // groups
    places, parts = pl.pallas_call(
        functools.partial(cut_kernel, ops=ops),
        name="cut",
        out_shape=(
            jax.ShapeDtypeStruct((groups, near, LANES), jnp.int32),
            jax.ShapeDtypeStruct((ops * LANES, 2 * LANES), bf16),
        ),
        in_specs=[VMEM] * 2,
        out_specs=(VMEM,) * 2,
        scratch_shapes=[pltpu.VMEM((ncoef * ops, LANES), f32)],
        compiler_params=PARAMS,
    )(near_list, operators)
    near_potential, low, rest, inexact = pl.pallas_call(
        functools.partial(near_kernel, ops=ops, sources=sources),
        name="near_counts",
        out_shape=(
            jax.ShapeDtypeStruct((tiles, LANES), f32),
            jax.ShapeDtypeStruct((leaves, ops * sources), bf16),
            jax.ShapeDtypeStruct((leaves, ops * sources), bf16),
            jax.ShapeDtypeStruct((8, LANES), f32),
        ),
        in_specs=[VMEM] * 7,
        out_specs=(VMEM,) * 4,
        scratch_shapes=[
            pltpu.VMEM((2 * PTS, 3 * leaves), jnp.int32),
            pltpu.VMEM((near, 5 * PTS, LANES), f32),
            pltpu.VMEM((groups, PTS, LANES), f32),
            pltpu.VMEM((leaves, codes), f32),
            pltpu.VMEM((leaves, block), f32),
            pltpu.VMEM((block, chunk), bf16),
            pltpu.VMEM((leaves, chunk), bf16),
        ],
        compiler_params=PARAMS,
    )(second, table, first, places, m2l_source, m2l_target, m2l_operator)

    local_exp = pl.pallas_call(
        functools.partial(far_kernel, ops=ops),
        name="far",
        out_shape=jax.ShapeDtypeStruct((ncoef, leaves), f32),
        in_specs=[VMEM] * 5,
        out_specs=VMEM,
        scratch_shapes=[pltpu.VMEM((2 * LANES, ops * sources), bf16)],
        compiler_params=PARAMS,
    )(inexact, parts, received, low, rest)
    return (local_exp, near_potential.reshape(npoints))


def solution(mesh):
    both = ("slab", "grp")
    return jax.shard_map(
        shards,
        mesh=mesh,
        in_specs=(
            P(None, both),
            P(both),
            P(None, both),
            P(),
            P(both, None),
            P(both, None),
            P(both, None),
            P(both, None),
            P(both, None),
        ),
        out_specs=(P(None, both), P(both)),
        check_vma=False,
    )
```

time: 22.1 us -> 20.3 us (0.919)
  local copies, waits for them, and re-layouts: 1.55 us -> 0 us
  Pallas kernels: 9.97 us -> 9.7 us
    unnamed x4 -> x0, local copies, waits for them, and re-layouts: 1.55 us -> none
    pallas_call x1, Pallas kernels: 2.51 us -> 2.07 us  [shards(): pl.pallas_call(functools.partial(prep_kernel, others=len(others)), name='...]
  transfers between devices with their start and end apart: 3 -> 3, of which waited for: 0 -> 0; matrix products, arithmetic and copies ran while one was open for 0% -> 0% of each run, Pallas kernels for 27% -> 31%
where the time goes in v4:
time: 20.3 us; the launch traced here: 20.1 us
  Pallas kernels  9.7 us (48%)
  starting transfers between devices  9.69 us (48%)
  between operations  0.67 us (3%)
    pallas_call x1, Pallas kernels, shards(): pl.pallas_call(functools.partial(near_kernel, ops=ops, sources=sources),...  5.98 us
    all_to_all x1, starting transfers between devices, shards(): lax.all_to_all(outgoing.reshape(peers, sources // peers, ncoef), 'grp', s...  5.14 us
    ppermute x2, starting transfers between devices, exchange(): return lax.ppermute(table, 'slab', ties + [(b, a) for a, b in ties])  4.55 us
    pallas_call x1, Pallas kernels, shards(): pl.pallas_call(functools.partial(prep_kernel, others=len(others)), name='...  2.07 us
    pallas_call x1, Pallas kernels, shards(): pl.pallas_call(functools.partial(far_kernel, ops=ops), name='far', out_sh...  1.48 us
  transfers between devices with their start and end apart: 3, of which 0 were waited for; matrix products, arithmetic and copies ran while one was open for 0% of the time, Pallas kernels for 31%

profile of v4, /device:TPU:11, one launch (start us, length us, event | category | flops | bytes accessed | tf_op | source)
XLA Modules:
  0.0 20.1 jit_solution(15703218183446820803)
XLA Ops:
  0.6 2.1 %prep.1 = (f32[64,512]{1,0:T(8,128)S(1)}, f32[128,121]{1,0:T(8,128)}, s32[8,512]{1,0:T(8,128)S(1)}, s32[1,4096]{1,0:T(1,128)S(1)}, s32[1,4096]{1,0:T(1,128)S(1)}...) custom-call(f32[64,3,128]{2,1,0:T(4,128)} %bitcast.13, f32[64,128]{1,0:T(8,128)} %bitcast.14, f32[121,512]{1,0:T(8,128)} %multipoles_hbm.1, ...), custom_call_target="tpu_custom_call" | custom-call | tf_op jit(solution)/shard_map/prep/pallas_call | solution.py:294
  2.7 0.2 %collective-permute-start.1 = (f32[64,512]{1,0:T(8,128)S(1)}, f32[64,512]{1,0:T(8,128)S(1)}, u32[]{:S(2)}, u32[]{:S(2)}) collective-permute-start(f32[64,512]{1,0:T(8,128)S(1)} %get-tuple-element.15.own_ref), channel_id=1, source_target_pairs={{0,8},{16,24},{8,0},{24,16},{1,9},{17,25},{9,1},{25,17},{2,10},{18... | collective-permute-start | bytes 393224 | tf_op jit(solution)/shard_map/ppermute | solution.py:320
  2.9 4.3 %collective-permute-start = (f32[64,512]{1,0:T(8,128)S(1)}, f32[64,512]{1,0:T(8,128)S(1)}, u32[]{:S(2)}, u32[]{:S(2)}) collective-permute-start(f32[64,512]{1,0:T(8,128)S(1)} %get-tuple-element.15.own_ref), channel_id=1, source_target_pairs={{8,16},{16,8},{9,17},{17,9},{10,18},{18,10},{11,19},{19,11},{12,20... | collective-permute-start | bytes 393224 | tf_op jit(solution)/shard_map/ppermute | solution.py:320
  7.3 5.1 %all-to-all-start = ((f32[8,16,121]{2,1,0:T(8,128)}), f32[8,16,121]{2,1,0:T(8,128)S(1)}, u32[]{:S(2)}, u32[]{:S(2)}) async-start(f32[8,16,121]{2,1,0:T(8,128)} %bitcast.6), calls=%async_computation | async-start | bytes 131072 | tf_op jit(solution)/shard_map/all_to_all | solution.py:313
  12.4 0.2 cut.1
  12.6 0.0 collective-permute-done.1.first_ref
  12.6 0.0 collective-permute-done.second_ref
  12.6 6.0 %near_counts.1 = (f32[64,128]{1,0:T(8,128)}, bf16[512,1024]{1,0:T(8,128)(2,1)S(1)}, bf16[512,1024]{1,0:T(8,128)(2,1)S(1)}, f32[8,128]{1,0:T(8,128)S(1)}) custom-call(f32[64,512]{1,0:T(8,128)S(1)} %collective-permute-done.second_ref, f32[64,512]{1,0:T(8,128)S(1)} %get-tuple-element.15.own_ref, f32[64,512]{1,0:T(8,128)S(1)} %collective-permute-done.1.first_ref, ...), custom_call_target="tpu_custom_call" | custom-call | tf_op jit(solution)/shard_map/near_counts/pallas_call | solution.py:341
  18.6 0.0 all-to-all-done
  18.6 1.5 %far.1 = f32[121,512]{1,0:T(8,128)} custom-call(f32[8,128]{1,0:T(8,128)S(1)} %get-tuple-element.22.inexact_ref, bf16[1024,256]{1,0:T(8,128)(2,1)S(1)} %get-tuple-element.23.parts_ref, f32[128,121]{1,0:T(8,128)S(1)} %bitcast.11, bf16[512,1024]{1,0:T(8,128)(2,1)S(1)} %get-tuple-element.25.low_ref, bf16[512,1024]{1,0:T(8,128)(2,1)S(1)} %get-tuple-element.26.rest_ref), custom_call_target="tpu_custom_call" | custom-call | tf_op jit(solution)/shard_map/far/pallas_call | solution.py:364
Async XLA Ops:
  2.7 9.9 %collective-permute-start.1 = (f32[64,512]{1,0:T(8,128)S(1)}, f32[64,512]{1,0:T(8,128)S(1)}, u32[]{:S(2)}, u32[]{:S(2)}) collective-permute-start(f32[64,512]{1,0:T(8,128)S(1)} %get-tuple-element.15.own_ref), channel_id=1, source_target_pairs={{0,8},{16,24},{8,0},{24,16},{1,9},{17,25},{9,1},{25,17},{2,10},{18... | collective-permute-start | bytes 393224 | tf_op jit(solution)/shard_map/ppermute | solution.py:320
  2.9 9.6 %collective-permute-start = (f32[64,512]{1,0:T(8,128)S(1)}, f32[64,512]{1,0:T(8,128)S(1)}, u32[]{:S(2)}, u32[]{:S(2)}) collective-permute-start(f32[64,512]{1,0:T(8,128)S(1)} %get-tuple-element.15.own_ref), channel_id=1, source_target_pairs={{8,16},{16,8},{9,17},{17,9},{10,18},{18,10},{11,19},{19,11},{12,20... | collective-permute-start | bytes 393224 | tf_op jit(solution)/shard_map/ppermute | solution.py:320
  7.3 11.3 %all-to-all-start = ((f32[8,16,121]{2,1,0:T(8,128)}), f32[8,16,121]{2,1,0:T(8,128)S(1)}, u32[]{:S(2)}, u32[]{:S(2)}) async-start(f32[8,16,121]{2,1,0:T(8,128)} %bitcast.6), calls=%async_computation | async-start | bytes 131072 | tf_op jit(solution)/shard_map/all_to_all | solution.py:313

commit v5 on v4

--- a/solution.py
+++ b/solution.py
@@ -104,8 +104,8 @@
 ):
     groups, near, _ = place_ref.shape
     leaves = own_ref.shape[1]
-    block, chunk = a_ref.shape
-    codes = acc_ref.shape[1]
+    _, codes, chunk = a_ref.shape
+    block = pair_ref.shape[1]
     f32, bf16 = jnp.float32, jnp.bfloat16
     iota = lax.broadcasted_iota(jnp.int32, (max(block, leaves), LANES), 0).astype(jnp.int16).reshape(-1, 16, LANES)
     zero = jnp.zeros((1, 16, LANES), bf16)
@@ -117,32 +117,35 @@
     def columns(ref, g, c):
         return ref[:, pl.ds(pl.multiple_of(g * chunk + c * LANES, LANES), LANES)]
 
-    def mark_leaves(g):
-        for c in range(chunk // LANES):
-            leaf = spread(columns(target_ref, g, c), jnp.int16)
-            marks = jnp.where(iota[: leaves // 16] == leaf, one, zero).reshape(leaves, LANES)
-            b_ref[:, LANES * c : LANES * (c + 1)] = marks
-
-    def mark_codes(g, first, size, shift, weigh):
-        for c in range(chunk // LANES):
-            op = columns(operator_ref, g, c)
-            code = spread((op >> shift) * sources + columns(source_ref, g, c) - first, jnp.int16)
-            marks = jnp.where(iota[: size // 16] == code, spread(weigh(op), bf16), zero).reshape(size, LANES)
-            a_ref[:size, LANES * c : LANES * (c + 1)] = marks
-
-    def products(size):
-        return lax.dot_general(b_ref[...], a_ref[:size, :], NT, preferred_element_type=f32)
+    def mark_leaves(g, c, ref):
+        leaf = spread(columns(target_ref, g, c), jnp.int16)
+        marks = jnp.where(iota[: leaves // 16] == leaf, one, zero).reshape(leaves, LANES)
+        ref[:, LANES * c : LANES * (c + 1)] = marks
+
+    def mark_codes(g, c, ref, first, shift, weigh):
+        size = ref.shape[0]
+        op = columns(operator_ref, g, c)
+        code = spread((op >> shift) * sources + columns(source_ref, g, c) - first, jnp.int16)
+        marks = jnp.where(iota[: size // 16] == code, spread(weigh(op), bf16), zero).reshape(size, LANES)
+        ref[:, LANES * c : LANES * (c + 1)] = marks
+
+    def products(leaf_ref, code_ref):
+        return lax.dot_general(leaf_ref[...], code_ref[...], NT, preferred_element_type=f32)
 
     def digit_weight(op):
         last = op & 3
         return jnp.where(last == 0, 1.0, jnp.where(last == 1, 64.0, jnp.where(last == 2, 4096.0, 2.0**18)))
 
-    def count(g):
-        mark_leaves(g)
+    def marks(g, side):
+        for c in range(chunk // LANES):
+            mark_leaves(g, c, b_ref.at[side])
+            for first in range(0, codes, block):
+                mark_codes(g, c, a_ref.at[side, first : first + block], first, 2, digit_weight)
+            yield
+
+    def count(side):
         for first in range(0, codes, block):
-            size = min(block, codes - first)
-            mark_codes(g, first, size, 2, digit_weight)
-            acc_ref[:, first : first + size] += products(size)
+            acc_ref[:, first : first + block] += products(b_ref.at[side], a_ref.at[side, first : first + block])
 
     acc_ref[...] = jnp.zeros_like(acc_ref)
     for k, ref in enumerate((first_ref, own_ref, second_ref)):
@@ -153,7 +156,8 @@
         packed_ref[:PTS, leaves * k : leaves * (k + 1)] = (x << 11) | ((y >> 10) & 2047)
         packed_ref[PTS:, leaves * k : leaves * (k + 1)] = (z << 11) | (y & 1023)
 
-    def gather(place):
+    def gather(g, n):
+        place = jnp.broadcast_to(place_ref[g, n : n + 1, :], (8, LANES))
         idx = place & (LANES - 1)
         group = place >> 7
         words = [jnp.zeros((8, LANES), jnp.int32) for _ in range(2 * PTS // 8)]
@@ -168,31 +172,46 @@
             for r in range(PTS // 8):
                 got = lane_gather(window[3 * PTS + 8 * r : 3 * PTS + 8 * r + 8, at], idx)
                 charge[r] = jnp.where(here, got, charge[r])
-        return words, charge
-
-    def step(g, carry):
-        count(g)
+            yield
+        for r in range(PTS // 8):
+            first, second = words[r], words[PTS // 8 + r]
+            x = (first >> 11).astype(f32)
+            y = (((first << 21) >> 11) | (second & 1023)).astype(f32)
+            z = (second >> 11).astype(f32)
+            for k, row in enumerate((x, y, z, charge[r], x * x + y * y + z * z)):
+                picked_ref[n, PTS * k + 8 * r : PTS * k + 8 * r + 8, :] = row
+
+    def quarter(g, side):
+        later = lax.rem(g + 1, groups)
+        count(side)
+        marking = marks(later, 1 - side)
         at = pl.ds(pl.multiple_of(g * LANES, LANES), LANES)
         tx, ty, tz = (own_ref[PTS * c : PTS * (c + 1), at] * SCALE for c in range(3))
         square = tx * tx + ty * ty + (tz * tz + SOFT2 * SCALE * SCALE)
         tx, ty, tz = -2.0 * tx, -2.0 * ty, -2.0 * tz
-        acc = jnp.zeros((PTS, LANES), f32)
+        sums = [jnp.zeros((PTS, LANES), f32) for _ in range(2)]
         for n in range(near):
-            words, charge = gather(jnp.broadcast_to(place_ref[g, n : n + 1, :], (8, LANES)))
-            for r in range(PTS // 8):
-                first, second = words[r], words[PTS // 8 + r]
-                x = (first >> 11).astype(f32)
-                y = (((first << 21) >> 11) | (second & 1023)).astype(f32)
-                z = (second >> 11).astype(f32)
-                for k, row in enumerate((x, y, z, charge[r], x * x + y * y + z * z)):
-                    picked_ref[n, PTS * k + 8 * r : PTS * k + 8 * r + 8, :] = row
+            coming = gather(g, n + 1) if n + 1 < near else gather(later, 0)
             for p in range(PTS):
                 sx, sy, sz, q, far = (picked_ref[n, PTS * c + p : PTS * c + p + 1, :] for c in range(5))
-                acc += q * lax.rsqrt((square + far) + tx * sx + (ty * sy + tz * sz))
-        pot_ref[g] = acc * SCALE
+                sums[p % 2] += q * lax.rsqrt((square + far) + tx * sx + (ty * sy + tz * sz))
+                next(coming, None)
+            next(marking, None)
+        for _ in marking:
+            pass
+        pot_ref[g] = (sums[0] + sums[1]) * SCALE
+
+    for _ in gather(0, 0):
+        pass
+    for _ in marks(0, 0):
+        pass
+
+    def step(i, carry):
+        quarter(2 * i, 0)
+        quarter(2 * i + 1, 1)
         return carry
 
-    lax.fori_loop(0, groups, step, 0)
+    lax.fori_loop(0, groups // 2, step, 0)
     half = LANES // 2
     pieces = []
     for g in range(groups):
@@ -217,14 +236,15 @@
     @pl.when(carried)
     def _():
         pairs = ops // 2 * sources
-        for first in range(0, pairs, block):
-            size = min(block, pairs - first)
-            pair_ref[:, :size] = jnp.full((leaves, size), -(2.0**24), f32)
+        size = pair_ref.shape[1]
+        for first in range(0, pairs, size):
+            pair_ref[...] = jnp.full(pair_ref.shape, -(2.0**24), f32)
 
             def more(g, carry):
-                mark_leaves(g)
-                mark_codes(g, first, size, 1, lambda op: jnp.where((op & 1) == 1, 8192.0, 1.0))
-                pair_ref[:, :size] += products(size)
+                for c in range(chunk // LANES):
+                    mark_leaves(g, c, b_ref.at[0])
+                    mark_codes(g, c, a_ref.at[0, :size], first, 1, lambda op: jnp.where((op & 1) == 1, 8192.0, 1.0))
+                pair_ref[...] += products(b_ref.at[0], a_ref.at[0, :size])
                 return carry
 
             lax.fori_loop(0, groups, more, 0)
@@ -323,7 +343,7 @@
     second = exchange(1)
 
     codes = ops // 4 * sources
-    block = min(2 * codes, 512)
+    block = min(codes, 512)
     groups = leaves // LANES
     chunk = entries // groups
     places, parts = pl.pallas_call(
@@ -355,10 +375,10 @@
             pltpu.VMEM((groups, PTS, LANES), f32),
             pltpu.VMEM((leaves, codes), f32),
             pltpu.VMEM((leaves, block), f32),
-            pltpu.VMEM((block, chunk), bf16),
-            pltpu.VMEM((leaves, chunk), bf16),
+            pltpu.VMEM((2, codes, chunk), bf16),
+            pltpu.VMEM((2, leaves, chunk), bf16),
         ],
-        compiler_params=PARAMS,
+        compiler_params=pltpu.CompilerParams(vmem_limit_bytes=(46 + sources // 64) * 1024 * 1024),
     )(second, table, first, places, m2l_source, m2l_target, m2l_operator)
 
     local_exp = pl.pallas_call(

time: 20.3 us -> 20.4 us (level)
  no operation moved by 1% of the time
where the time goes in v5:
time: 20.4 us; the launch traced here: 20.1 us
  Pallas kernels  9.77 us (48%)
  starting transfers between devices  9.69 us (48%)
  between operations  0.67 us (3%)
    pallas_call x1, Pallas kernels, shards(): pl.pallas_call(functools.partial(near_kernel, ops=ops, sources=sources),...  6.06 us
    all_to_all x1, starting transfers between devices, shards(): lax.all_to_all(outgoing.reshape(peers, sources // peers, ncoef), 'grp', s...  5.14 us
    ppermute x2, starting transfers between devices, exchange(): return lax.ppermute(table, 'slab', ties + [(b, a) for a, b in ties])  4.55 us
    pallas_call x1, Pallas kernels, shards(): pl.pallas_call(functools.partial(prep_kernel, others=len(others)), name='...  2.07 us
    pallas_call x1, Pallas kernels, shards(): pl.pallas_call(functools.partial(far_kernel, ops=ops), name='far', out_sh...  1.48 us
  transfers between devices with their start and end apart: 3, of which 0 were waited for; matrix products, arithmetic and copies ran while one was open for 0% of the time, Pallas kernels for 31%

profile of v5, /device:TPU:11, one launch (start us, length us, event | category | flops | bytes accessed | tf_op | source)
XLA Modules:
  0.0 20.1 jit_solution(9322875734981393048)
XLA Ops:
  0.6 2.1 %prep.1 = (f32[64,512]{1,0:T(8,128)S(1)}, f32[128,121]{1,0:T(8,128)}, s32[8,512]{1,0:T(8,128)S(1)}, s32[1,4096]{1,0:T(1,128)S(1)}, s32[1,4096]{1,0:T(1,128)S(1)}...) custom-call(f32[64,3,128]{2,1,0:T(4,128)} %bitcast.13, f32[64,128]{1,0:T(8,128)} %bitcast.14, f32[121,512]{1,0:T(8,128)} %multipoles_hbm.1, ...), custom_call_target="tpu_custom_call" | custom-call | tf_op jit(solution)/shard_map/prep/pallas_call | solution.py:314
  2.7 0.2 %collective-permute-start.1 = (f32[64,512]{1,0:T(8,128)S(1)}, f32[64,512]{1,0:T(8,128)S(1)}, u32[]{:S(2)}, u32[]{:S(2)}) collective-permute-start(f32[64,512]{1,0:T(8,128)S(1)} %get-tuple-element.15.own_ref), channel_id=1, source_target_pairs={{0,8},{16,24},{8,0},{24,16},{1,9},{17,25},{9,1},{25,17},{2,10},{18... | collective-permute-start | bytes 393224 | tf_op jit(solution)/shard_map/ppermute | solution.py:340
  2.9 4.3 %collective-permute-start = (f32[64,512]{1,0:T(8,128)S(1)}, f32[64,512]{1,0:T(8,128)S(1)}, u32[]{:S(2)}, u32[]{:S(2)}) collective-permute-start(f32[64,512]{1,0:T(8,128)S(1)} %get-tuple-element.15.own_ref), channel_id=1, source_target_pairs={{8,16},{16,8},{9,17},{17,9},{10,18},{18,10},{11,19},{19,11},{12,20... | collective-permute-start | bytes 393224 | tf_op jit(solution)/shard_map/ppermute | solution.py:340
  7.3 5.1 %all-to-all-start = ((f32[8,16,121]{2,1,0:T(8,128)}), f32[8,16,121]{2,1,0:T(8,128)S(1)}, u32[]{:S(2)}, u32[]{:S(2)}) async-start(f32[8,16,121]{2,1,0:T(8,128)} %bitcast.6), calls=%async_computation | async-start | bytes 131072 | tf_op jit(solution)/shard_map/all_to_all | solution.py:333
  12.4 0.2 cut.1
  12.6 0.0 collective-permute-done.1.first_ref
  12.6 0.0 collective-permute-done.second_ref
  12.6 6.1 %near_counts.1 = (f32[64,128]{1,0:T(8,128)}, bf16[512,1024]{1,0:T(8,128)(2,1)S(1)}, bf16[512,1024]{1,0:T(8,128)(2,1)S(1)}, f32[8,128]{1,0:T(8,128)S(1)}) custom-call(f32[64,512]{1,0:T(8,128)S(1)} %collective-permute-done.second_ref, f32[64,512]{1,0:T(8,128)S(1)} %get-tuple-element.15.own_ref, f32[64,512]{1,0:T(8,128)S(1)} %collective-permute-done.1.first_ref, ...), custom_call_target="tpu_custom_call" | custom-call | tf_op jit(solution)/shard_map/near_counts/pallas_call | solution.py:361
  18.7 0.0 all-to-all-done
  18.7 1.5 %far.1 = f32[121,512]{1,0:T(8,128)} custom-call(f32[8,128]{1,0:T(8,128)S(1)} %get-tuple-element.22.inexact_ref, bf16[1024,256]{1,0:T(8,128)(2,1)S(1)} %get-tuple-element.23.parts_ref, f32[128,121]{1,0:T(8,128)S(1)} %bitcast.11, bf16[512,1024]{1,0:T(8,128)(2,1)S(1)} %get-tuple-element.25.low_ref, bf16[512,1024]{1,0:T(8,128)(2,1)S(1)} %get-tuple-element.26.rest_ref), custom_call_target="tpu_custom_call" | custom-call | tf_op jit(solution)/shard_map/far/pallas_call | solution.py:384
Async XLA Ops:
  2.7 9.9 %collective-permute-start.1 = (f32[64,512]{1,0:T(8,128)S(1)}, f32[64,512]{1,0:T(8,128)S(1)}, u32[]{:S(2)}, u32[]{:S(2)}) collective-permute-start(f32[64,512]{1,0:T(8,128)S(1)} %get-tuple-element.15.own_ref), channel_id=1, source_target_pairs={{0,8},{16,24},{8,0},{24,16},{1,9},{17,25},{9,1},{25,17},{2,10},{18... | collective-permute-start | bytes 393224 | tf_op jit(solution)/shard_map/ppermute | solution.py:340
  2.9 9.6 %collective-permute-start = (f32[64,512]{1,0:T(8,128)S(1)}, f32[64,512]{1,0:T(8,128)S(1)}, u32[]{:S(2)}, u32[]{:S(2)}) collective-permute-start(f32[64,512]{1,0:T(8,128)S(1)} %get-tuple-element.15.own_ref), channel_id=1, source_target_pairs={{8,16},{16,8},{9,17},{17,9},{10,18},{18,10},{11,19},{19,11},{12,20... | collective-permute-start | bytes 393224 | tf_op jit(solution)/shard_map/ppermute | solution.py:340
  7.3 11.4 %all-to-all-start = ((f32[8,16,121]{2,1,0:T(8,128)}), f32[8,16,121]{2,1,0:T(8,128)S(1)}, u32[]{:S(2)}, u32[]{:S(2)}) async-start(f32[8,16,121]{2,1,0:T(8,128)} %bitcast.6), calls=%async_computation | async-start | bytes 131072 | tf_op jit(solution)/shard_map/all_to_all | solution.py:333

commit v6 on v5

--- a/solution.py
+++ b/solution.py
@@ -84,7 +84,7 @@
             row = jnp.where(part == s, lane_gather(list_ref[:, LANES * s : LANES * (s + 1)], idx), row)
         side = row >> 9
         side = jnp.where(even, 2 - side, side)
-        place_ref[g] = (side << 9) + ((row & 7) << 6) + ((row >> 3) & 63)
+        place_ref[near * g : near * (g + 1), :] = (side << 9) + ((row & 7) << 6) + ((row >> 3) & 63)
     wide_ref[...] = pad_lanes(operators_ref[...])
     for op in range(ops):
         matrix = wide_ref[pl.ds(op, ncoef, stride=ops), :]
@@ -100,11 +100,12 @@
 def near_kernel(
     second_ref, own_ref, first_ref, place_ref, source_ref, target_ref, operator_ref,
     near_ref, low_ref, rest_ref, inexact_ref,
-    packed_ref, picked_ref, pot_ref, acc_ref, pair_ref, a_ref, b_ref, *, ops, sources,
+    packed_ref, picked_ref, target_points_ref, pot_ref, acc_ref, pair_ref, a_ref, b_ref, *, ops, sources,
 ):
-    groups, near, _ = place_ref.shape
     leaves = own_ref.shape[1]
-    _, codes, chunk = a_ref.shape
+    groups = leaves // LANES
+    near = place_ref.shape[0] // groups
+    codes, chunk = a_ref.shape
     block = pair_ref.shape[1]
     f32, bf16 = jnp.float32, jnp.bfloat16
     iota = lax.broadcasted_iota(jnp.int32, (max(block, leaves), LANES), 0).astype(jnp.int16).reshape(-1, 16, LANES)
@@ -115,7 +116,7 @@
         return jnp.broadcast_to(row, (16, LANES)).astype(dtype)[None]
 
     def columns(ref, g, c):
-        return ref[:, pl.ds(pl.multiple_of(g * chunk + c * LANES, LANES), LANES)]
+        return ref[:, pl.ds(pl.multiple_of((g * (chunk // LANES) + c) * LANES, LANES), LANES)]
 
     def mark_leaves(g, c, ref):
         leaf = spread(columns(target_ref, g, c), jnp.int16)
@@ -136,16 +137,9 @@
         last = op & 3
         return jnp.where(last == 0, 1.0, jnp.where(last == 1, 64.0, jnp.where(last == 2, 4096.0, 2.0**18)))
 
-    def marks(g, side):
-        for c in range(chunk // LANES):
-            mark_leaves(g, c, b_ref.at[side])
-            for first in range(0, codes, block):
-                mark_codes(g, c, a_ref.at[side, first : first + block], first, 2, digit_weight)
-            yield
-
-    def count(side):
+    def count():
         for first in range(0, codes, block):
-            acc_ref[:, first : first + block] += products(b_ref.at[side], a_ref.at[side, first : first + block])
+            acc_ref[:, first : first + block] += products(b_ref, a_ref.at[first : first + block])
 
     acc_ref[...] = jnp.zeros_like(acc_ref)
     for k, ref in enumerate((first_ref, own_ref, second_ref)):
@@ -156,8 +150,17 @@
         packed_ref[:PTS, leaves * k : leaves * (k + 1)] = (x << 11) | ((y >> 10) & 2047)
         packed_ref[PTS:, leaves * k : leaves * (k + 1)] = (z << 11) | (y & 1023)
 
-    def gather(g, n):
-        place = jnp.broadcast_to(place_ref[g, n : n + 1, :], (8, LANES))
+    for g in range(groups):
+        at = slice(LANES * g, LANES * (g + 1))
+        tx, ty, tz = (own_ref[PTS * c : PTS * (c + 1), at] * SCALE for c in range(3))
+        square = tx * tx + ty * ty + (tz * tz + SOFT2 * SCALE * SCALE)
+        for k, rows in enumerate((-2.0 * tx, -2.0 * ty, -2.0 * tz, square)):
+            target_points_ref[g, PTS * k : PTS * (k + 1), :] = rows
+    pot_ref[...] = jnp.zeros_like(pot_ref)
+    steps = groups * near
+
+    def gather(step, side):
+        place = jnp.broadcast_to(place_ref[pl.ds(step, 1), :], (8, LANES))
         idx = place & (LANES - 1)
         group = place >> 7
         words = [jnp.zeros((8, LANES), jnp.int32) for _ in range(2 * PTS // 8)]
@@ -179,43 +182,42 @@
             y = (((first << 21) >> 11) | (second & 1023)).astype(f32)
             z = (second >> 11).astype(f32)
             for k, row in enumerate((x, y, z, charge[r], x * x + y * y + z * z)):
-                picked_ref[n, PTS * k + 8 * r : PTS * k + 8 * r + 8, :] = row
-
-    def quarter(g, side):
-        later = lax.rem(g + 1, groups)
-        count(side)
-        marking = marks(later, 1 - side)
-        at = pl.ds(pl.multiple_of(g * LANES, LANES), LANES)
-        tx, ty, tz = (own_ref[PTS * c : PTS * (c + 1), at] * SCALE for c in range(3))
-        square = tx * tx + ty * ty + (tz * tz + SOFT2 * SCALE * SCALE)
-        tx, ty, tz = -2.0 * tx, -2.0 * ty, -2.0 * tz
+                picked_ref[side, PTS * k + 8 * r : PTS * k + 8 * r + 8, :] = row
+
+    def pairs(step, side):
+        g = lax.div(step, near)
+        tx, ty, tz, square = (target_points_ref[g, PTS * k : PTS * (k + 1), :] for k in range(4))
+        coming = gather(lax.rem(step + 1, steps), 1 - side)
         sums = [jnp.zeros((PTS, LANES), f32) for _ in range(2)]
-        for n in range(near):
-            coming = gather(g, n + 1) if n + 1 < near else gather(later, 0)
-            for p in range(PTS):
-                sx, sy, sz, q, far = (picked_ref[n, PTS * c + p : PTS * c + p + 1, :] for c in range(5))
-                sums[p % 2] += q * lax.rsqrt((square + far) + tx * sx + (ty * sy + tz * sz))
-                next(coming, None)
-            next(marking, None)
-        for _ in marking:
-            pass
-        pot_ref[g] = (sums[0] + sums[1]) * SCALE
-
+        for p in range(PTS):
+            sx, sy, sz, q, far = (picked_ref[side, PTS * c + p : PTS * c + p + 1, :] for c in range(5))
+            sums[p % 2] += q * lax.rsqrt((square + far) + tx * sx + (ty * sy + tz * sz))
+            next(coming, None)
+        pot_ref[g] += sums[0] + sums[1]
+
+    def mark(part):
+        for c in range(chunk // LANES):
+            mark_leaves(part, c, b_ref)
+            for first in range(0, codes, block):
+                mark_codes(part, c, a_ref.at[first : first + block], first, 2, digit_weight)
+
+    passes = steps // 2
     for _ in gather(0, 0):
         pass
-    for _ in marks(0, 0):
-        pass
+    mark(0)
 
     def step(i, carry):
-        quarter(2 * i, 0)
-        quarter(2 * i + 1, 1)
+        count()
+        pairs(2 * i, 0)
+        pairs(2 * i + 1, 1)
+        mark(lax.rem(i + 1, passes))
         return carry
 
-    lax.fori_loop(0, groups // 2, step, 0)
+    lax.fori_loop(0, passes, step, 0)
     half = LANES // 2
     pieces = []
     for g in range(groups):
-        pot = pot_ref[g]
+        pot = pot_ref[g] * SCALE
         pieces += [pot[:, :half], pot[:, half:]]
     near_ref[...] = jnp.concatenate(pieces, axis=0).T
 
@@ -240,14 +242,14 @@
         for first in range(0, pairs, size):
             pair_ref[...] = jnp.full(pair_ref.shape, -(2.0**24), f32)
 
-            def more(g, carry):
+            def more(part, carry):
                 for c in range(chunk // LANES):
-                    mark_leaves(g, c, b_ref.at[0])
-                    mark_codes(g, c, a_ref.at[0, :size], first, 1, lambda op: jnp.where((op & 1) == 1, 8192.0, 1.0))
-                pair_ref[...] += products(b_ref.at[0], a_ref.at[0, :size])
+                    mark_leaves(part, c, b_ref)
+                    mark_codes(part, c, a_ref.at[:size], first, 1, lambda op: jnp.where((op & 1) == 1, 8192.0, 1.0))
+                pair_ref[...] += products(b_ref, a_ref.at[:size])
                 return carry
 
-            lax.fori_loop(0, groups, more, 0)
+            lax.fori_loop(0, passes, more, 0)
             for lane in range(first, first + size, LANES):
                 value = pair_ref[:, lane - first : lane - first + LANES]
                 odd = jnp.floor(value * (1.0 / 8192.0))
@@ -345,12 +347,12 @@
     codes = ops // 4 * sources
     block = min(codes, 512)
     groups = leaves // LANES
-    chunk = entries // groups
+    chunk = entries // (groups * near // 2)
     places, parts = pl.pallas_call(
         functools.partial(cut_kernel, ops=ops),
         name="cut",
         out_shape=(
-            jax.ShapeDtypeStruct((groups, near, LANES), jnp.int32),
+            jax.ShapeDtypeStruct((groups * near, LANES), jnp.int32),
             jax.ShapeDtypeStruct((ops * LANES, 2 * LANES), bf16),
         ),
         in_specs=[VMEM] * 2,
@@ -371,12 +373,13 @@
         out_specs=(VMEM,) * 4,
         scratch_shapes=[
             pltpu.VMEM((2 * PTS, 3 * leaves), jnp.int32),
-            pltpu.VMEM((near, 5 * PTS, LANES), f32),
+            pltpu.VMEM((2, 5 * PTS, LANES), f32),
+            pltpu.VMEM((groups, 4 * PTS, LANES), f32),
             pltpu.VMEM((groups, PTS, LANES), f32),
             pltpu.VMEM((leaves, codes), f32),
             pltpu.VMEM((leaves, block), f32),
-            pltpu.VMEM((2, codes, chunk), bf16),
-            pltpu.VMEM((2, leaves, chunk), bf16),
+            pltpu.VMEM((codes, chunk), bf16),
+            pltpu.VMEM((leaves, chunk), bf16),
         ],
         compiler_params=pltpu.CompilerParams(vmem_limit_bytes=(46 + sources // 64) * 1024 * 1024),
     )(second, table, first, places, m2l_source, m2l_target, m2l_operator)

time: 20.4 us -> 21.1 us (1.034)
  Pallas kernels: 9.77 us -> 10.4 us
    pallas_call x1, Pallas kernels: 6.06 us -> 6.71 us  [shards(): pl.pallas_call(functools.partial(near_kernel, ops=ops, sources=sources),...]
  transfers between devices with their start and end apart: 3 -> 3, of which waited for: 0 -> 0; matrix products, arithmetic and copies ran while one was open for 0% -> 0% of each run, Pallas kernels for 31% -> 33%
where the time goes in v6:
time: 21.1 us; the launch traced here: 20.8 us
  Pallas kernels  10.4 us (49%)
  starting transfers between devices  9.69 us (46%)
  between operations  0.67 us (3%)
    pallas_call x1, Pallas kernels, shards(): pl.pallas_call(functools.partial(near_kernel, ops=ops, sources=sources),...  6.71 us
    all_to_all x1, starting transfers between devices, shards(): lax.all_to_all(outgoing.reshape(peers, sources // peers, ncoef), 'grp', s...  5.14 us
    ppermute x2, starting transfers between devices, exchange(): return lax.ppermute(table, 'slab', ties + [(b, a) for a, b in ties])  4.55 us
    pallas_call x1, Pallas kernels, shards(): pl.pallas_call(functools.partial(prep_kernel, others=len(others)), name='...  2.07 us
    pallas_call x1, Pallas kernels, shards(): pl.pallas_call(functools.partial(far_kernel, ops=ops), name='far', out_sh...  1.48 us
  transfers between devices with their start and end apart: 3, of which 0 were waited for; matrix products, arithmetic and copies ran while one was open for 0% of the time, Pallas kernels for 33%

profile of v6, /device:TPU:11, one launch (start us, length us, event | category | flops | bytes accessed | tf_op | source)
XLA Modules:
  0.0 20.8 jit_solution(3389958962277645536)
XLA Ops:
  0.6 2.1 %prep.1 = (f32[64,512]{1,0:T(8,128)S(1)}, f32[128,121]{1,0:T(8,128)}, s32[8,512]{1,0:T(8,128)S(1)}, s32[1,4096]{1,0:T(1,128)S(1)}, s32[1,4096]{1,0:T(1,128)S(1)}...) custom-call(f32[64,3,128]{2,1,0:T(4,128)} %bitcast.13, f32[64,128]{1,0:T(8,128)} %bitcast.14, f32[121,512]{1,0:T(8,128)} %multipoles_hbm.1, ...), custom_call_target="tpu_custom_call" | custom-call | tf_op jit(solution)/shard_map/prep/pallas_call | solution.py:316
  2.7 0.2 %collective-permute-start.1 = (f32[64,512]{1,0:T(8,128)S(1)}, f32[64,512]{1,0:T(8,128)S(1)}, u32[]{:S(2)}, u32[]{:S(2)}) collective-permute-start(f32[64,512]{1,0:T(8,128)S(1)} %get-tuple-element.15.own_ref), channel_id=1, source_target_pairs={{0,8},{16,24},{8,0},{24,16},{1,9},{17,25},{9,1},{25,17},{2,10},{18... | collective-permute-start | bytes 393224 | tf_op jit(solution)/shard_map/ppermute | solution.py:342
  2.9 4.3 %collective-permute-start = (f32[64,512]{1,0:T(8,128)S(1)}, f32[64,512]{1,0:T(8,128)S(1)}, u32[]{:S(2)}, u32[]{:S(2)}) collective-permute-start(f32[64,512]{1,0:T(8,128)S(1)} %get-tuple-element.15.own_ref), channel_id=1, source_target_pairs={{8,16},{16,8},{9,17},{17,9},{10,18},{18,10},{11,19},{19,11},{12,20... | collective-permute-start | bytes 393224 | tf_op jit(solution)/shard_map/ppermute | solution.py:342
  7.3 5.1 %all-to-all-start = ((f32[8,16,121]{2,1,0:T(8,128)}), f32[8,16,121]{2,1,0:T(8,128)S(1)}, u32[]{:S(2)}, u32[]{:S(2)}) async-start(f32[8,16,121]{2,1,0:T(8,128)} %bitcast.6), calls=%async_computation | async-start | bytes 131072 | tf_op jit(solution)/shard_map/all_to_all | solution.py:335
  12.4 0.2 cut.1
  12.6 0.0 collective-permute-done.1.first_ref
  12.6 0.0 collective-permute-done.second_ref
  12.6 6.7 %near_counts.1 = (f32[64,128]{1,0:T(8,128)}, bf16[512,1024]{1,0:T(8,128)(2,1)S(1)}, bf16[512,1024]{1,0:T(8,128)(2,1)S(1)}, f32[8,128]{1,0:T(8,128)S(1)}) custom-call(f32[64,512]{1,0:T(8,128)S(1)} %collective-permute-done.second_ref, f32[64,512]{1,0:T(8,128)S(1)} %get-tuple-element.15.own_ref, f32[64,512]{1,0:T(8,128)S(1)} %collective-permute-done.1.first_ref, ...), custom_call_target="tpu_custom_call" | custom-call | tf_op jit(solution)/shard_map/near_counts/pallas_call | solution.py:363
  19.3 0.0 all-to-all-done
  19.3 1.5 %far.1 = f32[121,512]{1,0:T(8,128)} custom-call(f32[8,128]{1,0:T(8,128)S(1)} %get-tuple-element.22.inexact_ref, bf16[1024,256]{1,0:T(8,128)(2,1)S(1)} %get-tuple-element.23.parts_ref, f32[128,121]{1,0:T(8,128)S(1)} %bitcast.11, bf16[512,1024]{1,0:T(8,128)(2,1)S(1)} %get-tuple-element.25.low_ref, bf16[512,1024]{1,0:T(8,128)(2,1)S(1)} %get-tuple-element.26.rest_ref), custom_call_target="tpu_custom_call" | custom-call | tf_op jit(solution)/shard_map/far/pallas_call | solution.py:387
Async XLA Ops:
  2.7 9.9 %collective-permute-start.1 = (f32[64,512]{1,0:T(8,128)S(1)}, f32[64,512]{1,0:T(8,128)S(1)}, u32[]{:S(2)}, u32[]{:S(2)}) collective-permute-start(f32[64,512]{1,0:T(8,128)S(1)} %get-tuple-element.15.own_ref), channel_id=1, source_target_pairs={{0,8},{16,24},{8,0},{24,16},{1,9},{17,25},{9,1},{25,17},{2,10},{18... | collective-permute-start | bytes 393224 | tf_op jit(solution)/shard_map/ppermute | solution.py:342
  2.9 9.6 %collective-permute-start = (f32[64,512]{1,0:T(8,128)S(1)}, f32[64,512]{1,0:T(8,128)S(1)}, u32[]{:S(2)}, u32[]{:S(2)}) collective-permute-start(f32[64,512]{1,0:T(8,128)S(1)} %get-tuple-element.15.own_ref), channel_id=1, source_target_pairs={{8,16},{16,8},{9,17},{17,9},{10,18},{18,10},{11,19},{19,11},{12,20... | collective-permute-start | bytes 393224 | tf_op jit(solution)/shard_map/ppermute | solution.py:342
  7.3 12.0 %all-to-all-start = ((f32[8,16,121]{2,1,0:T(8,128)}), f32[8,16,121]{2,1,0:T(8,128)S(1)}, u32[]{:S(2)}, u32[]{:S(2)}) async-start(f32[8,16,121]{2,1,0:T(8,128)} %bitcast.6), calls=%async_computation | async-start | bytes 131072 | tf_op jit(solution)/shard_map/all_to_all | solution.py:335

commit v7 on v4

--- a/solution.py
+++ b/solution.py
@@ -98,9 +98,9 @@
 
 
 def near_kernel(
-    second_ref, own_ref, first_ref, place_ref, source_ref, target_ref, operator_ref,
+    third_ref, own_ref, second_ref, first_ref, place_ref, source_ref, target_ref, operator_ref,
     near_ref, low_ref, rest_ref, inexact_ref,
-    packed_ref, picked_ref, pot_ref, acc_ref, pair_ref, a_ref, b_ref, *, ops, sources,
+    words_ref, charge_ref, spread_ref, pot_ref, acc_ref, pair_ref, a_ref, b_ref, *, ops, sources,
 ):
     groups, near, _ = place_ref.shape
     leaves = own_ref.shape[1]
@@ -145,51 +145,68 @@
             acc_ref[:, first : first + size] += products(size)
 
     acc_ref[...] = jnp.zeros_like(acc_ref)
-    for k, ref in enumerate((first_ref, own_ref, second_ref)):
-        x, y, z = (
-            jnp.clip(jnp.floor(ref[PTS * c : PTS * (c + 1), :] * SCALE + 0.5), -SCALE, SCALE - 1.0).astype(jnp.int32)
-            for c in range(3)
-        )
-        packed_ref[:PTS, leaves * k : leaves * (k + 1)] = (x << 11) | ((y >> 10) & 2047)
-        packed_ref[PTS:, leaves * k : leaves * (k + 1)] = (z << 11) | (y & 1023)
-
-    def gather(place):
+    early = lax.axis_index("slab") < 2
+    for k in range(3):
+        for c in range(groups):
+            at = slice(LANES * c, LANES * (c + 1))
+            if k == 0:
+                block4 = jnp.where(early, first_ref[:, at], third_ref[:, at])
+            else:
+                block4 = (own_ref, second_ref)[k - 1][:, at]
+            x, y, z = (
+                jnp.clip(
+                    jnp.floor(block4[PTS * i : PTS * (i + 1), :] * SCALE + 0.5), -SCALE, SCALE - 1.0
+                ).astype(jnp.int32)
+                for i in range(3)
+            )
+            for w, word in enumerate(((x << 11) | ((y >> 10) & 2047), (z << 11) | (y & 1023))):
+                for j in range(PTS):
+                    words_ref[w, j, groups * k + c] = jnp.broadcast_to(word[j : j + 1, :], (near, LANES))
+            for j in range(PTS):
+                charge_ref[j, groups * k + c] = jnp.broadcast_to(
+                    block4[3 * PTS + j : 3 * PTS + j + 1, :], (near, LANES)
+                )
+    for g in range(groups):
+        at = slice(LANES * g, LANES * (g + 1))
+        tx, ty, tz = (own_ref[PTS * c : PTS * (c + 1), at] * SCALE for c in range(3))
+        square = tx * tx + ty * ty + (tz * tz + SOFT2 * SCALE * SCALE)
+        for k, rows in enumerate((-2.0 * tx, -2.0 * ty, -2.0 * tz, square)):
+            for p in range(PTS):
+                spread_ref[g, p, k] = jnp.broadcast_to(rows[p : p + 1, :], (near, LANES))
+
+    def gather(place, j, found):
         idx = place & (LANES - 1)
         group = place >> 7
-        words = [jnp.zeros((8, LANES), jnp.int32) for _ in range(2 * PTS // 8)]
-        charge = [jnp.zeros((8, LANES), f32) for _ in range(PTS // 8)]
+        points = [[jnp.zeros((near, LANES), t) for t in (jnp.int32, jnp.int32, f32)] for _ in range(2)]
         for s in range(3 * groups):
             here = group == s
-            window = (first_ref, own_ref, second_ref)[s // groups]
-            at = slice(LANES * (s % groups), LANES * (s % groups + 1))
-            for r in range(2 * PTS // 8):
-                got = lane_gather(packed_ref[8 * r : 8 * r + 8, LANES * s : LANES * (s + 1)], idx)
-                words[r] = jnp.where(here, got, words[r])
-            for r in range(PTS // 8):
-                got = lane_gather(window[3 * PTS + 8 * r : 3 * PTS + 8 * r + 8, at], idx)
-                charge[r] = jnp.where(here, got, charge[r])
-        return words, charge
+            for i, point in enumerate(points):
+                for w, ref in enumerate((words_ref.at[0], words_ref.at[1], charge_ref)):
+                    point[w] = jnp.where(here, lane_gather(ref[j + i, s], idx), point[w])
+            yield
+        for first, second, charge in points:
+            x = (first >> 11).astype(f32)
+            y = (((first << 21) >> 11) | (second & 1023)).astype(f32)
+            z = (second >> 11).astype(f32)
+            found.append((x, y, z, x * x + y * y + z * z, charge))
 
     def step(g, carry):
         count(g)
-        at = pl.ds(pl.multiple_of(g * LANES, LANES), LANES)
-        tx, ty, tz = (own_ref[PTS * c : PTS * (c + 1), at] * SCALE for c in range(3))
-        square = tx * tx + ty * ty + (tz * tz + SOFT2 * SCALE * SCALE)
-        tx, ty, tz = -2.0 * tx, -2.0 * ty, -2.0 * tz
-        acc = jnp.zeros((PTS, LANES), f32)
-        for n in range(near):
-            words, charge = gather(jnp.broadcast_to(place_ref[g, n : n + 1, :], (8, LANES)))
-            for r in range(PTS // 8):
-                first, second = words[r], words[PTS // 8 + r]
-                x = (first >> 11).astype(f32)
-                y = (((first << 21) >> 11) | (second & 1023)).astype(f32)
-                z = (second >> 11).astype(f32)
-                for k, row in enumerate((x, y, z, charge[r], x * x + y * y + z * z)):
-                    picked_ref[n, PTS * k + 8 * r : PTS * k + 8 * r + 8, :] = row
+        place = place_ref[g]
+        sums = [jnp.zeros((near, LANES), f32) for _ in range(PTS)]
+        found = []
+        for _ in gather(place, 0, found):
+            pass
+        for j in range(0, PTS, 2):
+            now, found = found, []
+            coming = gather(place, j + 2, found) if j + 2 < PTS else iter(())
             for p in range(PTS):
-                sx, sy, sz, q, far = (picked_ref[n, PTS * c + p : PTS * c + p + 1, :] for c in range(5))
-                acc += q * lax.rsqrt((square + far) + tx * sx + (ty * sy + tz * sz))
-        pot_ref[g] = acc * SCALE
+                tx, ty, tz, square = (spread_ref[g, p, k] for k in range(4))
+                for x, y, z, far, charge in now:
+                    sums[p] += charge * lax.rsqrt((square + far) + tx * x + (ty * y + tz * z))
+                next(coming, None)
+        for p in range(PTS):
+            pot_ref[g, p : p + 1, :] = jnp.sum(sums[p], axis=0, keepdims=True) * SCALE
         return carry
 
     lax.fori_loop(0, groups, step, 0)
@@ -315,12 +332,12 @@
     ).reshape(sources, ncoef)
     slabs = lax.axis_size("slab")
 
-    def exchange(start):
-        ties = [(i, i + 1) for i in range(start, slabs - 1, 2)]
+    def exchange(ties):
         return lax.ppermute(table, "slab", ties + [(b, a) for a, b in ties])
 
-    first = exchange(0)
-    second = exchange(1)
+    first = exchange([(0, 1)])
+    second = exchange([(i, i + 1) for i in range(1, slabs - 1, 2)])
+    third = exchange([(i, i + 1) for i in range(2, slabs - 1, 2)])
 
     codes = ops // 4 * sources
     block = min(2 * codes, 512)
@@ -347,11 +364,12 @@
             jax.ShapeDtypeStruct((leaves, ops * sources), bf16),
             jax.ShapeDtypeStruct((8, LANES), f32),
         ),
-        in_specs=[VMEM] * 7,
+        in_specs=[VMEM] * 8,
         out_specs=(VMEM,) * 4,
         scratch_shapes=[
-            pltpu.VMEM((2 * PTS, 3 * leaves), jnp.int32),
-            pltpu.VMEM((near, 5 * PTS, LANES), f32),
+            pltpu.VMEM((2, PTS, 3 * groups, near, LANES), jnp.int32),
+            pltpu.VMEM((PTS, 3 * groups, near, LANES), f32),
+            pltpu.VMEM((groups, PTS, 4, near, LANES), f32),
             pltpu.VMEM((groups, PTS, LANES), f32),
             pltpu.VMEM((leaves, codes), f32),
             pltpu.VMEM((leaves, block), f32),
@@ -359,7 +377,7 @@
             pltpu.VMEM((leaves, chunk), bf16),
         ],
         compiler_params=PARAMS,
-    )(second, table, first, places, m2l_source, m2l_target, m2l_operator)
+    )(third, table, second, first, places, m2l_source, m2l_target, m2l_operator)
 
     local_exp = pl.pallas_call(
         functools.partial(far_kernel, ops=ops),

time: 20.3 us -> 22.4 us (1.10)
  the two profiles are of different devices: /device:TPU:11 before, /device:TPU:27 now
where the time goes in v7:
time: 22.4 us; the launch traced here: 22.1 us
  starting transfers between devices  11.7 us (52%)
  Pallas kernels  9.79 us (44%)
  between operations  0.69 us (3%)
    ppermute x3, starting transfers between devices, exchange(): return lax.ppermute(table, 'slab', ties + [(b, a) for a, b in ties])  6.23 us
    pallas_call x1, Pallas kernels, shards(): pl.pallas_call(functools.partial(near_kernel, ops=ops, sources=sources),...  6.08 us
    all_to_all x1, starting transfers between devices, shards(): lax.all_to_all(outgoing.reshape(peers, sources // peers, ncoef), 'grp', s...  5.42 us
    pallas_call x1, Pallas kernels, shards(): pl.pallas_call(functools.partial(prep_kernel, others=len(others)), name='...  2.07 us
    pallas_call x1, Pallas kernels, shards(): pl.pallas_call(functools.partial(far_kernel, ops=ops), name='far', out_sh...  1.48 us
  transfers between devices with their start and end apart: 4, of which 0 were waited for; matrix products, arithmetic and copies ran while one was open for 0% of the time, Pallas kernels for 28%

profile of v7, /device:TPU:27, one launch (start us, length us, event | category | flops | bytes accessed | tf_op | source)
XLA Modules:
  0.0 22.1 jit_solution(5361846447124052451)
XLA Ops:
  0.6 2.1 %prep.1 = (f32[64,512]{1,0:T(8,128)S(1)}, f32[128,121]{1,0:T(8,128)}, s32[8,512]{1,0:T(8,128)S(1)}, s32[1,4096]{1,0:T(1,128)S(1)}, s32[1,4096]{1,0:T(1,128)S(1)}...) custom-call(f32[64,3,128]{2,1,0:T(4,128)} %bitcast.13, f32[64,128]{1,0:T(8,128)} %bitcast.14, f32[121,512]{1,0:T(8,128)} %multipoles_hbm.1, ...), custom_call_target="tpu_custom_call" | custom-call | tf_op jit(solution)/shard_map/prep/pallas_call | solution.py:311
  2.7 0.7 %collective-permute-start.2 = (f32[64,512]{1,0:T(8,128)S(1)}, f32[64,512]{1,0:T(8,128)S(1)}, u32[]{:S(2)}, u32[]{:S(2)}) collective-permute-start(f32[64,512]{1,0:T(8,128)S(1)} %get-tuple-element.15.own_ref), channel_id=1, source_target_pairs={{0,8},{8,0},{1,9},{9,1},{2,10},{10,2},{3,11},{11,3},{4,12},{12,4},... | collective-permute-start | bytes 393224 | tf_op jit(solution)/shard_map/ppermute | solution.py:336
  3.4 0.7 %collective-permute-start.1 = (f32[64,512]{1,0:T(8,128)S(1)}, f32[64,512]{1,0:T(8,128)S(1)}, u32[]{:S(2)}, u32[]{:S(2)}) collective-permute-start(f32[64,512]{1,0:T(8,128)S(1)} %get-tuple-element.15.own_ref), channel_id=1, source_target_pairs={{8,16},{16,8},{9,17},{17,9},{10,18},{18,10},{11,19},{19,11},{12,20... | collective-permute-start | bytes 393224 | tf_op jit(solution)/shard_map/ppermute | solution.py:336
  4.1 4.9 %collective-permute-start = (f32[64,512]{1,0:T(8,128)S(1)}, f32[64,512]{1,0:T(8,128)S(1)}, u32[]{:S(2)}, u32[]{:S(2)}) collective-permute-start(f32[64,512]{1,0:T(8,128)S(1)} %get-tuple-element.15.own_ref), channel_id=1, source_target_pairs={{16,24},{24,16},{17,25},{25,17},{18,26},{26,18},{19,27},{27,19},{2... | collective-permute-start | bytes 393224 | tf_op jit(solution)/shard_map/ppermute | solution.py:336
  9.0 5.4 %all-to-all-start = ((f32[8,16,121]{2,1,0:T(8,128)}), f32[8,16,121]{2,1,0:T(8,128)S(1)}, u32[]{:S(2)}, u32[]{:S(2)}) async-start(f32[8,16,121]{2,1,0:T(8,128)} %bitcast.6), calls=%async_computation | async-start | bytes 131072 | tf_op jit(solution)/shard_map/all_to_all | solution.py:330
  14.4 0.2 cut.1
  14.6 0.0 collective-permute-done.2.first_ref
  14.6 0.0 collective-permute-done.1.second_ref
  14.6 0.0 collective-permute-done.third_ref
  14.6 6.1 %near_counts.1 = (f32[64,128]{1,0:T(8,128)}, bf16[512,1024]{1,0:T(8,128)(2,1)S(1)}, bf16[512,1024]{1,0:T(8,128)(2,1)S(1)}, f32[8,128]{1,0:T(8,128)S(1)}) custom-call(f32[64,512]{1,0:T(8,128)S(1)} %collective-permute-done.third_ref, f32[64,512]{1,0:T(8,128)S(1)} %get-tuple-element.15.own_ref, f32[64,512]{1,0:T(8,128)S(1)} %collective-permute-done.1.second_ref, ...), custom_call_target="tpu_custom_call" | custom-call | tf_op jit(solution)/shard_map/near_counts/pallas_call | solution.py:358
  20.7 0.0 all-to-all-done
  20.7 1.5 %far.1 = f32[121,512]{1,0:T(8,128)} custom-call(f32[8,128]{1,0:T(8,128)S(1)} %get-tuple-element.22.inexact_ref, bf16[1024,256]{1,0:T(8,128)(2,1)S(1)} %get-tuple-element.23.parts_ref, f32[128,121]{1,0:T(8,128)S(1)} %bitcast.11, bf16[512,1024]{1,0:T(8,128)(2,1)S(1)} %get-tuple-element.25.low_ref, bf16[512,1024]{1,0:T(8,128)(2,1)S(1)} %get-tuple-element.26.rest_ref), custom_call_target="tpu_custom_call" | custom-call | tf_op jit(solution)/shard_map/far/pallas_call | solution.py:382
Async XLA Ops:
  2.7 11.8 %collective-permute-start.2 = (f32[64,512]{1,0:T(8,128)S(1)}, f32[64,512]{1,0:T(8,128)S(1)}, u32[]{:S(2)}, u32[]{:S(2)}) collective-permute-start(f32[64,512]{1,0:T(8,128)S(1)} %get-tuple-element.15.own_ref), channel_id=1, source_target_pairs={{0,8},{8,0},{1,9},{9,1},{2,10},{10,2},{3,11},{11,3},{4,12},{12,4},... | collective-permute-start | bytes 393224 | tf_op jit(solution)/shard_map/ppermute | solution.py:336
  3.4 11.2 %collective-permute-start.1 = (f32[64,512]{1,0:T(8,128)S(1)}, f32[64,512]{1,0:T(8,128)S(1)}, u32[]{:S(2)}, u32[]{:S(2)}) collective-permute-start(f32[64,512]{1,0:T(8,128)S(1)} %get-tuple-element.15.own_ref), channel_id=1, source_target_pairs={{8,16},{16,8},{9,17},{17,9},{10,18},{18,10},{11,19},{19,11},{12,20... | collective-permute-start | bytes 393224 | tf_op jit(solution)/shard_map/ppermute | solution.py:336
  4.1 10.5 %collective-permute-start = (f32[64,512]{1,0:T(8,128)S(1)}, f32[64,512]{1,0:T(8,128)S(1)}, u32[]{:S(2)}, u32[]{:S(2)}) collective-permute-start(f32[64,512]{1,0:T(8,128)S(1)} %get-tuple-element.15.own_ref), channel_id=1, source_target_pairs={{16,24},{24,16},{17,25},{25,17},{18,26},{26,18},{19,27},{27,19},{2... | collective-permute-start | bytes 393224 | tf_op jit(solution)/shard_map/ppermute | solution.py:336
  9.0 11.7 %all-to-all-start = ((f32[8,16,121]{2,1,0:T(8,128)}), f32[8,16,121]{2,1,0:T(8,128)S(1)}, u32[]{:S(2)}, u32[]{:S(2)}) async-start(f32[8,16,121]{2,1,0:T(8,128)} %bitcast.6), calls=%async_computation | async-start | bytes 131072 | tf_op jit(solution)/shard_map/all_to_all | solution.py:330

commit v8 on v4

v8 whole, which is shorter than its diff:
```python
import functools

import jax
import jax.numpy as jnp
from jax import lax
from jax.experimental import pallas as pl
from jax.experimental.pallas import tpu as pltpu
from jax.sharding import PartitionSpec as P

SOFT2 = 0.0625
LANES = 128
PTS = 16
UNITS = 2.0**20
SCALE = 2.0**31
VMEM = pl.BlockSpec(memory_space=pltpu.VMEM)
ANY = pl.BlockSpec(memory_space=pl.ANY)
PARAMS = pltpu.CompilerParams(vmem_limit_bytes=48 * 1024 * 1024)
NT = (((1,), (1,)), ((), ()))


def lane_gather(x, idx):
    return jnp.take_along_axis(x, idx, axis=1, mode="promise_in_bounds")


def split(x):
    hi = x.astype(jnp.bfloat16)
    return hi, (x - hi.astype(jnp.float32)).astype(jnp.bfloat16)


def pad_lanes(x):
    return jnp.concatenate([x, jnp.zeros((x.shape[0], LANES - x.shape[1]), x.dtype)], axis=1)


def prep_kernel(coords_hbm, charges_hbm, multipoles_hbm, send_hbm, *refs, others):
    sources, refs = refs[:others], refs[others:]
    (table_ref, out_ref, *targets), refs = refs[: others + 2], refs[others + 2 :]
    coords_ref, charges_ref, multipoles_ref, send_ref, sems = refs
    pairs = (
        (coords_hbm, coords_ref),
        (charges_hbm, charges_ref),
        (send_hbm, send_ref),
        (multipoles_hbm, multipoles_ref),
        *zip(sources, targets),
    )
    copies = [pltpu.make_async_copy(src, dst, sems.at[i]) for i, (src, dst) in enumerate(pairs)]
    for copy in copies:
        copy.start()
    copies[0].wait()
    copies[1].wait()
    for c in range(4):
        rows = charges_ref[...] if c == 3 else coords_ref[:, c, :]
        cols = rows.T
        for pair in range(4):
            a = cols[32 * pair : 32 * pair + 16, :]
            b = cols[32 * pair + 16 : 32 * pair + 32, :]
            table_ref[16 * c : 16 * c + 16, LANES * pair : LANES * (pair + 1)] = jnp.concatenate([a, b], axis=1)
    copies[2].wait()
    copies[3].wait()
    ncoef, leaves = multipoles_ref.shape
    for sb in range(send_ref.shape[1] // LANES):
        send = send_ref[:, LANES * sb : LANES * (sb + 1)]
        lane = send & (LANES - 1)
        group = send >> 7
        idx = jnp.broadcast_to(lane, (ncoef, LANES))
        picked = jnp.zeros((ncoef, LANES), jnp.float32)
        for g in range(leaves // LANES):
            got = lane_gather(multipoles_ref[:, LANES * g : LANES * (g + 1)], idx)
            picked = jnp.where(group == g, got, picked)
        out_ref[LANES * sb : LANES * (sb + 1), :] = picked.T
    for copy in copies[4:]:
        copy.wait()


def cut_kernel(list_ref, operators_ref, place_ref, parts_ref, wide_ref, *, ops):
    near, leaves = list_ref.shape
    ncoef = operators_ref.shape[1]
    groups = leaves // LANES
    even = lax.axis_index("slab") % 2 == 0
    lane = lax.broadcasted_iota(jnp.int32, (near, LANES), 1)
    for g in range(groups):
        idx = 8 * (lane & 15) + 2 * g + (lane >> 6)
        part = (lane & 63) >> 4
        row = jnp.zeros((near, LANES), jnp.int32)
        for s in range(groups):
            row = jnp.where(part == s, lane_gather(list_ref[:, LANES * s : LANES * (s + 1)], idx), row)
        side = row >> 9
        side = jnp.where(even, 2 - side, side)
        place_ref[g] = (side << 9) + ((row & 7) << 6) + ((row >> 3) & 63)
    wide_ref[...] = pad_lanes(operators_ref[...])
    for op in range(ops):
        matrix = wide_ref[pl.ds(op, ncoef, stride=ops), :]
        matrix = jnp.concatenate([matrix, jnp.zeros((LANES - ncoef, LANES), jnp.float32)], axis=0)
        hi, lo = split(matrix)
        parts_ref[LANES * spot(op, ops) : LANES * (spot(op, ops) + 1), :] = jnp.concatenate([hi, lo], axis=1)


def spot(op, ops):
    return (op % 4) * (ops // 4) + op // 4


class Marks:
    def __init__(self, rows, chunk):
        self.iota = lax.broadcasted_iota(jnp.int32, (rows, LANES), 0).astype(jnp.int16).reshape(-1, 16, LANES)
        self.chunk = chunk

    def columns(self, ref, part, c):
        return ref[:, pl.ds(pl.multiple_of(part * self.chunk + c * LANES, LANES), LANES)]

    def put(self, ref, c, code, weight):
        size = ref.shape[0]
        code, weight = (
            jnp.broadcast_to(x, (16, LANES)).astype(t)[None] for x, t in ((code, jnp.int16), (weight, jnp.bfloat16))
        )
        marks = jnp.where(self.iota[: size // 16] == code, weight, jnp.zeros((1, 16, LANES), jnp.bfloat16))
        ref[:, LANES * c : LANES * (c + 1)] = marks.reshape(size, LANES)


def near_kernel(
    second_ref, own_ref, first_ref, place_ref, source_ref, target_ref, operator_ref,
    near_ref, low_ref, peak_ref,
    packed_ref, charge_ref, picked_ref, pot_ref, acc_ref, a_ref, b_ref, *, sources,
):
    groups, near, _ = place_ref.shape
    leaves = own_ref.shape[1]
    half, codes = acc_ref.shape
    block, chunk = a_ref.shape
    f32 = jnp.float32
    marks = Marks(max(block, half), chunk)

    def count(g):
        for c in range(chunk // LANES):
            leaf = marks.columns(target_ref, g, c)
            upper = leaf >= half
            leaf = jnp.where(leaf < leaves, jnp.where(upper, leaf - half, leaf), -1)
            marks.put(b_ref, c, leaf, jnp.where(upper, 4096.0, 1.0))
        for first in range(0, codes, block):
            for c in range(chunk // LANES):
                op = marks.columns(operator_ref, g, c)
                code = (op >> 2) * sources + marks.columns(source_ref, g, c) - first
                last = op & 3
                weight = jnp.where(last == 0, 1.0, jnp.where(last == 1, 8.0, jnp.where(last == 2, 64.0, 512.0)))
                marks.put(a_ref, c, code, weight)
            acc_ref[:, first : first + block] += lax.dot_general(b_ref[...], a_ref[...], NT, preferred_element_type=f32)

    acc_ref[...] = jnp.zeros_like(acc_ref)
    me = lax.axis_index("slab")
    last = lax.axis_size("slab") - 1
    from_right = me % 2 == 0
    ends = (jnp.logical_and(from_right, me == last), False, jnp.where(from_right, me == 0, me == last))
    for k, (ref, end) in enumerate(zip((first_ref, own_ref, second_ref), ends)):
        x, y, z = (
            jnp.clip(jnp.floor(ref[PTS * c : PTS * (c + 1), :] * UNITS), -UNITS, UNITS - 1.0).astype(jnp.int32)
            for c in range(3)
        )
        at = slice(leaves * k, leaves * (k + 1))
        packed_ref[:PTS, at] = (x << 11) | ((y >> 10) & 2047)
        packed_ref[PTS:, at] = (z << 11) | ((y & 1023) << 1)
        charge_ref[:, at] = jnp.where(end, 0.0, ref[3 * PTS :, :])

    def gather(place):
        idx = place & (LANES - 1)
        group = place >> 7
        refs = [packed_ref.at[8 * r : 8 * r + 8] for r in range(2 * PTS // 8)]
        refs += [charge_ref.at[8 * r : 8 * r + 8] for r in range(PTS // 8)]
        found = [lane_gather(ref[:, :LANES], idx) for ref in refs]
        for s in range(1, 3 * groups):
            here = group == s
            for r, ref in enumerate(refs):
                found[r] = jnp.where(here, lane_gather(ref[:, LANES * s : LANES * (s + 1)], idx), found[r])
        return found

    def step(g, carry):
        count(g)
        at = pl.ds(pl.multiple_of(g * LANES, LANES), LANES)
        tx, ty, tz = (own_ref[PTS * c : PTS * (c + 1), at] * SCALE for c in range(3))
        square = tx * tx + ty * ty + (tz * tz + SOFT2 * SCALE * SCALE)
        tx, ty, tz = -2.0 * tx, -2.0 * ty, -2.0 * tz
        acc = jnp.zeros((PTS, LANES), f32)
        for n in range(near):
            found = gather(jnp.broadcast_to(place_ref[g, n : n + 1, :], (8, LANES)))
            for r in range(PTS // 8):
                first, second, charge = found[r :: PTS // 8]
                x = first.astype(f32)
                y = ((first << 21) | ((second & 2047) << 10)).astype(f32)
                z = second.astype(f32)
                for k, row in enumerate((x, y, z, charge, x * x + y * y + z * z)):
                    picked_ref[n, PTS * k + 8 * r : PTS * k + 8 * r + 8, :] = row
            for p in range(PTS):
                sx, sy, sz, q, far = (picked_ref[n, PTS * c + p : PTS * c + p + 1, :] for c in range(5))
                acc += q * lax.rsqrt((square + far) + tx * sx + (ty * sy + tz * sz))
        pot_ref[g] = acc * SCALE
        return carry

    lax.fori_loop(0, groups, step, 0)
    width = LANES // 2
    pieces = []
    for g in range(groups):
        pot = pot_ref[g]
        pieces += [pot[:, :width], pot[:, width:]]
    near_ref[...] = jnp.concatenate(pieces, axis=0).T

    value = acc_ref[...]
    peak_ref[...] = jnp.max(value.reshape(-1, 8, codes), axis=0)
    value = value.astype(jnp.int32)
    for digit in range(8):
        h, d = digit // 4, digit % 4
        here = (value >> (3 * digit)) & 7
        low_ref[half * h : half * (h + 1), codes * d : codes * (d + 1)] = here.astype(f32).astype(jnp.bfloat16)


def far_kernel(
    parts_ref, received_ref, low_ref, peak_ref, source_ref, target_ref, operator_ref,
    out_ref, split_ref, pair_ref, a_ref, b_ref, *, ops,
):
    ncoef, leaves = out_ref.shape
    sources = received_ref.shape[0]
    f32 = jnp.float32
    hi, lo = split(pad_lanes(received_ref[...]))
    table = lax.dot_general(
        parts_ref[...], jnp.concatenate([hi, hi], axis=1), NT, preferred_element_type=f32
    ) + lax.dot_general(parts_ref[:, :LANES], lo, NT, preferred_element_type=f32)
    ones = jnp.where(lax.broadcasted_iota(jnp.int32, (LANES, sources), 0) == LANES - 1, 1.0, 0.0)
    for k in range(ops):
        hi, lo = split(table[LANES * k : LANES * (k + 1), :] + ones)
        split_ref[:LANES, sources * k : sources * (k + 1)] = hi
        split_ref[LANES:, sources * k : sources * (k + 1)] = lo
    both = lax.dot_general(split_ref[...], low_ref[...], NT, preferred_element_type=f32)
    out_ref[...] = both[:ncoef, :] + both[LANES : LANES + ncoef, :]

    used = jnp.sum(jnp.where(target_ref[...] < leaves, 1.0, 0.0))
    total = jnp.sum(both[LANES - 1 : LANES, :])
    carried = jnp.logical_or(total != used, jnp.max(peak_ref[...]) >= 2.0**24)

    @pl.when(carried)
    def _():
        size, chunk = a_ref.shape
        marks = Marks(max(size, leaves), chunk)
        out_ref[...] = jnp.zeros_like(out_ref)
        for first in range(0, ops // 2 * sources, size):
            pair_ref[...] = jnp.full(pair_ref.shape, -(2.0**24), f32)

            def more(part, carry):
                for c in range(chunk // LANES):
                    op = marks.columns(operator_ref, part, c)
                    code = (op >> 1) * sources + marks.columns(source_ref, part, c) - first
                    marks.put(a_ref, c, code, jnp.where((op & 1) == 1, 8192.0, 1.0))
                    marks.put(b_ref, c, marks.columns(target_ref, part, c), jnp.ones((1, LANES), f32))
                pair_ref[...] += lax.dot_general(b_ref[...], a_ref[...], NT, preferred_element_type=f32)
                return carry

            lax.fori_loop(0, target_ref.shape[1] // chunk, more, 0)
            for lane in range(first, first + size, LANES):
                value = pair_ref[:, lane - first : lane - first + LANES]
                odd = jnp.floor(value * (1.0 / 8192.0))
                for parity, count in enumerate((value - 8192.0 * odd, odd + 2048.0)):
                    at = spot(2 * (lane // sources) + parity, ops) * sources + lane % sources
                    rows = split_ref[:, at : at + LANES].astype(f32)
                    rows = rows[:ncoef, :] + rows[LANES : LANES + ncoef, :]
                    out_ref[...] += lax.dot_general(
                        rows, count, NT, precision=lax.Precision.HIGHEST, preferred_element_type=f32
                    )


def shards(
    coords,
    charges,
    multipoles,
    operators,
    send_list,
    near_list,
    m2l_source,
    m2l_target,
    m2l_operator,
):
    ncoef, leaves = multipoles.shape
    npoints = charges.shape[0]
    near = near_list.shape[1]
    entries = m2l_source.shape[1]
    ops = operators.shape[0]
    sources = send_list.shape[1]
    peers = lax.axis_size("grp")
    f32, bf16 = jnp.float32, jnp.bfloat16

    tiles = npoints // LANES
    points = (jnp.transpose(coords.reshape(3, tiles, LANES), (1, 0, 2)), charges.reshape(tiles, LANES))
    others = (
        near_list.T,
        m2l_source,
        m2l_target,
        m2l_operator,
        jnp.transpose(operators, (1, 0, 2)).reshape(ncoef * ops, ncoef),
    )
    table, outgoing, near_list, m2l_source, m2l_target, m2l_operator, operators = pl.pallas_call(
        functools.partial(prep_kernel, others=len(others)),
        name="prep",
        out_shape=(
            pltpu.VMEM((4 * PTS, leaves), f32),
            pltpu.VMEM((sources, ncoef), f32),
            *(pltpu.VMEM(x.shape, x.dtype) for x in others),
        ),
        in_specs=[ANY] * (4 + len(others)),
        out_specs=(VMEM,) * (2 + len(others)),
        scratch_shapes=[
            pltpu.VMEM((tiles, 3, LANES), f32),
            pltpu.VMEM((tiles, LANES), f32),
            pltpu.VMEM((ncoef, leaves), f32),
            pltpu.VMEM((1, sources), jnp.int32),
            pltpu.SemaphoreType.DMA((4 + len(others),)),
        ],
        compiler_params=PARAMS,
    )(*(pltpu.with_memory_space_constraint(x, pltpu.HBM) for x in (*points, multipoles, send_list, *others)))
    received = lax.all_to_all(
        outgoing.reshape(peers, sources // peers, ncoef), "grp", split_axis=0, concat_axis=0, tiled=True
    ).reshape(sources, ncoef)
    slabs = lax.axis_size("slab")

    def exchange(start):
        partner = list(range(slabs))
        for i in range(start, slabs - 1, 2):
            partner[i], partner[i + 1] = i + 1, i
        return lax.ppermute(table, "slab", list(enumerate(partner)))

    first = exchange(0)
    second = exchange(1)

    codes = ops // 4 * sources
    block = min(codes, 512)
    groups = leaves // LANES
    chunk = entries // groups
    places, parts = pl.pallas_call(
        functools.partial(cut_kernel, ops=ops),
        name="cut",
        out_shape=(
            jax.ShapeDtypeStruct((groups, near, LANES), jnp.int32),
            jax.ShapeDtypeStruct((ops * LANES, 2 * LANES), bf16),
        ),
        in_specs=[VMEM] * 2,
        out_specs=(VMEM,) * 2,
        scratch_shapes=[pltpu.VMEM((ncoef * ops, LANES), f32)],
        compiler_params=PARAMS,
    )(near_list, operators)
    near_potential, low, peak = pl.pallas_call(
        functools.partial(near_kernel, sources=sources),
        name="near_counts",
        out_shape=(
            jax.ShapeDtypeStruct((tiles, LANES), f32),
            jax.ShapeDtypeStruct((leaves, ops * sources), bf16),
            jax.ShapeDtypeStruct((8, codes), f32),
        ),
        in_specs=[VMEM] * 7,
        out_specs=(VMEM,) * 3,
        scratch_shapes=[
            pltpu.VMEM((2 * PTS, 3 * leaves), jnp.int32),
            pltpu.VMEM((PTS, 3 * leaves), f32),
            pltpu.VMEM((near, 5 * PTS, LANES), f32),
            pltpu.VMEM((groups, PTS, LANES), f32),
            pltpu.VMEM((leaves // 2, codes), f32),
            pltpu.VMEM((block, chunk), bf16),
            pltpu.VMEM((leaves // 2, chunk), bf16),
        ],
        compiler_params=PARAMS,
    )(second, table, first, places, m2l_source, m2l_target, m2l_operator)

    local_exp = pl.pallas_call(
        functools.partial(far_kernel, ops=ops),
        name="far",
        out_shape=jax.ShapeDtypeStruct((ncoef, leaves), f32),
        in_specs=[VMEM] * 7,
        out_specs=VMEM,
        scratch_shapes=[
            pltpu.VMEM((2 * LANES, ops * sources), bf16),
            pltpu.VMEM((leaves, 512), f32),
            pltpu.VMEM((512, 512), bf16),
            pltpu.VMEM((leaves, 512), bf16),
        ],
        compiler_params=PARAMS,
    )(parts, received, low, peak, m2l_source, m2l_target, m2l_operator)
    return (local_exp, near_potential.reshape(npoints))


def solution(mesh):
    both = ("slab", "grp")
    return jax.shard_map(
        shards,
        mesh=mesh,
        in_specs=(
            P(None, both),
            P(both),
            P(None, both),
            P(),
            P(both, None),
            P(both, None),
            P(both, None),
            P(both, None),
            P(both, None),
        ),
        out_specs=(P(None, both), P(both)),
        check_vma=False,
    )
```

time: 20.3 us -> 19.2 us (0.946)
  Pallas kernels: 9.7 us -> 8.55 us
    pallas_call x1, Pallas kernels: 5.98 us -> 4.76 us  [shards(): pl.pallas_call(functools.partial(near_kernel, sources=sources), name='nea...]
  transfers between devices with their start and end apart: 3 -> 3, of which waited for: 0 -> 0; matrix products, arithmetic and copies ran while one was open for 0% -> 0% of each run, Pallas kernels for 31% -> 26%
where the time goes in v8:
time: 19.2 us; the launch traced here: 18.9 us
  starting transfers between devices  9.69 us (50%)
  Pallas kernels  8.55 us (45%)
  between operations  0.67 us (3%)
    all_to_all x1, starting transfers between devices, shards(): lax.all_to_all(outgoing.reshape(peers, sources // peers, ncoef), 'grp', s...  5.14 us
    pallas_call x1, Pallas kernels, shards(): pl.pallas_call(functools.partial(near_kernel, sources=sources), name='nea...  4.76 us
    ppermute x2, starting transfers between devices, exchange(): return lax.ppermute(table, 'slab', list(enumerate(partner)))  4.55 us
    pallas_call x1, Pallas kernels, shards(): pl.pallas_call(functools.partial(prep_kernel, others=len(others)), name='...  2.07 us
    pallas_call x1, Pallas kernels, shards(): pl.pallas_call(functools.partial(far_kernel, ops=ops), name='far', out_sh...  1.57 us
  transfers between devices with their start and end apart: 3, of which 0 were waited for; matrix products, arithmetic and copies ran while one was open for 0% of the time, Pallas kernels for 26%

profile of v8, /device:TPU:11, one launch (start us, length us, event | category | flops | bytes accessed | tf_op | source)
XLA Modules:
  0.0 18.9 jit_solution(838365879351367546)
XLA Ops:
  0.6 2.1 %prep.1 = (f32[64,512]{1,0:T(8,128)S(1)}, f32[128,121]{1,0:T(8,128)}, s32[8,512]{1,0:T(8,128)S(1)}, s32[1,4096]{1,0:T(1,128)S(1)}, s32[1,4096]{1,0:T(1,128)S(1)}...) custom-call(f32[64,3,128]{2,1,0:T(4,128)} %bitcast.13, f32[64,128]{1,0:T(8,128)} %bitcast.14, f32[121,512]{1,0:T(8,128)} %multipoles_hbm.1, ...), custom_call_target="tpu_custom_call" | custom-call | tf_op jit(solution)/shard_map/prep/pallas_call | solution.py:293
  2.7 0.2 %collective-permute-start.1 = (f32[64,512]{1,0:T(8,128)S(1)}, f32[64,512]{1,0:T(8,128)S(1)}, u32[]{:S(2)}, u32[]{:S(2)}) collective-permute-start(f32[64,512]{1,0:T(8,128)S(1)} %get-tuple-element.18.own_ref), channel_id=1, source_target_pairs={{0,8},{8,0},{16,24},{24,16},{1,9},{9,1},{17,25},{25,17},{2,10},{10... | collective-permute-start | bytes 393224 | tf_op jit(solution)/shard_map/ppermute | solution.py:321
  2.9 4.3 %collective-permute-start = (f32[64,512]{1,0:T(8,128)S(1)}, f32[64,512]{1,0:T(8,128)S(1)}, u32[]{:S(2)}, u32[]{:S(2)}) collective-permute-start(f32[64,512]{1,0:T(8,128)S(1)} %get-tuple-element.18.own_ref), channel_id=1, source_target_pairs={{0,0},{8,16},{16,8},{24,24},{1,1},{9,17},{17,9},{25,25},{2,2},{10,... | collective-permute-start | bytes 393224 | tf_op jit(solution)/shard_map/ppermute | solution.py:321
  7.3 5.1 %all-to-all-start = ((f32[8,16,121]{2,1,0:T(8,128)}), f32[8,16,121]{2,1,0:T(8,128)S(1)}, u32[]{:S(2)}, u32[]{:S(2)}) async-start(f32[8,16,121]{2,1,0:T(8,128)} %bitcast.6), calls=%async_computation | async-start | bytes 131072 | tf_op jit(solution)/shard_map/all_to_all | solution.py:312
  12.4 0.2 cut.1
  12.6 0.0 collective-permute-done.1.first_ref
  12.6 0.0 collective-permute-done.second_ref
  12.6 4.8 %near_counts.1 = (f32[64,128]{1,0:T(8,128)}, bf16[512,1024]{1,0:T(8,128)(2,1)S(1)}, f32[8,256]{1,0:T(8,128)S(1)}) custom-call(f32[64,512]{1,0:T(8,128)S(1)} %collective-permute-done.second_ref, f32[64,512]{1,0:T(8,128)S(1)} %get-tuple-element.18.own_ref, f32[64,512]{1,0:T(8,128)S(1)} %collective-permute-done.1.first_ref, ...), custom_call_target="tpu_custom_call" | custom-call | tf_op jit(solution)/shard_map/near_counts/pallas_call | solution.py:342
  17.4 0.0 all-to-all-done
  17.4 1.6 %far.1 = f32[121,512]{1,0:T(8,128)} custom-call(bf16[1024,256]{1,0:T(8,128)(2,1)S(1)} %get-tuple-element.16.parts_ref, f32[128,121]{1,0:T(8,128)S(1)} %bitcast.11, bf16[512,1024]{1,0:T(8,128)(2,1)S(1)} %get-tuple-element.23.low_ref, f32[8,256]{1,0:T(8,128)S(1)} %get-tuple-element.24.peak_ref, s32[1,4096]{1,0:T(1,128)S(1)} %get-tuple-element.20.source_ref, ...), custom_call_target="tpu_custom_call" | custom-call | tf_op jit(solution)/shard_map/far/pallas_call | solution.py:364
Async XLA Ops:
  2.7 9.9 %collective-permute-start.1 = (f32[64,512]{1,0:T(8,128)S(1)}, f32[64,512]{1,0:T(8,128)S(1)}, u32[]{:S(2)}, u32[]{:S(2)}) collective-permute-start(f32[64,512]{1,0:T(8,128)S(1)} %get-tuple-element.18.own_ref), channel_id=1, source_target_pairs={{0,8},{8,0},{16,24},{24,16},{1,9},{9,1},{17,25},{25,17},{2,10},{10... | collective-permute-start | bytes 393224 | tf_op jit(solution)/shard_map/ppermute | solution.py:321
  2.9 9.6 %collective-permute-start = (f32[64,512]{1,0:T(8,128)S(1)}, f32[64,512]{1,0:T(8,128)S(1)}, u32[]{:S(2)}, u32[]{:S(2)}) collective-permute-start(f32[64,512]{1,0:T(8,128)S(1)} %get-tuple-element.18.own_ref), channel_id=1, source_target_pairs={{0,0},{8,16},{16,8},{24,24},{1,1},{9,17},{17,9},{25,25},{2,2},{10,... | collective-permute-start | bytes 393224 | tf_op jit(solution)/shard_map/ppermute | solution.py:321
  7.3 10.1 %all-to-all-start = ((f32[8,16,121]{2,1,0:T(8,128)}), f32[8,16,121]{2,1,0:T(8,128)S(1)}, u32[]{:S(2)}, u32[]{:S(2)}) async-start(f32[8,16,121]{2,1,0:T(8,128)} %bitcast.6), calls=%async_computation | async-start | bytes 131072 | tf_op jit(solution)/shard_map/all_to_all | solution.py:312

commit v9 on v8

--- a/solution.py
+++ b/solution.py
@@ -316,6 +316,8 @@
 
     def exchange(start):
         partner = list(range(slabs))
+        if start == 1 and slabs % 2 == 0:
+            partner[0], partner[-1] = slabs - 1, 0
         for i in range(start, slabs - 1, 2):
             partner[i], partner[i + 1] = i + 1, i
         return lax.ppermute(table, "slab", list(enumerate(partner)))

time: 19.2 us -> 21 us (1.094)
  the two profiles are of different devices: /device:TPU:11 before, /device:TPU:0 now
where the time goes in v9:
time: 21 us; the launch traced here: 20.7 us
  starting transfers between devices  9.29 us (44%)
  Pallas kernels  8.55 us (41%)
  waiting for transfers between devices  2.24 us (11%)
  between operations  0.66 us (3%)
    ppermute x2, starting transfers between devices, exchange(): return lax.ppermute(table, 'slab', list(enumerate(partner)))  5.56 us
    pallas_call x1, Pallas kernels, shards(): pl.pallas_call(functools.partial(near_kernel, sources=sources), name='nea...  4.75 us
    all_to_all x1, starting transfers between devices, shards(): lax.all_to_all(outgoing.reshape(peers, sources // peers, ncoef), 'grp', s...  3.72 us
    ppermute x2, waiting for transfers between devices, exchange(): return lax.ppermute(table, 'slab', list(enumerate(partner)))  2.23 us
    pallas_call x1, Pallas kernels, shards(): pl.pallas_call(functools.partial(prep_kernel, others=len(others)), name='...  2.07 us
    pallas_call x1, Pallas kernels, shards(): pl.pallas_call(functools.partial(far_kernel, ops=ops), name='far', out_sh...  1.57 us
  transfers between devices with their start and end apart: 3, of which 1 were waited for; matrix products, arithmetic and copies ran while one was open for 0% of the time, Pallas kernels for 24%

profile of v9, /device:TPU:0, one launch (start us, length us, event | category | flops | bytes accessed | tf_op | source)
XLA Modules:
  0.0 20.7 jit_solution(14791820090151554455)
XLA Ops:
  0.6 2.1 %prep.1 = (f32[64,512]{1,0:T(8,128)S(1)}, f32[128,121]{1,0:T(8,128)}, s32[8,512]{1,0:T(8,128)S(1)}, s32[1,4096]{1,0:T(1,128)S(1)}, s32[1,4096]{1,0:T(1,128)S(1)}...) custom-call(f32[64,3,128]{2,1,0:T(4,128)} %bitcast.13, f32[64,128]{1,0:T(8,128)} %bitcast.14, f32[121,512]{1,0:T(8,128)} %multipoles_hbm.1, ...), custom_call_target="tpu_custom_call" | custom-call | tf_op jit(solution)/shard_map/prep/pallas_call | solution.py:293
  2.7 3.1 %collective-permute-start.1 = (f32[64,512]{1,0:T(8,128)S(1)}, f32[64,512]{1,0:T(8,128)S(1)}, u32[]{:S(2)}, u32[]{:S(2)}) collective-permute-start(f32[64,512]{1,0:T(8,128)S(1)} %get-tuple-element.18.own_ref), channel_id=1, source_target_pairs={{0,8},{8,0},{16,24},{24,16},{1,9},{9,1},{17,25},{25,17},{2,10},{10... | collective-permute-start | bytes 393224 | tf_op jit(solution)/shard_map/ppermute | solution.py:323
  5.8 2.5 %collective-permute-start = (f32[64,512]{1,0:T(8,128)S(1)}, f32[64,512]{1,0:T(8,128)S(1)}, u32[]{:S(2)}, u32[]{:S(2)}) collective-permute-start(f32[64,512]{1,0:T(8,128)S(1)} %get-tuple-element.18.own_ref), channel_id=1, source_target_pairs={{0,24},{8,16},{16,8},{24,0},{1,25},{9,17},{17,9},{25,1},{2,26},{10... | collective-permute-start | bytes 393224 | tf_op jit(solution)/shard_map/ppermute | solution.py:323
  8.3 3.7 %all-to-all-start = ((f32[8,16,121]{2,1,0:T(8,128)}), f32[8,16,121]{2,1,0:T(8,128)S(1)}, u32[]{:S(2)}, u32[]{:S(2)}) async-start(f32[8,16,121]{2,1,0:T(8,128)} %bitcast.6), calls=%async_computation | async-start | bytes 131072 | tf_op jit(solution)/shard_map/all_to_all | solution.py:312
  12.0 0.2 cut.1
  12.2 0.0 collective-permute-done.1.first_ref
  12.2 2.2 %collective-permute-done.second_ref = f32[64,512]{1,0:T(8,128)S(1)} collective-permute-done((f32[64,512]{1,0:T(8,128)S(1)}, f32[64,512]{1,0:T(8,128)S(1)}, u32[]{:S(2)}, u32[]{:S(2)}) %collective-permute-start) | collective-permute-done | bytes 131104 | tf_op jit(solution)/shard_map/ppermute | solution.py:323
  14.4 4.8 %near_counts.1 = (f32[64,128]{1,0:T(8,128)}, bf16[512,1024]{1,0:T(8,128)(2,1)S(1)}, f32[8,256]{1,0:T(8,128)S(1)}) custom-call(f32[64,512]{1,0:T(8,128)S(1)} %collective-permute-done.second_ref, f32[64,512]{1,0:T(8,128)S(1)} %get-tuple-element.18.own_ref, f32[64,512]{1,0:T(8,128)S(1)} %collective-permute-done.1.first_ref, ...), custom_call_target="tpu_custom_call" | custom-call | tf_op jit(solution)/shard_map/near_counts/pallas_call | solution.py:344
  19.2 0.0 all-to-all-done
  19.2 1.6 %far.1 = f32[121,512]{1,0:T(8,128)} custom-call(bf16[1024,256]{1,0:T(8,128)(2,1)S(1)} %get-tuple-element.16.parts_ref, f32[128,121]{1,0:T(8,128)S(1)} %bitcast.11, bf16[512,1024]{1,0:T(8,128)(2,1)S(1)} %get-tuple-element.23.low_ref, f32[8,256]{1,0:T(8,128)S(1)} %get-tuple-element.24.peak_ref, s32[1,4096]{1,0:T(1,128)S(1)} %get-tuple-element.20.source_ref, ...), custom_call_target="tpu_custom_call" | custom-call | tf_op jit(solution)/shard_map/far/pallas_call | solution.py:366
Async XLA Ops:
  2.7 9.5 %collective-permute-start.1 = (f32[64,512]{1,0:T(8,128)S(1)}, f32[64,512]{1,0:T(8,128)S(1)}, u32[]{:S(2)}, u32[]{:S(2)}) collective-permute-start(f32[64,512]{1,0:T(8,128)S(1)} %get-tuple-element.18.own_ref), channel_id=1, source_target_pairs={{0,8},{8,0},{16,24},{24,16},{1,9},{9,1},{17,25},{25,17},{2,10},{10... | collective-permute-start | bytes 393224 | tf_op jit(solution)/shard_map/ppermute | solution.py:323
  5.8 8.6 %collective-permute-start = (f32[64,512]{1,0:T(8,128)S(1)}, f32[64,512]{1,0:T(8,128)S(1)}, u32[]{:S(2)}, u32[]{:S(2)}) collective-permute-start(f32[64,512]{1,0:T(8,128)S(1)} %get-tuple-element.18.own_ref), channel_id=1, source_target_pairs={{0,24},{8,16},{16,8},{24,0},{1,25},{9,17},{17,9},{25,1},{2,26},{10... | collective-permute-start | bytes 393224 | tf_op jit(solution)/shard_map/ppermute | solution.py:323
  8.3 10.9 %all-to-all-start = ((f32[8,16,121]{2,1,0:T(8,128)}), f32[8,16,121]{2,1,0:T(8,128)S(1)}, u32[]{:S(2)}, u32[]{:S(2)}) async-start(f32[8,16,121]{2,1,0:T(8,128)} %bitcast.6), calls=%async_computation | async-start | bytes 131072 | tf_op jit(solution)/shard_map/all_to_all | solution.py:312

commit v10 on v8

--- a/solution.py
+++ b/solution.py
@@ -315,10 +315,15 @@
     slabs = lax.axis_size("slab")
 
     def exchange(start):
-        partner = list(range(slabs))
-        for i in range(start, slabs - 1, 2):
-            partner[i], partner[i + 1] = i + 1, i
-        return lax.ppermute(table, "slab", list(enumerate(partner)))
+        to = {}
+        for slab in range(slabs):
+            other = slab + 1 if (slab - start) % 2 == 0 else slab - 1
+            for peer in range(peers):
+                if 0 <= other < slabs:
+                    to[slab * peers + peer] = other * peers + peer
+                else:
+                    to[slab * peers + peer] = slab * peers + min(peer ^ 1, peers - 1)
+        return lax.ppermute(table, ("slab", "grp"), sorted(to.items()))
 
     first = exchange(0)
     second = exchange(1)

time: 19.2 us -> 17.3 us (0.901)
  starting transfers between devices: 9.69 us -> 7.79 us
    ppermute x2, starting transfers between devices: 4.55 us -> 2.66 us  [exchange(): return lax.ppermute(table, ('slab', 'grp'), sorted(to.items()))]
  transfers between devices with their start and end apart: 3 -> 3, of which waited for: 0 -> 0; matrix products, arithmetic and copies ran while one was open for 0% -> 0% of each run, Pallas kernels for 26% -> 29%
where the time goes in v10:
time: 17.3 us; the launch traced here: 17 us
  Pallas kernels  8.56 us (49%)
  starting transfers between devices  7.79 us (45%)
  between operations  0.66 us (4%)
    all_to_all x1, starting transfers between devices, shards(): lax.all_to_all(outgoing.reshape(peers, sources // peers, ncoef), 'grp', s...  5.13 us
    pallas_call x1, Pallas kernels, shards(): pl.pallas_call(functools.partial(near_kernel, sources=sources), name='nea...  4.76 us
    ppermute x2, starting transfers between devices, exchange(): return lax.ppermute(table, ('slab', 'grp'), sorted(to.items()))  2.66 us
    pallas_call x1, Pallas kernels, shards(): pl.pallas_call(functools.partial(prep_kernel, others=len(others)), name='...  2.07 us
    pallas_call x1, Pallas kernels, shards(): pl.pallas_call(functools.partial(far_kernel, ops=ops), name='far', out_sh...  1.57 us
  transfers between devices with their start and end apart: 3, of which 0 were waited for; matrix products, arithmetic and copies ran while one was open for 0% of the time, Pallas kernels for 29%

profile of v10, /device:TPU:11, one launch (start us, length us, event | category | flops | bytes accessed | tf_op | source)
XLA Modules:
  0.0 17.0 jit_solution(14962839530707957317)
XLA Ops:
  0.6 2.1 %prep.1 = (f32[64,512]{1,0:T(8,128)S(1)}, f32[128,121]{1,0:T(8,128)}, s32[8,512]{1,0:T(8,128)S(1)}, s32[1,4096]{1,0:T(1,128)S(1)}, s32[1,4096]{1,0:T(1,128)S(1)}...) custom-call(f32[64,3,128]{2,1,0:T(4,128)} %bitcast.13, f32[64,128]{1,0:T(8,128)} %bitcast.14, f32[121,512]{1,0:T(8,128)} %multipoles_hbm.1, ...), custom_call_target="tpu_custom_call" | custom-call | tf_op jit(solution)/shard_map/prep/pallas_call | solution.py:293
  2.7 0.2 %collective-permute-start.1 = (f32[64,512]{1,0:T(8,128)S(1)}, f32[64,512]{1,0:T(8,128)S(1)}, u32[]{:S(2)}, u32[]{:S(2)}) collective-permute-start(f32[64,512]{1,0:T(8,128)S(1)} %get-tuple-element.18.own_ref), channel_id=1, source_target_pairs={{0,8},{1,9},{2,10},{3,11},{4,12},{5,13},{6,14},{7,15},{8,0},{9,1},... | collective-permute-start | bytes 393224 | tf_op jit(solution)/shard_map/ppermute | solution.py:326
  2.9 2.4 %collective-permute-start = (f32[64,512]{1,0:T(8,128)S(1)}, f32[64,512]{1,0:T(8,128)S(1)}, u32[]{:S(2)}, u32[]{:S(2)}) collective-permute-start(f32[64,512]{1,0:T(8,128)S(1)} %get-tuple-element.18.own_ref), channel_id=1, source_target_pairs={{0,1},{1,0},{2,3},{3,2},{4,5},{5,4},{6,7},{7,6},{8,16},{9,17},{10,... | collective-permute-start | bytes 393224 | tf_op jit(solution)/shard_map/ppermute | solution.py:326
  5.4 5.1 %all-to-all-start = ((f32[8,16,121]{2,1,0:T(8,128)}), f32[8,16,121]{2,1,0:T(8,128)S(1)}, u32[]{:S(2)}, u32[]{:S(2)}) async-start(f32[8,16,121]{2,1,0:T(8,128)} %bitcast.6), calls=%async_computation | async-start | bytes 131072 | tf_op jit(solution)/shard_map/all_to_all | solution.py:312
  10.5 0.2 cut.1
  10.7 0.0 collective-permute-done.1.first_ref
  10.7 0.0 collective-permute-done.second_ref
  10.7 4.8 %near_counts.1 = (f32[64,128]{1,0:T(8,128)}, bf16[512,1024]{1,0:T(8,128)(2,1)S(1)}, f32[8,256]{1,0:T(8,128)S(1)}) custom-call(f32[64,512]{1,0:T(8,128)S(1)} %collective-permute-done.second_ref, f32[64,512]{1,0:T(8,128)S(1)} %get-tuple-element.18.own_ref, f32[64,512]{1,0:T(8,128)S(1)} %collective-permute-done.1.first_ref, ...), custom_call_target="tpu_custom_call" | custom-call | tf_op jit(solution)/shard_map/near_counts/pallas_call | solution.py:347
  15.4 0.0 all-to-all-done
  15.4 1.6 %far.1 = f32[121,512]{1,0:T(8,128)} custom-call(bf16[1024,256]{1,0:T(8,128)(2,1)S(1)} %get-tuple-element.16.parts_ref, f32[128,121]{1,0:T(8,128)S(1)} %bitcast.11, bf16[512,1024]{1,0:T(8,128)(2,1)S(1)} %get-tuple-element.23.low_ref, f32[8,256]{1,0:T(8,128)S(1)} %get-tuple-element.24.peak_ref, s32[1,4096]{1,0:T(1,128)S(1)} %get-tuple-element.20.source_ref, ...), custom_call_target="tpu_custom_call" | custom-call | tf_op jit(solution)/shard_map/far/pallas_call | solution.py:369
Async XLA Ops:
  2.7 8.0 %collective-permute-start.1 = (f32[64,512]{1,0:T(8,128)S(1)}, f32[64,512]{1,0:T(8,128)S(1)}, u32[]{:S(2)}, u32[]{:S(2)}) collective-permute-start(f32[64,512]{1,0:T(8,128)S(1)} %get-tuple-element.18.own_ref), channel_id=1, source_target_pairs={{0,8},{1,9},{2,10},{3,11},{4,12},{5,13},{6,14},{7,15},{8,0},{9,1},... | collective-permute-start | bytes 393224 | tf_op jit(solution)/shard_map/ppermute | solution.py:326
  2.9 7.7 %collective-permute-start = (f32[64,512]{1,0:T(8,128)S(1)}, f32[64,512]{1,0:T(8,128)S(1)}, u32[]{:S(2)}, u32[]{:S(2)}) collective-permute-start(f32[64,512]{1,0:T(8,128)S(1)} %get-tuple-element.18.own_ref), channel_id=1, source_target_pairs={{0,1},{1,0},{2,3},{3,2},{4,5},{5,4},{6,7},{7,6},{8,16},{9,17},{10,... | collective-permute-start | bytes 393224 | tf_op jit(solution)/shard_map/ppermute | solution.py:326
  5.4 10.1 %all-to-all-start = ((f32[8,16,121]{2,1,0:T(8,128)}), f32[8,16,121]{2,1,0:T(8,128)S(1)}, u32[]{:S(2)}, u32[]{:S(2)}) async-start(f32[8,16,121]{2,1,0:T(8,128)} %bitcast.6), calls=%async_computation | async-start | bytes 131072 | tf_op jit(solution)/shard_map/all_to_all | solution.py:312

commit v11 on v10

--- a/solution.py
+++ b/solution.py
@@ -31,10 +31,10 @@
     return jnp.concatenate([x, jnp.zeros((x.shape[0], LANES - x.shape[1]), x.dtype)], axis=1)
 
 
-def prep_kernel(coords_hbm, charges_hbm, multipoles_hbm, send_hbm, *refs, others):
+def prep_kernel(coords_hbm, charges_hbm, multipoles_hbm, send_hbm, *refs, others, cap):
     sources, refs = refs[:others], refs[others:]
-    (table_ref, out_ref, *targets), refs = refs[: others + 2], refs[others + 2 :]
-    coords_ref, charges_ref, multipoles_ref, send_ref, sems = refs
+    (table_ref, same_ref, other_ref, *targets), refs = refs[: others + 3], refs[others + 3 :]
+    coords_ref, charges_ref, multipoles_ref, send_ref, rows_ref, sems = refs
     pairs = (
         (coords_hbm, coords_ref),
         (charges_hbm, charges_ref),
@@ -66,9 +66,33 @@
         for g in range(leaves // LANES):
             got = lane_gather(multipoles_ref[:, LANES * g : LANES * (g + 1)], idx)
             picked = jnp.where(group == g, got, picked)
-        out_ref[LANES * sb : LANES * (sb + 1), :] = picked.T
+        rows_ref[LANES * sb : LANES * (sb + 1), :] = picked.T
+    side = lax.axis_index("grp") % 2 if cap else 0
+    count = rows_ref.shape[0] // cap if cap else 0
+    for k in range(count // 2):
+        for ref, peer in ((same_ref, 2 * k + side), (other_ref, 2 * k + 1 - side)):
+            ref[cap * k : cap * (k + 1), :] = rows_ref[pl.ds(pl.multiple_of(peer * cap, cap), cap), :]
+    if not cap:
+        same_ref[...] = rows_ref[: same_ref.shape[0], :]
+        other_ref[...] = rows_ref[same_ref.shape[0] :, :]
     for copy in copies[4:]:
         copy.wait()
+
+
+def join_kernel(out_ref, came_ref, *join_refs, cap):
+    chip = lax.axis_index("grp") // 2
+    for m, ref in enumerate(join_refs):
+        at = pl.ds(pl.multiple_of((chip ^ m) * cap, cap), cap)
+        ref[:cap, :] = out_ref[at, :]
+        ref[cap:, :] = came_ref[at, :]
+
+
+def placed(join_refs, rows_ref, cap):
+    me = lax.axis_index("grp")
+    for m, ref in enumerate(join_refs):
+        peer = me ^ (2 * m)
+        rows_ref[pl.ds(pl.multiple_of(peer * cap, cap), cap), :] = ref[:cap, :]
+        rows_ref[pl.ds(pl.multiple_of((peer ^ 1) * cap, cap), cap), :] = ref[cap:, :]
 
 
 def cut_kernel(list_ref, operators_ref, place_ref, parts_ref, wide_ref, *, ops):
@@ -209,9 +233,13 @@
 
 
 def far_kernel(
-    parts_ref, received_ref, low_ref, peak_ref, source_ref, target_ref, operator_ref,
-    out_ref, split_ref, pair_ref, a_ref, b_ref, *, ops,
+    parts_ref, low_ref, peak_ref, source_ref, target_ref, operator_ref, *refs, ops, cap,
 ):
+    *join_refs, out_ref, received_ref, split_ref, pair_ref, a_ref, b_ref = refs
+    if cap:
+        placed(join_refs, received_ref, cap)
+    else:
+        received_ref = join_refs[0]
     ncoef, leaves = out_ref.shape
     sources = received_ref.shape[0]
     f32 = jnp.float32
@@ -282,6 +310,7 @@
     f32, bf16 = jnp.float32, jnp.bfloat16
 
     tiles = npoints // LANES
+    cap = sources // peers if peers == 8 else 0
     points = (jnp.transpose(coords.reshape(3, tiles, LANES), (1, 0, 2)), charges.reshape(tiles, LANES))
     others = (
         near_list.T,
@@ -290,28 +319,46 @@
         m2l_operator,
         jnp.transpose(operators, (1, 0, 2)).reshape(ncoef * ops, ncoef),
     )
-    table, outgoing, near_list, m2l_source, m2l_target, m2l_operator, operators = pl.pallas_call(
-        functools.partial(prep_kernel, others=len(others)),
+    table, same, other, near_list, m2l_source, m2l_target, m2l_operator, operators = pl.pallas_call(
+        functools.partial(prep_kernel, others=len(others), cap=cap),
         name="prep",
         out_shape=(
             pltpu.VMEM((4 * PTS, leaves), f32),
-            pltpu.VMEM((sources, ncoef), f32),
+            pltpu.VMEM((sources // 2, ncoef), f32),
+            pltpu.VMEM((sources // 2, ncoef), f32),
             *(pltpu.VMEM(x.shape, x.dtype) for x in others),
         ),
         in_specs=[ANY] * (4 + len(others)),
-        out_specs=(VMEM,) * (2 + len(others)),
+        out_specs=(VMEM,) * (3 + len(others)),
         scratch_shapes=[
             pltpu.VMEM((tiles, 3, LANES), f32),
             pltpu.VMEM((tiles, LANES), f32),
             pltpu.VMEM((ncoef, leaves), f32),
             pltpu.VMEM((1, sources), jnp.int32),
+            pltpu.VMEM((sources, ncoef), f32),
             pltpu.SemaphoreType.DMA((4 + len(others),)),
         ],
         compiler_params=PARAMS,
     )(*(pltpu.with_memory_space_constraint(x, pltpu.HBM) for x in (*points, multipoles, send_list, *others)))
-    received = lax.all_to_all(
-        outgoing.reshape(peers, sources // peers, ncoef), "grp", split_axis=0, concat_axis=0, tiled=True
-    ).reshape(sources, ncoef)
+    if cap:
+        came = lax.ppermute(other, "grp", [(i, i ^ 1) for i in range(peers)])
+        joins = pl.pallas_call(
+            functools.partial(join_kernel, cap=cap),
+            name="join",
+            out_shape=(jax.ShapeDtypeStruct((2 * cap, ncoef), f32),) * (peers // 2),
+            in_specs=[VMEM] * 2,
+            out_specs=(VMEM,) * (peers // 2),
+            compiler_params=PARAMS,
+        )(same, came)
+        received = [joins[0]] + [
+            lax.ppermute(joins[m], "grp", [(i, i ^ (2 * m)) for i in range(peers)]) for m in range(1, peers // 2)
+        ]
+    else:
+        received = [
+            lax.all_to_all(
+                jnp.concatenate([same, other]).reshape(peers, sources // peers, ncoef), "grp", split_axis=0, concat_axis=0, tiled=True
+            ).reshape(sources, ncoef)
+        ]
     slabs = lax.axis_size("slab")
 
     def exchange(start):
@@ -367,19 +414,20 @@
     )(second, table, first, places, m2l_source, m2l_target, m2l_operator)
 
     local_exp = pl.pallas_call(
-        functools.partial(far_kernel, ops=ops),
+        functools.partial(far_kernel, ops=ops, cap=cap),
         name="far",
         out_shape=jax.ShapeDtypeStruct((ncoef, leaves), f32),
-        in_specs=[VMEM] * 7,
+        in_specs=[VMEM] * (6 + len(received)),
         out_specs=VMEM,
         scratch_shapes=[
+            pltpu.VMEM((sources, ncoef), f32),
             pltpu.VMEM((2 * LANES, ops * sources), bf16),
             pltpu.VMEM((leaves, 512), f32),
             pltpu.VMEM((512, 512), bf16),
             pltpu.VMEM((leaves, 512), bf16),
         ],
         compiler_params=PARAMS,
-    )(parts, received, low, peak, m2l_source, m2l_target, m2l_operator)
+    )(parts, low, peak, m2l_source, m2l_target, m2l_operator, *received)
     return (local_exp, near_potential.reshape(npoints))
 
 

time: 17.3 us -> 16.8 us (0.971)
  the two profiles are of different devices: /device:TPU:11 before, /device:TPU:0 now
where the time goes in v11:
time: 16.8 us; the launch traced here: 16.6 us
  Pallas kernels  7.96 us (47%)
  starting transfers between devices  7.09 us (42%)
  waiting for transfers between devices  0.9 us (5%)
  between operations  0.67 us (4%)
    pallas_call x1, Pallas kernels, shards(): pl.pallas_call(functools.partial(near_kernel, sources=sources), name='nea...  4.76 us
    ppermute x3, starting transfers between devices, shards(): lax.ppermute(joins[m], 'grp', [(i, i ^ 2 * m) for i in range(peers)])  3.49 us
    ppermute x2, starting transfers between devices, exchange(): return lax.ppermute(table, ('slab', 'grp'), sorted(to.items()))  3.09 us
    pallas_call x1, Pallas kernels, shards(): pl.pallas_call(functools.partial(far_kernel, ops=ops, cap=cap), name='far...  1.58 us
    pallas_call x1, Pallas kernels, shards(): pl.pallas_call(functools.partial(prep_kernel, others=len(others), cap=cap...  1.46 us
    ppermute x1, waiting for transfers between devices, shards(): came = lax.ppermute(other, 'grp', [(i, i ^ 1) for i in range(peers)])  0.88 us
    ppermute x1, starting transfers between devices, shards(): came = lax.ppermute(other, 'grp', [(i, i ^ 1) for i in range(peers)])  0.51 us
  transfers between devices with their start and end apart: 6, of which 1 were waited for; matrix products, arithmetic and copies ran while one was open for 0% of the time, Pallas kernels for 30%

profile of v11, /device:TPU:0, one launch (start us, length us, event | category | flops | bytes accessed | tf_op | source)
XLA Modules:
  0.0 16.6 jit_solution(9659711940734134925)
XLA Ops:
  0.6 1.5 %prep.1 = (f32[64,512]{1,0:T(8,128)S(1)}, f32[64,121]{1,0:T(8,128)S(1)}, f32[64,121]{1,0:T(8,128)S(1)}, s32[8,512]{1,0:T(8,128)S(1)}, s32[1,4096]{1,0:T(1,128)S(...) custom-call(f32[64,3,128]{2,1,0:T(4,128)} %bitcast.10, f32[64,128]{1,0:T(8,128)} %bitcast.11, ...), custom_call_target="tpu_custom_call" | custom-call | tf_op jit(solution)/shard_map/prep/pallas_call | solution.py:322
  2.1 3.1 %collective-permute-start.1 = (f32[64,512]{1,0:T(8,128)S(1)}, f32[64,512]{1,0:T(8,128)S(1)}, u32[]{:S(2)}, u32[]{:S(2)}) collective-permute-start(f32[64,512]{1,0:T(8,128)S(1)} %get-tuple-element.22.own_ref), channel_id=1, source_target_pairs={{0,8},{1,9},{2,10},{3,11},{4,12},{5,13},{6,14},{7,15},{8,0},{9,1},... | collective-permute-start | bytes 393224 | tf_op jit(solution)/shard_map/ppermute | solution.py:373
  5.2 0.0 collective-permute-start
  5.2 0.5 %collective-permute-start.2 = (f32[64,121]{1,0:T(8,128)S(1)}, f32[64,121]{1,0:T(8,128)S(1)}, u32[]{:S(2)}, u32[]{:S(2)}) collective-permute-start(f32[64,121]{1,0:T(8,128)S(1)} %get-tuple-element.30), channel_id=1, source_target_pairs={{0,1},{1,0},{2,3},{3,2},{4,5},{5,4},{6,7},{7,6},{8,9},{9,8},{10,11... | collective-permute-start | bytes 92936 | tf_op jit(solution)/shard_map/ppermute | solution.py:344
  5.7 0.9 %collective-permute-done.2.came_ref = f32[64,121]{1,0:T(8,128)S(1)} collective-permute-done((f32[64,121]{1,0:T(8,128)S(1)}, f32[64,121]{1,0:T(8,128)S(1)}, u32[]{:S(2)}, u32[]{:S(2)}) %collective-permute-start.2) | collective-permute-done | bytes 31008 | tf_op jit(solution)/shard_map/ppermute | solution.py:344
  6.6 1.5 %collective-permute-start.3 = (f32[32,121]{1,0:T(8,128)S(1)}, f32[32,121]{1,0:T(8,128)S(1)}, u32[]{:S(2)}, u32[]{:S(2)}) collective-permute-start(f32[32,121]{1,0:T(8,128)S(1)} %get-tuple-element.32), channel_id=1, source_target_pairs={{0,2},{1,3},{2,0},{3,1},{4,6},{5,7},{6,4},{7,5},{8,10},{9,11},{10,... | collective-permute-start | bytes 46472 | tf_op jit(solution)/shard_map/ppermute | solution.py:354
  8.1 1.5 %collective-permute-start.4 = (f32[32,121]{1,0:T(8,128)S(1)}, f32[32,121]{1,0:T(8,128)S(1)}, u32[]{:S(2)}, u32[]{:S(2)}) collective-permute-start(f32[32,121]{1,0:T(8,128)S(1)} %get-tuple-element.33), channel_id=1, source_target_pairs={{0,4},{1,5},{2,6},{3,7},{4,0},{5,1},{6,2},{7,3},{8,12},{9,13},{10,... | collective-permute-start | bytes 46472 | tf_op jit(solution)/shard_map/ppermute | solution.py:354
  9.6 0.5 %collective-permute-start.5 = (f32[32,121]{1,0:T(8,128)S(1)}, f32[32,121]{1,0:T(8,128)S(1)}, u32[]{:S(2)}, u32[]{:S(2)}) collective-permute-start(f32[32,121]{1,0:T(8,128)S(1)} %get-tuple-element.34), channel_id=1, source_target_pairs={{0,6},{1,7},{2,4},{3,5},{4,2},{5,3},{6,0},{7,1},{8,14},{9,15},{10,... | collective-permute-start | bytes 46472 | tf_op jit(solution)/shard_map/ppermute | solution.py:354
  10.1 0.2 cut.1
  10.2 0.0 collective-permute-done.1.first_ref
  10.2 0.0 collective-permute-done.second_ref
  10.3 4.8 %near_counts.1 = (f32[64,128]{1,0:T(8,128)}, bf16[512,1024]{1,0:T(8,128)(2,1)S(1)}, f32[8,256]{1,0:T(8,128)S(1)}) custom-call(f32[64,512]{1,0:T(8,128)S(1)} %collective-permute-done.second_ref, f32[64,512]{1,0:T(8,128)S(1)} %get-tuple-element.22.own_ref, f32[64,512]{1,0:T(8,128)S(1)} %collective-permute-done.1.first_ref, ...), custom_call_target="tpu_custom_call" | custom-call | tf_op jit(solution)/shard_map/near_counts/pallas_call | solution.py:394
  15.0 0.0 collective-permute-done.3.refs_1_
  15.0 0.0 collective-permute-done.4.refs_2_
  15.0 0.0 collective-permute-done.5.refs_3_
  15.0 1.6 %far.1 = f32[121,512]{1,0:T(8,128)} custom-call(bf16[1024,256]{1,0:T(8,128)(2,1)S(1)} %get-tuple-element.21.parts_ref, bf16[512,1024]{1,0:T(8,128)(2,1)S(1)} %get-tuple-element.27.low_ref, f32[8,256]{1,0:T(8,128)S(1)} %get-tuple-element.28.peak_ref, s32[1,4096]{1,0:T(1,128)S(1)} %get-tuple-element.24.source_ref, s32[1,4096]{1,0:T(1,128)S(1)} %get-tuple-element.25.target_ref, ...), custom_call_target="tpu_custom_call" | custom-call | tf_op jit(solution)/shard_map/far/pallas_call | solution.py:416
  (1 shorter events, 0.0 us)
Async XLA Ops:
  2.1 8.1 %collective-permute-start.1 = (f32[64,512]{1,0:T(8,128)S(1)}, f32[64,512]{1,0:T(8,128)S(1)}, u32[]{:S(2)}, u32[]{:S(2)}) collective-permute-start(f32[64,512]{1,0:T(8,128)S(1)} %get-tuple-element.22.own_ref), channel_id=1, source_target_pairs={{0,8},{1,9},{2,10},{3,11},{4,12},{5,13},{6,14},{7,15},{8,0},{9,1},... | collective-permute-start | bytes 393224 | tf_op jit(solution)/shard_map/ppermute | solution.py:373
  5.2 5.1 %collective-permute-start = (f32[64,512]{1,0:T(8,128)S(1)}, f32[64,512]{1,0:T(8,128)S(1)}, u32[]{:S(2)}, u32[]{:S(2)}) collective-permute-start(f32[64,512]{1,0:T(8,128)S(1)} %get-tuple-element.22.own_ref), channel_id=1, source_target_pairs={{0,1},{1,0},{2,3},{3,2},{4,5},{5,4},{6,7},{7,6},{8,16},{9,17},{10,... | collective-permute-start | bytes 393224 | tf_op jit(solution)/shard_map/ppermute | solution.py:373
  5.2 1.4 %collective-permute-start.2 = (f32[64,121]{1,0:T(8,128)S(1)}, f32[64,121]{1,0:T(8,128)S(1)}, u32[]{:S(2)}, u32[]{:S(2)}) collective-permute-start(f32[64,121]{1,0:T(8,128)S(1)} %get-tuple-element.30), channel_id=1, source_target_pairs={{0,1},{1,0},{2,3},{3,2},{4,5},{5,4},{6,7},{7,6},{8,9},{9,8},{10,11... | collective-permute-start | bytes 92936 | tf_op jit(solution)/shard_map/ppermute | solution.py:344
  6.6 8.4 %collective-permute-start.3 = (f32[32,121]{1,0:T(8,128)S(1)}, f32[32,121]{1,0:T(8,128)S(1)}, u32[]{:S(2)}, u32[]{:S(2)}) collective-permute-start(f32[32,121]{1,0:T(8,128)S(1)} %get-tuple-element.32), channel_id=1, source_target_pairs={{0,2},{1,3},{2,0},{3,1},{4,6},{5,7},{6,4},{7,5},{8,10},{9,11},{10,... | collective-permute-start | bytes 46472 | tf_op jit(solution)/shard_map/ppermute | solution.py:354
  8.1 6.9 %collective-permute-start.4 = (f32[32,121]{1,0:T(8,128)S(1)}, f32[32,121]{1,0:T(8,128)S(1)}, u32[]{:S(2)}, u32[]{:S(2)}) collective-permute-start(f32[32,121]{1,0:T(8,128)S(1)} %get-tuple-element.33), channel_id=1, source_target_pairs={{0,4},{1,5},{2,6},{3,7},{4,0},{5,1},{6,2},{7,3},{8,12},{9,13},{10,... | collective-permute-start | bytes 46472 | tf_op jit(solution)/shard_map/ppermute | solution.py:354
  9.6 5.4 %collective-permute-start.5 = (f32[32,121]{1,0:T(8,128)S(1)}, f32[32,121]{1,0:T(8,128)S(1)}, u32[]{:S(2)}, u32[]{:S(2)}) collective-permute-start(f32[32,121]{1,0:T(8,128)S(1)} %get-tuple-element.34), channel_id=1, source_target_pairs={{0,6},{1,7},{2,4},{3,5},{4,2},{5,3},{6,0},{7,1},{8,14},{9,15},{10,... | collective-permute-start | bytes 46472 | tf_op jit(solution)/shard_map/ppermute | solution.py:354

commit v12 on v11

--- a/solution.py
+++ b/solution.py
@@ -79,7 +79,8 @@
         copy.wait()
 
 
-def join_kernel(out_ref, came_ref, *join_refs, cap):
+def join_kernel(out_ref, came_ref, peak_ref, *join_refs, cap):
+    del peak_ref
     chip = lax.axis_index("grp") // 2
     for m, ref in enumerate(join_refs):
         at = pl.ds(pl.multiple_of((chip ^ m) * cap, cap), cap)
@@ -95,10 +96,16 @@
         rows_ref[pl.ds(pl.multiple_of((peer ^ 1) * cap, cap), cap), :] = ref[cap:, :]
 
 
-def cut_kernel(list_ref, operators_ref, place_ref, parts_ref, wide_ref, *, ops):
+def counts_kernel(
+    list_ref, operators_ref, source_ref, target_ref, operator_ref, place_ref, parts_ref, low_ref, peak_ref,
+    wide_ref, code_ref, weight_ref, acc_ref, a_ref, b_ref, *, ops, sources,
+):
     near, leaves = list_ref.shape
     ncoef = operators_ref.shape[1]
     groups = leaves // LANES
+    half, codes = acc_ref.shape
+    _, block, chunk = a_ref.shape
+    f32 = jnp.float32
     even = lax.axis_index("slab") % 2 == 0
     lane = lax.broadcasted_iota(jnp.int32, (near, LANES), 1)
     for g in range(groups):
@@ -110,25 +117,52 @@
         side = row >> 9
         side = jnp.where(even, 2 - side, side)
         place_ref[g] = (side << 9) + ((row & 7) << 6) + ((row >> 3) & 63)
+
+    leaf, op = target_ref[...], operator_ref[...]
+    upper = leaf >= half
+    code_ref[0] = (op >> 2) * sources + source_ref[...]
+    weight_ref[0] = (1 << (3 * (op & 3))).astype(f32)
+    code_ref[1] = jnp.where(leaf < leaves, jnp.where(upper, leaf - half, leaf), -1)
+    weight_ref[1] = jnp.where(upper, 4096.0, 1.0)
+    marks = Marks(max(block, half))
+    for part in range(target_ref.shape[0] * LANES // chunk):
+        turn = part % 2
+        for c in range(chunk // LANES):
+            at = slice(part * (chunk // LANES) + c, part * (chunk // LANES) + c + 1)
+            marks.put(b_ref.at[turn], c, code_ref[1, at, :], weight_ref[1, at, :])
+        for first in range(0, codes, block):
+            for c in range(chunk // LANES):
+                at = slice(part * (chunk // LANES) + c, part * (chunk // LANES) + c + 1)
+                marks.put(a_ref.at[turn], c, code_ref[0, at, :] - first, weight_ref[0, at, :])
+            product = lax.dot_general(b_ref[turn], a_ref[turn], NT, preferred_element_type=f32)
+            if part == 0:
+                acc_ref[:, first : first + block] = product
+            else:
+                acc_ref[:, first : first + block] += product
+
     wide_ref[...] = pad_lanes(operators_ref[...])
     for op in range(ops):
         matrix = wide_ref[pl.ds(op, ncoef, stride=ops), :]
-        matrix = jnp.concatenate([matrix, jnp.zeros((LANES - ncoef, LANES), jnp.float32)], axis=0)
+        matrix = jnp.concatenate([matrix, jnp.zeros((LANES - ncoef, LANES), f32)], axis=0)
         hi, lo = split(matrix)
         parts_ref[LANES * spot(op, ops) : LANES * (spot(op, ops) + 1), :] = jnp.concatenate([hi, lo], axis=1)
 
+    value = acc_ref[...]
+    peak_ref[...] = jnp.max(value.reshape(-1, 8, codes), axis=0)
+    value = value.astype(jnp.int32)
+    for digit in range(8):
+        h, d = digit // 4, digit % 4
+        here = (value >> (3 * digit)) & 7
+        low_ref[half * h : half * (h + 1), codes * d : codes * (d + 1)] = here.astype(f32).astype(jnp.bfloat16)
+
 
 def spot(op, ops):
     return (op % 4) * (ops // 4) + op // 4
 
 
 class Marks:
-    def __init__(self, rows, chunk):
+    def __init__(self, rows):
         self.iota = lax.broadcasted_iota(jnp.int32, (rows, LANES), 0).astype(jnp.int16).reshape(-1, 16, LANES)
-        self.chunk = chunk
-
-    def columns(self, ref, part, c):
-        return ref[:, pl.ds(pl.multiple_of(part * self.chunk + c * LANES, LANES), LANES)]
 
     def put(self, ref, c, code, weight):
         size = ref.shape[0]
@@ -140,40 +174,18 @@
 
 
 def near_kernel(
-    second_ref, own_ref, first_ref, place_ref, source_ref, target_ref, operator_ref,
-    near_ref, low_ref, peak_ref,
-    packed_ref, charge_ref, picked_ref, pot_ref, acc_ref, a_ref, b_ref, *, sources,
+    first_ref, own_ref, second_ref, place_ref, near_ref, packed_ref, charge_ref, picked_ref, pot_ref
 ):
     groups, near, _ = place_ref.shape
     leaves = own_ref.shape[1]
-    half, codes = acc_ref.shape
-    block, chunk = a_ref.shape
     f32 = jnp.float32
-    marks = Marks(max(block, half), chunk)
-
-    def count(g):
-        for c in range(chunk // LANES):
-            leaf = marks.columns(target_ref, g, c)
-            upper = leaf >= half
-            leaf = jnp.where(leaf < leaves, jnp.where(upper, leaf - half, leaf), -1)
-            marks.put(b_ref, c, leaf, jnp.where(upper, 4096.0, 1.0))
-        for first in range(0, codes, block):
-            for c in range(chunk // LANES):
-                op = marks.columns(operator_ref, g, c)
-                code = (op >> 2) * sources + marks.columns(source_ref, g, c) - first
-                last = op & 3
-                weight = jnp.where(last == 0, 1.0, jnp.where(last == 1, 8.0, jnp.where(last == 2, 64.0, 512.0)))
-                marks.put(a_ref, c, code, weight)
-            acc_ref[:, first : first + block] += lax.dot_general(b_ref[...], a_ref[...], NT, preferred_element_type=f32)
-
-    acc_ref[...] = jnp.zeros_like(acc_ref)
     me = lax.axis_index("slab")
     last = lax.axis_size("slab") - 1
     from_right = me % 2 == 0
     ends = (jnp.logical_and(from_right, me == last), False, jnp.where(from_right, me == 0, me == last))
     for k, (ref, end) in enumerate(zip((first_ref, own_ref, second_ref), ends)):
         x, y, z = (
-            jnp.clip(jnp.floor(ref[PTS * c : PTS * (c + 1), :] * UNITS), -UNITS, UNITS - 1.0).astype(jnp.int32)
+            jnp.minimum(jnp.floor(ref[PTS * c : PTS * (c + 1), :] * UNITS), UNITS - 1.0).astype(jnp.int32)
             for c in range(3)
         )
         at = slice(leaves * k, leaves * (k + 1))
@@ -194,7 +206,6 @@
         return found
 
     def step(g, carry):
-        count(g)
         at = pl.ds(pl.multiple_of(g * LANES, LANES), LANES)
         tx, ty, tz = (own_ref[PTS * c : PTS * (c + 1), at] * SCALE for c in range(3))
         square = tx * tx + ty * ty + (tz * tz + SOFT2 * SCALE * SCALE)
@@ -223,19 +234,11 @@
         pieces += [pot[:, :width], pot[:, width:]]
     near_ref[...] = jnp.concatenate(pieces, axis=0).T
 
-    value = acc_ref[...]
-    peak_ref[...] = jnp.max(value.reshape(-1, 8, codes), axis=0)
-    value = value.astype(jnp.int32)
-    for digit in range(8):
-        h, d = digit // 4, digit % 4
-        here = (value >> (3 * digit)) & 7
-        low_ref[half * h : half * (h + 1), codes * d : codes * (d + 1)] = here.astype(f32).astype(jnp.bfloat16)
-
 
 def far_kernel(
     parts_ref, low_ref, peak_ref, source_ref, target_ref, operator_ref, *refs, ops, cap,
 ):
-    *join_refs, out_ref, received_ref, split_ref, pair_ref, a_ref, b_ref = refs
+    _, *join_refs, out_ref, received_ref, split_ref, pair_ref, a_ref, b_ref = refs
     if cap:
         placed(join_refs, received_ref, cap)
     else:
@@ -262,21 +265,22 @@
     @pl.when(carried)
     def _():
         size, chunk = a_ref.shape
-        marks = Marks(max(size, leaves), chunk)
+        marks = Marks(max(size, leaves))
         out_ref[...] = jnp.zeros_like(out_ref)
         for first in range(0, ops // 2 * sources, size):
             pair_ref[...] = jnp.full(pair_ref.shape, -(2.0**24), f32)
 
             def more(part, carry):
                 for c in range(chunk // LANES):
-                    op = marks.columns(operator_ref, part, c)
-                    code = (op >> 1) * sources + marks.columns(source_ref, part, c) - first
+                    at = pl.ds(part * (chunk // LANES) + c, 1)
+                    op = operator_ref[at, :]
+                    code = (op >> 1) * sources + source_ref[at, :] - first
                     marks.put(a_ref, c, code, jnp.where((op & 1) == 1, 8192.0, 1.0))
-                    marks.put(b_ref, c, marks.columns(target_ref, part, c), jnp.ones((1, LANES), f32))
+                    marks.put(b_ref, c, target_ref[at, :], jnp.ones((1, LANES), f32))
                 pair_ref[...] += lax.dot_general(b_ref[...], a_ref[...], NT, preferred_element_type=f32)
                 return carry
 
-            lax.fori_loop(0, target_ref.shape[1] // chunk, more, 0)
+            lax.fori_loop(0, target_ref.shape[0] * LANES // chunk, more, 0)
             for lane in range(first, first + size, LANES):
                 value = pair_ref[:, lane - first : lane - first + LANES]
                 odd = jnp.floor(value * (1.0 / 8192.0))
@@ -314,9 +318,7 @@
     points = (jnp.transpose(coords.reshape(3, tiles, LANES), (1, 0, 2)), charges.reshape(tiles, LANES))
     others = (
         near_list.T,
-        m2l_source,
-        m2l_target,
-        m2l_operator,
+        *(x.reshape(entries // LANES, LANES) for x in (m2l_source, m2l_target, m2l_operator)),
         jnp.transpose(operators, (1, 0, 2)).reshape(ncoef * ops, ncoef),
     )
     table, same, other, near_list, m2l_source, m2l_target, m2l_operator, operators = pl.pallas_call(
@@ -340,16 +342,41 @@
         ],
         compiler_params=PARAMS,
     )(*(pltpu.with_memory_space_constraint(x, pltpu.HBM) for x in (*points, multipoles, send_list, *others)))
+    codes = ops // 4 * sources
+    block = min(codes, 512)
+    groups = leaves // LANES
+    chunk = entries // 4
+    places, parts, low, peak = pl.pallas_call(
+        functools.partial(counts_kernel, ops=ops, sources=sources),
+        name="counts",
+        out_shape=(
+            jax.ShapeDtypeStruct((groups, near, LANES), jnp.int32),
+            jax.ShapeDtypeStruct((ops * LANES, 2 * LANES), bf16),
+            jax.ShapeDtypeStruct((leaves, ops * sources), bf16),
+            jax.ShapeDtypeStruct((8, codes), f32),
+        ),
+        in_specs=[VMEM] * 5,
+        out_specs=(VMEM,) * 4,
+        scratch_shapes=[
+            pltpu.VMEM((ncoef * ops, LANES), f32),
+            pltpu.VMEM((2, entries // LANES, LANES), jnp.int32),
+            pltpu.VMEM((2, entries // LANES, LANES), f32),
+            pltpu.VMEM((leaves // 2, codes), f32),
+            pltpu.VMEM((2, block, chunk), bf16),
+            pltpu.VMEM((2, leaves // 2, chunk), bf16),
+        ],
+        compiler_params=PARAMS,
+    )(near_list, operators, m2l_source, m2l_target, m2l_operator)
     if cap:
         came = lax.ppermute(other, "grp", [(i, i ^ 1) for i in range(peers)])
         joins = pl.pallas_call(
             functools.partial(join_kernel, cap=cap),
             name="join",
             out_shape=(jax.ShapeDtypeStruct((2 * cap, ncoef), f32),) * (peers // 2),
-            in_specs=[VMEM] * 2,
+            in_specs=[VMEM, VMEM, ANY],
             out_specs=(VMEM,) * (peers // 2),
             compiler_params=PARAMS,
-        )(same, came)
+        )(same, came, peak)
         received = [joins[0]] + [
             lax.ppermute(joins[m], "grp", [(i, i ^ (2 * m)) for i in range(peers)]) for m in range(1, peers // 2)
         ]
@@ -375,49 +402,26 @@
     first = exchange(0)
     second = exchange(1)
 
-    codes = ops // 4 * sources
-    block = min(codes, 512)
-    groups = leaves // LANES
-    chunk = entries // groups
-    places, parts = pl.pallas_call(
-        functools.partial(cut_kernel, ops=ops),
-        name="cut",
-        out_shape=(
-            jax.ShapeDtypeStruct((groups, near, LANES), jnp.int32),
-            jax.ShapeDtypeStruct((ops * LANES, 2 * LANES), bf16),
-        ),
-        in_specs=[VMEM] * 2,
-        out_specs=(VMEM,) * 2,
-        scratch_shapes=[pltpu.VMEM((ncoef * ops, LANES), f32)],
-        compiler_params=PARAMS,
-    )(near_list, operators)
-    near_potential, low, peak = pl.pallas_call(
-        functools.partial(near_kernel, sources=sources),
-        name="near_counts",
-        out_shape=(
-            jax.ShapeDtypeStruct((tiles, LANES), f32),
-            jax.ShapeDtypeStruct((leaves, ops * sources), bf16),
-            jax.ShapeDtypeStruct((8, codes), f32),
-        ),
-        in_specs=[VMEM] * 7,
-        out_specs=(VMEM,) * 3,
+    near_potential = pl.pallas_call(
+        near_kernel,
+        name="near",
+        out_shape=jax.ShapeDtypeStruct((tiles, LANES), f32),
+        in_specs=[VMEM] * 4,
+        out_specs=VMEM,
         scratch_shapes=[
             pltpu.VMEM((2 * PTS, 3 * leaves), jnp.int32),
             pltpu.VMEM((PTS, 3 * leaves), f32),
             pltpu.VMEM((near, 5 * PTS, LANES), f32),
             pltpu.VMEM((groups, PTS, LANES), f32),
-            pltpu.VMEM((leaves // 2, codes), f32),
-            pltpu.VMEM((block, chunk), bf16),
-            pltpu.VMEM((leaves // 2, chunk), bf16),
         ],
         compiler_params=PARAMS,
-    )(second, table, first, places, m2l_source, m2l_target, m2l_operator)
+    )(first, table, second, places)
 
     local_exp = pl.pallas_call(
         functools.partial(far_kernel, ops=ops, cap=cap),
         name="far",
         out_shape=jax.ShapeDtypeStruct((ncoef, leaves), f32),
-        in_specs=[VMEM] * (6 + len(received)),
+        in_specs=[VMEM] * 6 + [ANY] + [VMEM] * len(received),
         out_specs=VMEM,
         scratch_shapes=[
             pltpu.VMEM((sources, ncoef), f32),
@@ -427,7 +431,7 @@
             pltpu.VMEM((leaves, 512), bf16),
         ],
         compiler_params=PARAMS,
-    )(parts, low, peak, m2l_source, m2l_target, m2l_operator, *received)
+    )(parts, low, peak, m2l_source, m2l_target, m2l_operator, near_potential, *received)
     return (local_exp, near_potential.reshape(npoints))
 
 

time: 16.8 us -> 17.6 us (1.048)
  local copies, waits for them, and re-layouts: 0 us -> 0.76 us
  waiting for transfers between devices: 0.9 us -> 0.33 us
  Pallas kernels: 7.96 us -> 8.46 us
    ppermute x1, waiting for transfers between devices: 0.88 us -> 0.01 us  [shards(): came = lax.ppermute(other, 'grp', [(i, i ^ 1) for i in range(peers)])]
    unnamed x0 -> x2, local copies, waits for them, and re-layouts: none -> 0.76 us
    pallas_call x2, Pallas kernels: 4.91 us -> 5.4 us  [the longest x1 3.83 us: shards(): pl.pallas_call(near_kernel, name='near', out_shape=jax.ShapeDtypeStruct((...]
    ppermute x3, waiting for transfers between devices: 0.01 us -> 0.32 us  [shards(): lax.ppermute(joins[m], 'grp', [(i, i ^ 2 * m) for i in range(peers)])]
  transfers between devices with their start and end apart: 6 -> 6, of which waited for: 1 -> 1; matrix products, arithmetic and copies ran while one was open for 0% -> 0% of each run, Pallas kernels for 30% -> 31%
where the time goes in v12:
time: 17.6 us; the launch traced here: 17.4 us
  Pallas kernels  8.46 us (48%)
  starting transfers between devices  7.15 us (41%)
  local copies, waits for them, and re-layouts  0.76 us (4%)
  between operations  0.67 us (4%)
  waiting for transfers between devices  0.33 us (2%)
    pallas_call x1, Pallas kernels, shards(): pl.pallas_call(near_kernel, name='near', out_shape=jax.ShapeDtypeStruct((...  3.83 us
    ppermute x3, starting transfers between devices, shards(): lax.ppermute(joins[m], 'grp', [(i, i ^ 2 * m) for i in range(peers)])  3.55 us
    ppermute x2, starting transfers between devices, exchange(): return lax.ppermute(table, ('slab', 'grp'), sorted(to.items()))  3.09 us
    pallas_call x1, Pallas kernels, shards(): pl.pallas_call(functools.partial(far_kernel, ops=ops, cap=cap), name='far...  1.58 us
    pallas_call x1, Pallas kernels, shards(): pl.pallas_call(functools.partial(counts_kernel, ops=ops, sources=sources)...  1.57 us
    pallas_call x1, Pallas kernels, shards(): pl.pallas_call(functools.partial(prep_kernel, others=len(others), cap=cap...  1.46 us
    unnamed x2, local copies, waits for them, and re-layouts  0.76 us
    ppermute x1, starting transfers between devices, shards(): came = lax.ppermute(other, 'grp', [(i, i ^ 1) for i in range(peers)])  0.51 us
  transfers between devices with their start and end apart: 6, of which 1 were waited for; matrix products, arithmetic and copies ran while one was open for 0% of the time, Pallas kernels for 31%

profile of v12, /device:TPU:0, one launch (start us, length us, event | category | flops | bytes accessed | tf_op | source)
XLA Modules:
  0.0 17.4 jit_solution(17287221534941249230)
XLA Ops:
  0.6 1.5 %prep.1 = (f32[64,512]{1,0:T(8,128)S(1)}, f32[64,121]{1,0:T(8,128)S(1)}, f32[64,121]{1,0:T(8,128)S(1)}, s32[8,512]{1,0:T(8,128)S(1)}, s32[32,128]{1,0:T(8,128)S(...) custom-call(f32[64,3,128]{2,1,0:T(4,128)} %bitcast.14, f32[64,128]{1,0:T(8,128)} %bitcast.15, ...), custom_call_target="tpu_custom_call" | custom-call | tf_op jit(solution)/shard_map/prep/pallas_call | solution.py:324
  2.1 3.1 %collective-permute-start = (f32[64,512]{1,0:T(8,128)S(1)}, f32[64,512]{1,0:T(8,128)S(1)}, u32[]{:S(2)}, u32[]{:S(2)}) collective-permute-start(f32[64,512]{1,0:T(8,128)S(1)} %get-tuple-element.26.own_ref), channel_id=1, source_target_pairs={{0,8},{1,9},{2,10},{3,11},{4,12},{5,13},{6,14},{7,15},{8,0},{9,1},... | collective-permute-start | bytes 393224 | tf_op jit(solution)/shard_map/ppermute | solution.py:400
  5.2 0.0 collective-permute-start.1
  5.2 0.5 %collective-permute-start.2 = (f32[64,121]{1,0:T(8,128)S(1)}, f32[64,121]{1,0:T(8,128)S(1)}, u32[]{:S(2)}, u32[]{:S(2)}) collective-permute-start(f32[64,121]{1,0:T(8,128)S(1)} %get-tuple-element.29), channel_id=1, source_target_pairs={{0,1},{1,0},{2,3},{3,2},{4,5},{5,4},{6,7},{7,6},{8,9},{9,8},{10,11... | collective-permute-start | bytes 92936 | tf_op jit(solution)/shard_map/ppermute | solution.py:371
  5.7 1.6 %counts.1 = (s32[4,8,128]{2,1,0:T(8,128)S(1)}, bf16[1024,256]{1,0:T(8,128)(2,1)S(1)}, bf16[512,1024]{1,0:T(8,128)(2,1)S(1)}, f32[8,256]{1,0:T(8,128)S(1)}) custom-call(s32[8,512]{1,0:T(8,128)S(1)} %get-tuple-element.18.list_ref, f32[968,121]{1,0:T(8,128)S(1)} %get-tuple-element.19.operators_ref, s32[32,128]{1,0:T(8,128)S(1)} %get-tuple-element.20.source_ref, ...), custom_call_target="tpu_custom_call" | custom-call | tf_op jit(solution)/shard_map/counts/pallas_call | solution.py:349
  7.3 0.0 collective-permute-done.2.came_ref
  7.3 1.6 %collective-permute-start.3 = (f32[32,121]{1,0:T(8,128)S(1)}, f32[32,121]{1,0:T(8,128)S(1)}, u32[]{:S(2)}, u32[]{:S(2)}) collective-permute-start(f32[32,121]{1,0:T(8,128)S(1)} %get-tuple-element.31), channel_id=1, source_target_pairs={{0,2},{1,3},{2,0},{3,1},{4,6},{5,7},{6,4},{7,5},{8,10},{9,11},{10,... | collective-permute-start | bytes 46472 | tf_op jit(solution)/shard_map/ppermute | solution.py:381
  8.9 1.5 %collective-permute-start.4 = (f32[32,121]{1,0:T(8,128)S(1)}, f32[32,121]{1,0:T(8,128)S(1)}, u32[]{:S(2)}, u32[]{:S(2)}) collective-permute-start(f32[32,121]{1,0:T(8,128)S(1)} %get-tuple-element.32), channel_id=1, source_target_pairs={{0,4},{1,5},{2,6},{3,7},{4,0},{5,1},{6,2},{7,3},{8,12},{9,13},{10,... | collective-permute-start | bytes 46472 | tf_op jit(solution)/shard_map/ppermute | solution.py:381
  10.4 0.5 %collective-permute-start.5 = (f32[32,121]{1,0:T(8,128)S(1)}, f32[32,121]{1,0:T(8,128)S(1)}, u32[]{:S(2)}, u32[]{:S(2)}) collective-permute-start(f32[32,121]{1,0:T(8,128)S(1)} %get-tuple-element.33), channel_id=1, source_target_pairs={{0,6},{1,7},{2,4},{3,5},{4,2},{5,3},{6,0},{7,1},{8,14},{9,15},{10,... | collective-permute-start | bytes 46472 | tf_op jit(solution)/shard_map/ppermute | solution.py:381
  10.9 0.0 collective-permute-done.first_ref
  10.9 0.0 collective-permute-done.1.second_ref
  10.9 3.8 %near.1.refs_0_ = f32[64,128]{1,0:T(8,128)} custom-call(f32[64,512]{1,0:T(8,128)S(1)} %collective-permute-done.first_ref, f32[64,512]{1,0:T(8,128)S(1)} %get-tuple-element.26.own_ref, f32[64,512]{1,0:T(8,128)S(1)} %collective-permute-done.1.second_ref, s32[4,8,128]{2,1,0:T(8,128)S(1)} %get-tuple-element.27.place_ref), custom_call_target="tpu_custom_call" | custom-call | tf_op jit(solution)/shard_map/near/pallas_call | solution.py:405
  14.7 0.0 collective-permute-done.3.refs_2_
  14.7 0.0 collective-permute-done.4.refs_3_
  14.7 0.3 %collective-permute-done.5.refs_4_ = f32[32,121]{1,0:T(8,128)S(1)} collective-permute-done((f32[32,121]{1,0:T(8,128)S(1)}, f32[32,121]{1,0:T(8,128)S(1)}, u32[]{:S(2)}, u32[]{:S(2)}) %collective-permute-start.5) | collective-permute-done | bytes 15520 | tf_op jit(solution)/shard_map/ppermute | solution.py:381
  15.0 0.0 copy-start
  15.0 0.8 %copy-done = f32[64,128]{1,0:T(8,128)S(1)} copy-done((f32[64,128]{1,0:T(8,128)S(1)}, f32[64,128]{1,0:T(8,128)}, u32[]{:S(2)}) %copy-start) | copy-done | bytes 32792
  15.8 1.6 %far.1 = f32[121,512]{1,0:T(8,128)} custom-call(bf16[1024,256]{1,0:T(8,128)(2,1)S(1)} %get-tuple-element.23.parts_ref, bf16[512,1024]{1,0:T(8,128)(2,1)S(1)} %get-tuple-element.24.low_ref, f32[8,256]{1,0:T(8,128)S(1)} %get-tuple-element.25.peak_ref, s32[32,128]{1,0:T(8,128)S(1)} %get-tuple-element.20.source_ref, s32[32,128]{1,0:T(8,128)S(1)} %get-tuple-element.21.target_ref, ...), custom_call_target="tpu_custom_call" | custom-call | tf_op jit(solution)/shard_map/far/pallas_call | solution.py:420
  (1 shorter events, 0.0 us)
Async XLA Ops:
  2.1 8.8 %collective-permute-start = (f32[64,512]{1,0:T(8,128)S(1)}, f32[64,512]{1,0:T(8,128)S(1)}, u32[]{:S(2)}, u32[]{:S(2)}) collective-permute-start(f32[64,512]{1,0:T(8,128)S(1)} %get-tuple-element.26.own_ref), channel_id=1, source_target_pairs={{0,8},{1,9},{2,10},{3,11},{4,12},{5,13},{6,14},{7,15},{8,0},{9,1},... | collective-permute-start | bytes 393224 | tf_op jit(solution)/shard_map/ppermute | solution.py:400
  5.2 5.7 %collective-permute-start.1 = (f32[64,512]{1,0:T(8,128)S(1)}, f32[64,512]{1,0:T(8,128)S(1)}, u32[]{:S(2)}, u32[]{:S(2)}) collective-permute-start(f32[64,512]{1,0:T(8,128)S(1)} %get-tuple-element.26.own_ref), channel_id=1, source_target_pairs={{0,1},{1,0},{2,3},{3,2},{4,5},{5,4},{6,7},{7,6},{8,16},{9,17},{10,... | collective-permute-start | bytes 393224 | tf_op jit(solution)/shard_map/ppermute | solution.py:400
  5.2 2.1 %collective-permute-start.2 = (f32[64,121]{1,0:T(8,128)S(1)}, f32[64,121]{1,0:T(8,128)S(1)}, u32[]{:S(2)}, u32[]{:S(2)}) collective-permute-start(f32[64,121]{1,0:T(8,128)S(1)} %get-tuple-element.29), channel_id=1, source_target_pairs={{0,1},{1,0},{2,3},{3,2},{4,5},{5,4},{6,7},{7,6},{8,9},{9,8},{10,11... | collective-permute-start | bytes 92936 | tf_op jit(solution)/shard_map/ppermute | solution.py:371
  7.3 7.4 %collective-permute-start.3 = (f32[32,121]{1,0:T(8,128)S(1)}, f32[32,121]{1,0:T(8,128)S(1)}, u32[]{:S(2)}, u32[]{:S(2)}) collective-permute-start(f32[32,121]{1,0:T(8,128)S(1)} %get-tuple-element.31), channel_id=1, source_target_pairs={{0,2},{1,3},{2,0},{3,1},{4,6},{5,7},{6,4},{7,5},{8,10},{9,11},{10,... | collective-permute-start | bytes 46472 | tf_op jit(solution)/shard_map/ppermute | solution.py:381
  8.9 5.8 %collective-permute-start.4 = (f32[32,121]{1,0:T(8,128)S(1)}, f32[32,121]{1,0:T(8,128)S(1)}, u32[]{:S(2)}, u32[]{:S(2)}) collective-permute-start(f32[32,121]{1,0:T(8,128)S(1)} %get-tuple-element.32), channel_id=1, source_target_pairs={{0,4},{1,5},{2,6},{3,7},{4,0},{5,1},{6,2},{7,3},{8,12},{9,13},{10,... | collective-permute-start | bytes 46472 | tf_op jit(solution)/shard_map/ppermute | solution.py:381
  10.4 4.6 %collective-permute-start.5 = (f32[32,121]{1,0:T(8,128)S(1)}, f32[32,121]{1,0:T(8,128)S(1)}, u32[]{:S(2)}, u32[]{:S(2)}) collective-permute-start(f32[32,121]{1,0:T(8,128)S(1)} %get-tuple-element.33), channel_id=1, source_target_pairs={{0,6},{1,7},{2,4},{3,5},{4,2},{5,3},{6,0},{7,1},{8,14},{9,15},{10,... | collective-permute-start | bytes 46472 | tf_op jit(solution)/shard_map/ppermute | solution.py:381
  15.0 0.8 %copy-start = (f32[64,128]{1,0:T(8,128)S(1)}, f32[64,128]{1,0:T(8,128)}, u32[]{:S(2)}) copy-start(f32[64,128]{1,0:T(8,128)} %near.1.refs_0_) | copy-start | bytes 98308

commit v13 on v12

--- a/solution.py
+++ b/solution.py
@@ -79,8 +79,8 @@
         copy.wait()
 
 
-def join_kernel(out_ref, came_ref, peak_ref, *join_refs, cap):
-    del peak_ref
+def join_kernel(out_ref, came_ref, digits_ref, *join_refs, cap):
+    del digits_ref
     chip = lax.axis_index("grp") // 2
     for m, ref in enumerate(join_refs):
         at = pl.ds(pl.multiple_of((chip ^ m) * cap, cap), cap)
@@ -97,8 +97,8 @@
 
 
 def counts_kernel(
-    list_ref, operators_ref, source_ref, target_ref, operator_ref, place_ref, parts_ref, low_ref, peak_ref,
-    wide_ref, code_ref, weight_ref, acc_ref, a_ref, b_ref, *, ops, sources,
+    list_ref, operators_ref, source_ref, target_ref, operator_ref, place_ref, parts_ref, acc_ref,
+    wide_ref, code_ref, weight_ref, a_ref, b_ref, *, ops, sources,
 ):
     near, leaves = list_ref.shape
     ncoef = operators_ref.shape[1]
@@ -147,6 +147,32 @@
         hi, lo = split(matrix)
         parts_ref[LANES * spot(op, ops) : LANES * (spot(op, ops) + 1), :] = jnp.concatenate([hi, lo], axis=1)
 
+
+def spot(op, ops):
+    return (op % 4) * (ops // 4) + op // 4
+
+
+class Marks:
+    def __init__(self, rows):
+        self.iota = lax.broadcasted_iota(jnp.int32, (rows, LANES), 0).astype(jnp.int16).reshape(-1, 16, LANES)
+
+    def put(self, ref, c, code, weight):
+        size = ref.shape[0]
+        code, weight = (
+            jnp.broadcast_to(x, (16, LANES)).astype(t)[None] for x, t in ((code, jnp.int16), (weight, jnp.bfloat16))
+        )
+        marks = jnp.where(self.iota[: size // 16] == code, weight, jnp.zeros((1, 16, LANES), jnp.bfloat16))
+        ref[:, LANES * c : LANES * (c + 1)] = marks.reshape(size, LANES)
+
+
+def near_kernel(
+    second_ref, own_ref, first_ref, place_ref, acc_ref, near_ref, low_ref, peak_ref,
+    packed_ref, charge_ref, picked_ref, pot_ref,
+):
+    groups, near, _ = place_ref.shape
+    leaves = own_ref.shape[1]
+    half, codes = acc_ref.shape
+    f32 = jnp.float32
     value = acc_ref[...]
     peak_ref[...] = jnp.max(value.reshape(-1, 8, codes), axis=0)
     value = value.astype(jnp.int32)
@@ -155,30 +181,6 @@
         here = (value >> (3 * digit)) & 7
         low_ref[half * h : half * (h + 1), codes * d : codes * (d + 1)] = here.astype(f32).astype(jnp.bfloat16)
 
-
-def spot(op, ops):
-    return (op % 4) * (ops // 4) + op // 4
-
-
-class Marks:
-    def __init__(self, rows):
-        self.iota = lax.broadcasted_iota(jnp.int32, (rows, LANES), 0).astype(jnp.int16).reshape(-1, 16, LANES)
-
-    def put(self, ref, c, code, weight):
-        size = ref.shape[0]
-        code, weight = (
-            jnp.broadcast_to(x, (16, LANES)).astype(t)[None] for x, t in ((code, jnp.int16), (weight, jnp.bfloat16))
-        )
-        marks = jnp.where(self.iota[: size // 16] == code, weight, jnp.zeros((1, 16, LANES), jnp.bfloat16))
-        ref[:, LANES * c : LANES * (c + 1)] = marks.reshape(size, LANES)
-
-
-def near_kernel(
-    first_ref, own_ref, second_ref, place_ref, near_ref, packed_ref, charge_ref, picked_ref, pot_ref
-):
-    groups, near, _ = place_ref.shape
-    leaves = own_ref.shape[1]
-    f32 = jnp.float32
     me = lax.axis_index("slab")
     last = lax.axis_size("slab") - 1
     from_right = me % 2 == 0
@@ -238,7 +240,7 @@
 def far_kernel(
     parts_ref, low_ref, peak_ref, source_ref, target_ref, operator_ref, *refs, ops, cap,
 ):
-    _, *join_refs, out_ref, received_ref, split_ref, pair_ref, a_ref, b_ref = refs
+    *join_refs, out_hbm, out_ref, received_ref, split_ref, pair_ref, a_ref, b_ref, sem = refs
     if cap:
         placed(join_refs, received_ref, cap)
     else:
@@ -257,10 +259,13 @@
         split_ref[LANES:, sources * k : sources * (k + 1)] = lo
     both = lax.dot_general(split_ref[...], low_ref[...], NT, preferred_element_type=f32)
     out_ref[...] = both[:ncoef, :] + both[LANES : LANES + ncoef, :]
+    result = pltpu.make_async_copy(out_ref, out_hbm, sem)
+    result.start()
 
     used = jnp.sum(jnp.where(target_ref[...] < leaves, 1.0, 0.0))
     total = jnp.sum(both[LANES - 1 : LANES, :])
     carried = jnp.logical_or(total != used, jnp.max(peak_ref[...]) >= 2.0**24)
+    result.wait()
 
     @pl.when(carried)
     def _():
@@ -291,6 +296,9 @@
                     out_ref[...] += lax.dot_general(
                         rows, count, NT, precision=lax.Precision.HIGHEST, preferred_element_type=f32
                     )
+        again = pltpu.make_async_copy(out_ref, out_hbm, sem)
+        again.start()
+        again.wait()
 
 
 def shards(
@@ -346,22 +354,20 @@
     block = min(codes, 512)
     groups = leaves // LANES
     chunk = entries // 4
-    places, parts, low, peak = pl.pallas_call(
+    places, parts, digits = pl.pallas_call(
         functools.partial(counts_kernel, ops=ops, sources=sources),
         name="counts",
         out_shape=(
             jax.ShapeDtypeStruct((groups, near, LANES), jnp.int32),
             jax.ShapeDtypeStruct((ops * LANES, 2 * LANES), bf16),
-            jax.ShapeDtypeStruct((leaves, ops * sources), bf16),
-            jax.ShapeDtypeStruct((8, codes), f32),
+            jax.ShapeDtypeStruct((leaves // 2, codes), f32),
         ),
         in_specs=[VMEM] * 5,
-        out_specs=(VMEM,) * 4,
+        out_specs=(VMEM,) * 3,
         scratch_shapes=[
             pltpu.VMEM((ncoef * ops, LANES), f32),
             pltpu.VMEM((2, entries // LANES, LANES), jnp.int32),
             pltpu.VMEM((2, entries // LANES, LANES), f32),
-            pltpu.VMEM((leaves // 2, codes), f32),
             pltpu.VMEM((2, block, chunk), bf16),
             pltpu.VMEM((2, leaves // 2, chunk), bf16),
         ],
@@ -376,7 +382,7 @@
             in_specs=[VMEM, VMEM, ANY],
             out_specs=(VMEM,) * (peers // 2),
             compiler_params=PARAMS,
-        )(same, came, peak)
+        )(same, came, digits)
         received = [joins[0]] + [
             lax.ppermute(joins[m], "grp", [(i, i ^ (2 * m)) for i in range(peers)]) for m in range(1, peers // 2)
         ]
@@ -402,12 +408,16 @@
     first = exchange(0)
     second = exchange(1)
 
-    near_potential = pl.pallas_call(
+    near_potential, low, peak = pl.pallas_call(
         near_kernel,
         name="near",
-        out_shape=jax.ShapeDtypeStruct((tiles, LANES), f32),
-        in_specs=[VMEM] * 4,
-        out_specs=VMEM,
+        out_shape=(
+            jax.ShapeDtypeStruct((tiles, LANES), f32),
+            jax.ShapeDtypeStruct((leaves, ops * sources), bf16),
+            jax.ShapeDtypeStruct((8, codes), f32),
+        ),
+        in_specs=[VMEM] * 5,
+        out_specs=(VMEM,) * 3,
         scratch_shapes=[
             pltpu.VMEM((2 * PTS, 3 * leaves), jnp.int32),
             pltpu.VMEM((PTS, 3 * leaves), f32),
@@ -415,23 +425,25 @@
             pltpu.VMEM((groups, PTS, LANES), f32),
         ],
         compiler_params=PARAMS,
-    )(first, table, second, places)
+    )(second, table, first, places, digits)
 
     local_exp = pl.pallas_call(
         functools.partial(far_kernel, ops=ops, cap=cap),
         name="far",
         out_shape=jax.ShapeDtypeStruct((ncoef, leaves), f32),
-        in_specs=[VMEM] * 6 + [ANY] + [VMEM] * len(received),
-        out_specs=VMEM,
+        in_specs=[VMEM] * (6 + len(received)),
+        out_specs=ANY,
         scratch_shapes=[
+            pltpu.VMEM((ncoef, leaves), f32),
             pltpu.VMEM((sources, ncoef), f32),
             pltpu.VMEM((2 * LANES, ops * sources), bf16),
             pltpu.VMEM((leaves, 512), f32),
             pltpu.VMEM((512, 512), bf16),
             pltpu.VMEM((leaves, 512), bf16),
+            pltpu.SemaphoreType.DMA,
         ],
         compiler_params=PARAMS,
-    )(parts, low, peak, m2l_source, m2l_target, m2l_operator, near_potential, *received)
+    )(parts, low, peak, m2l_source, m2l_target, m2l_operator, *received)
     return (local_exp, near_potential.reshape(npoints))
 
 

time: 17.6 us -> 16.4 us (0.932)
  local copies, waits for them, and re-layouts: 0.76 us -> 0 us
  waiting for transfers between devices: 0.33 us -> 0.07 us
    unnamed x2 -> x0, local copies, waits for them, and re-layouts: 0.76 us -> none
    pallas_call x1, Pallas kernels: 1.57 us -> 1.29 us  [shards(): pl.pallas_call(functools.partial(counts_kernel, ops=ops, sources=sources)...]
    pallas_call x1, Pallas kernels: 3.83 us -> 4.09 us  [shards(): pl.pallas_call(near_kernel, name='near', out_shape=(jax.ShapeDtypeStruct(...]
    ppermute x3, waiting for transfers between devices: 0.32 us -> 0.07 us  [shards(): lax.ppermute(joins[m], 'grp', [(i, i ^ 2 * m) for i in range(peers)])]
  transfers between devices with their start and end apart: 6 -> 6, of which waited for: 1 -> 1; matrix products, arithmetic and copies ran while one was open for 0% -> 0% of each run, Pallas kernels for 31% -> 33%
where the time goes in v13:
time: 16.4 us; the launch traced here: 16.2 us
  Pallas kernels  8.35 us (51%)
  starting transfers between devices  7.15 us (44%)
  between operations  0.67 us (4%)
    pallas_call x1, Pallas kernels, shards(): pl.pallas_call(near_kernel, name='near', out_shape=(jax.ShapeDtypeStruct(...  4.09 us
    ppermute x3, starting transfers between devices, shards(): lax.ppermute(joins[m], 'grp', [(i, i ^ 2 * m) for i in range(peers)])  3.55 us
    ppermute x2, starting transfers between devices, exchange(): return lax.ppermute(table, ('slab', 'grp'), sorted(to.items()))  3.09 us
    pallas_call x1, Pallas kernels, shards(): pl.pallas_call(functools.partial(far_kernel, ops=ops, cap=cap), name='far...  1.5 us
    pallas_call x1, Pallas kernels, shards(): pl.pallas_call(functools.partial(prep_kernel, others=len(others), cap=cap...  1.46 us
    pallas_call x1, Pallas kernels, shards(): pl.pallas_call(functools.partial(counts_kernel, ops=ops, sources=sources)...  1.29 us
    ppermute x1, starting transfers between devices, shards(): came = lax.ppermute(other, 'grp', [(i, i ^ 1) for i in range(peers)])  0.51 us
  transfers between devices with their start and end apart: 6, of which 1 were waited for; matrix products, arithmetic and copies ran while one was open for 0% of the time, Pallas kernels for 33%

profile of v13, /device:TPU:0, one launch (start us, length us, event | category | flops | bytes accessed | tf_op | source)
XLA Modules:
  0.0 16.2 jit_solution(16277331227000727869)
XLA Ops:
  0.6 1.5 %prep.1 = (f32[64,512]{1,0:T(8,128)S(1)}, f32[64,121]{1,0:T(8,128)S(1)}, f32[64,121]{1,0:T(8,128)S(1)}, s32[8,512]{1,0:T(8,128)S(1)}, s32[32,128]{1,0:T(8,128)S(...) custom-call(f32[64,3,128]{2,1,0:T(4,128)} %bitcast.13, f32[64,128]{1,0:T(8,128)} %bitcast.14, ...), custom_call_target="tpu_custom_call" | custom-call | tf_op jit(solution)/shard_map/prep/pallas_call | solution.py:332
  2.1 3.1 %collective-permute-start.1 = (f32[64,512]{1,0:T(8,128)S(1)}, f32[64,512]{1,0:T(8,128)S(1)}, u32[]{:S(2)}, u32[]{:S(2)}) collective-permute-start(f32[64,512]{1,0:T(8,128)S(1)} %get-tuple-element.26.own_ref), channel_id=1, source_target_pairs={{0,8},{1,9},{2,10},{3,11},{4,12},{5,13},{6,14},{7,15},{8,0},{9,1},... | collective-permute-start | bytes 393224 | tf_op jit(solution)/shard_map/ppermute | solution.py:406
  5.2 0.0 collective-permute-start
  5.2 0.5 %collective-permute-start.2 = (f32[64,121]{1,0:T(8,128)S(1)}, f32[64,121]{1,0:T(8,128)S(1)}, u32[]{:S(2)}, u32[]{:S(2)}) collective-permute-start(f32[64,121]{1,0:T(8,128)S(1)} %get-tuple-element.32), channel_id=1, source_target_pairs={{0,1},{1,0},{2,3},{3,2},{4,5},{5,4},{6,7},{7,6},{8,9},{9,8},{10,11... | collective-permute-start | bytes 92936 | tf_op jit(solution)/shard_map/ppermute | solution.py:377
  5.7 1.3 %counts.1 = (s32[4,8,128]{2,1,0:T(8,128)S(1)}, bf16[1024,256]{1,0:T(8,128)(2,1)S(1)}, f32[256,256]{1,0:T(8,128)S(1)}) custom-call(s32[8,512]{1,0:T(8,128)S(1)} %get-tuple-element.20.list_ref, f32[968,121]{1,0:T(8,128)S(1)} %get-tuple-element.21.operators_ref, s32[32,128]{1,0:T(8,128)S(1)} %get-tuple-element.22.source_ref, ...), custom_call_target="tpu_custom_call" | custom-call | tf_op jit(solution)/shard_map/counts/pallas_call | solution.py:357
  7.0 0.0 collective-permute-done.2.came_ref
  7.0 1.6 %collective-permute-start.3 = (f32[32,121]{1,0:T(8,128)S(1)}, f32[32,121]{1,0:T(8,128)S(1)}, u32[]{:S(2)}, u32[]{:S(2)}) collective-permute-start(f32[32,121]{1,0:T(8,128)S(1)} %get-tuple-element.34), channel_id=1, source_target_pairs={{0,2},{1,3},{2,0},{3,1},{4,6},{5,7},{6,4},{7,5},{8,10},{9,11},{10,... | collective-permute-start | bytes 46472 | tf_op jit(solution)/shard_map/ppermute | solution.py:387
  8.6 1.5 %collective-permute-start.4 = (f32[32,121]{1,0:T(8,128)S(1)}, f32[32,121]{1,0:T(8,128)S(1)}, u32[]{:S(2)}, u32[]{:S(2)}) collective-permute-start(f32[32,121]{1,0:T(8,128)S(1)} %get-tuple-element.35), channel_id=1, source_target_pairs={{0,4},{1,5},{2,6},{3,7},{4,0},{5,1},{6,2},{7,3},{8,12},{9,13},{10,... | collective-permute-start | bytes 46472 | tf_op jit(solution)/shard_map/ppermute | solution.py:387
  10.1 0.5 %collective-permute-start.5 = (f32[32,121]{1,0:T(8,128)S(1)}, f32[32,121]{1,0:T(8,128)S(1)}, u32[]{:S(2)}, u32[]{:S(2)}) collective-permute-start(f32[32,121]{1,0:T(8,128)S(1)} %get-tuple-element.36), channel_id=1, source_target_pairs={{0,6},{1,7},{2,4},{3,5},{4,2},{5,3},{6,0},{7,1},{8,14},{9,15},{10,... | collective-permute-start | bytes 46472 | tf_op jit(solution)/shard_map/ppermute | solution.py:387
  10.6 0.0 collective-permute-done.1.first_ref
  10.6 0.0 collective-permute-done.second_ref
  10.6 4.1 %near.1 = (f32[64,128]{1,0:T(8,128)}, bf16[512,1024]{1,0:T(8,128)(2,1)S(1)}, f32[8,256]{1,0:T(8,128)S(1)}) custom-call(f32[64,512]{1,0:T(8,128)S(1)} %collective-permute-done.second_ref, f32[64,512]{1,0:T(8,128)S(1)} %get-tuple-element.26.own_ref, f32[64,512]{1,0:T(8,128)S(1)} %collective-permute-done.1.first_ref, ...), custom_call_target="tpu_custom_call" | custom-call | tf_op jit(solution)/shard_map/near/pallas_call | solution.py:411
  14.7 0.0 collective-permute-done.3.refs_1_
  14.7 0.0 collective-permute-done.4.refs_2_
  14.7 0.1 collective-permute-done.5.refs_3_
  14.8 1.5 %far.1 = f32[121,512]{1,0:T(8,128)} custom-call(bf16[1024,256]{1,0:T(8,128)(2,1)S(1)} %get-tuple-element.25.parts_ref, bf16[512,1024]{1,0:T(8,128)(2,1)S(1)} %get-tuple-element.29.low_ref, f32[8,256]{1,0:T(8,128)S(1)} %get-tuple-element.30.peak_ref, s32[32,128]{1,0:T(8,128)S(1)} %get-tuple-element.22.source_ref, s32[32,128]{1,0:T(8,128)S(1)} %get-tuple-element.23.target_ref, ...), custom_call_target="tpu_custom_call" | custom-call | tf_op jit(solution)/shard_map/far/pallas_call | solution.py:430
  (1 shorter events, 0.0 us)
Async XLA Ops:
  2.1 8.5 %collective-permute-start.1 = (f32[64,512]{1,0:T(8,128)S(1)}, f32[64,512]{1,0:T(8,128)S(1)}, u32[]{:S(2)}, u32[]{:S(2)}) collective-permute-start(f32[64,512]{1,0:T(8,128)S(1)} %get-tuple-element.26.own_ref), channel_id=1, source_target_pairs={{0,8},{1,9},{2,10},{3,11},{4,12},{5,13},{6,14},{7,15},{8,0},{9,1},... | collective-permute-start | bytes 393224 | tf_op jit(solution)/shard_map/ppermute | solution.py:406
  5.2 5.4 %collective-permute-start = (f32[64,512]{1,0:T(8,128)S(1)}, f32[64,512]{1,0:T(8,128)S(1)}, u32[]{:S(2)}, u32[]{:S(2)}) collective-permute-start(f32[64,512]{1,0:T(8,128)S(1)} %get-tuple-element.26.own_ref), channel_id=1, source_target_pairs={{0,1},{1,0},{2,3},{3,2},{4,5},{5,4},{6,7},{7,6},{8,16},{9,17},{10,... | collective-permute-start | bytes 393224 | tf_op jit(solution)/shard_map/ppermute | solution.py:406
  5.2 1.8 %collective-permute-start.2 = (f32[64,121]{1,0:T(8,128)S(1)}, f32[64,121]{1,0:T(8,128)S(1)}, u32[]{:S(2)}, u32[]{:S(2)}) collective-permute-start(f32[64,121]{1,0:T(8,128)S(1)} %get-tuple-element.32), channel_id=1, source_target_pairs={{0,1},{1,0},{2,3},{3,2},{4,5},{5,4},{6,7},{7,6},{8,9},{9,8},{10,11... | collective-permute-start | bytes 92936 | tf_op jit(solution)/shard_map/ppermute | solution.py:377
  7.0 7.7 %collective-permute-start.3 = (f32[32,121]{1,0:T(8,128)S(1)}, f32[32,121]{1,0:T(8,128)S(1)}, u32[]{:S(2)}, u32[]{:S(2)}) collective-permute-start(f32[32,121]{1,0:T(8,128)S(1)} %get-tuple-element.34), channel_id=1, source_target_pairs={{0,2},{1,3},{2,0},{3,1},{4,6},{5,7},{6,4},{7,5},{8,10},{9,11},{10,... | collective-permute-start | bytes 46472 | tf_op jit(solution)/shard_map/ppermute | solution.py:387
  8.6 6.1 %collective-permute-start.4 = (f32[32,121]{1,0:T(8,128)S(1)}, f32[32,121]{1,0:T(8,128)S(1)}, u32[]{:S(2)}, u32[]{:S(2)}) collective-permute-start(f32[32,121]{1,0:T(8,128)S(1)} %get-tuple-element.35), channel_id=1, source_target_pairs={{0,4},{1,5},{2,6},{3,7},{4,0},{5,1},{6,2},{7,3},{8,12},{9,13},{10,... | collective-permute-start | bytes 46472 | tf_op jit(solution)/shard_map/ppermute | solution.py:387
  10.1 4.6 %collective-permute-start.5 = (f32[32,121]{1,0:T(8,128)S(1)}, f32[32,121]{1,0:T(8,128)S(1)}, u32[]{:S(2)}, u32[]{:S(2)}) collective-permute-start(f32[32,121]{1,0:T(8,128)S(1)} %get-tuple-element.36), channel_id=1, source_target_pairs={{0,6},{1,7},{2,4},{3,5},{4,2},{5,3},{6,0},{7,1},{8,14},{9,15},{10,... | collective-permute-start | bytes 46472 | tf_op jit(solution)/shard_map/ppermute | solution.py:387

commit v14 on v13

--- a/solution.py
+++ b/solution.py
@@ -9,6 +9,7 @@
 
 SOFT2 = 0.0625
 LANES = 128
+CHIPS = (0, 3, 1, 2)
 PTS = 16
 UNITS = 2.0**20
 SCALE = 2.0**31
@@ -90,7 +91,7 @@
 
 def placed(join_refs, rows_ref, cap):
     me = lax.axis_index("grp")
-    for m, ref in enumerate(join_refs):
+    for m, ref in zip(CHIPS, join_refs):
         peer = me ^ (2 * m)
         rows_ref[pl.ds(pl.multiple_of(peer * cap, cap), cap), :] = ref[:cap, :]
         rows_ref[pl.ds(pl.multiple_of((peer ^ 1) * cap, cap), cap), :] = ref[cap:, :]
@@ -240,7 +241,7 @@
 def far_kernel(
     parts_ref, low_ref, peak_ref, source_ref, target_ref, operator_ref, *refs, ops, cap,
 ):
-    *join_refs, out_hbm, out_ref, received_ref, split_ref, pair_ref, a_ref, b_ref, sem = refs
+    *join_refs, out_hbm, out_ref, received_ref, split_ref, pair_ref, a_ref, b_ref, sems = refs
     if cap:
         placed(join_refs, received_ref, cap)
     else:
@@ -257,15 +258,20 @@
         hi, lo = split(table[LANES * k : LANES * (k + 1), :] + ones)
         split_ref[:LANES, sources * k : sources * (k + 1)] = hi
         split_ref[LANES:, sources * k : sources * (k + 1)] = lo
-    both = lax.dot_general(split_ref[...], low_ref[...], NT, preferred_element_type=f32)
-    out_ref[...] = both[:ncoef, :] + both[LANES : LANES + ncoef, :]
-    result = pltpu.make_async_copy(out_ref, out_hbm, sem)
-    result.start()
+    results = []
+    total = jnp.zeros((), f32)
+    for part in range(2):
+        at = pl.ds(leaves // 2 * part, leaves // 2)
+        both = lax.dot_general(split_ref[...], low_ref[at, :], NT, preferred_element_type=f32)
+        out_ref[:, at] = both[:ncoef, :] + both[LANES : LANES + ncoef, :]
+        results.append(pltpu.make_async_copy(out_ref.at[:, at], out_hbm.at[:, at], sems.at[part]))
+        results[part].start()
+        total += jnp.sum(both[LANES - 1 : LANES, :])
 
     used = jnp.sum(jnp.where(target_ref[...] < leaves, 1.0, 0.0))
-    total = jnp.sum(both[LANES - 1 : LANES, :])
     carried = jnp.logical_or(total != used, jnp.max(peak_ref[...]) >= 2.0**24)
-    result.wait()
+    for result in results:
+        result.wait()
 
     @pl.when(carried)
     def _():
@@ -296,7 +302,7 @@
                     out_ref[...] += lax.dot_general(
                         rows, count, NT, precision=lax.Precision.HIGHEST, preferred_element_type=f32
                     )
-        again = pltpu.make_async_copy(out_ref, out_hbm, sem)
+        again = pltpu.make_async_copy(out_ref, out_hbm, sems.at[0])
         again.start()
         again.wait()
 
@@ -384,7 +390,7 @@
             compiler_params=PARAMS,
         )(same, came, digits)
         received = [joins[0]] + [
-            lax.ppermute(joins[m], "grp", [(i, i ^ (2 * m)) for i in range(peers)]) for m in range(1, peers // 2)
+            lax.ppermute(joins[m], "grp", [(i, i ^ (2 * m)) for i in range(peers)]) for m in CHIPS[1:]
         ]
     else:
         received = [
@@ -440,7 +446,7 @@
             pltpu.VMEM((leaves, 512), f32),
             pltpu.VMEM((512, 512), bf16),
             pltpu.VMEM((leaves, 512), bf16),
-            pltpu.SemaphoreType.DMA,
+            pltpu.SemaphoreType.DMA((2,)),
         ],
         compiler_params=PARAMS,
     )(parts, low, peak, m2l_source, m2l_target, m2l_operator, *received)

time: 16.4 us -> 16.4 us (level)
  transfers between devices with their start and end apart: 6 -> 6, of which waited for: 1 -> 0; matrix products, arithmetic and copies ran while one was open for 0% -> 0% of each run, Pallas kernels for 33% -> 33%
where the time goes in v14:
time: 16.4 us; the launch traced here: 16.2 us
  Pallas kernels  8.36 us (51%)
  starting transfers between devices  7.15 us (44%)
  between operations  0.67 us (4%)
    pallas_call x1, Pallas kernels, shards(): pl.pallas_call(near_kernel, name='near', out_shape=(jax.ShapeDtypeStruct(...  4.09 us
    ppermute x3, starting transfers between devices, shards(): lax.ppermute(joins[m], 'grp', [(i, i ^ 2 * m) for i in range(peers)])  3.55 us
    ppermute x2, starting transfers between devices, exchange(): return lax.ppermute(table, ('slab', 'grp'), sorted(to.items()))  3.09 us
    pallas_call x1, Pallas kernels, shards(): pl.pallas_call(functools.partial(far_kernel, ops=ops, cap=cap), name='far...  1.51 us
    pallas_call x1, Pallas kernels, shards(): pl.pallas_call(functools.partial(prep_kernel, others=len(others), cap=cap...  1.46 us
    pallas_call x1, Pallas kernels, shards(): pl.pallas_call(functools.partial(counts_kernel, ops=ops, sources=sources)...  1.29 us
    ppermute x1, starting transfers between devices, shards(): came = lax.ppermute(other, 'grp', [(i, i ^ 1) for i in range(peers)])  0.51 us
  transfers between devices with their start and end apart: 6, of which 0 were waited for; matrix products, arithmetic and copies ran while one was open for 0% of the time, Pallas kernels for 33%

profile of v14, /device:TPU:0, one launch (start us, length us, event | category | flops | bytes accessed | tf_op | source)
XLA Modules:
  0.0 16.2 jit_solution(4828104312533938869)
XLA Ops:
  0.6 1.5 %prep.1 = (f32[64,512]{1,0:T(8,128)S(1)}, f32[64,121]{1,0:T(8,128)S(1)}, f32[64,121]{1,0:T(8,128)S(1)}, s32[8,512]{1,0:T(8,128)S(1)}, s32[32,128]{1,0:T(8,128)S(...) custom-call(f32[64,3,128]{2,1,0:T(4,128)} %bitcast.13, f32[64,128]{1,0:T(8,128)} %bitcast.14, ...), custom_call_target="tpu_custom_call" | custom-call | tf_op jit(solution)/shard_map/prep/pallas_call | solution.py:338
  2.1 3.1 %collective-permute-start.1 = (f32[64,512]{1,0:T(8,128)S(1)}, f32[64,512]{1,0:T(8,128)S(1)}, u32[]{:S(2)}, u32[]{:S(2)}) collective-permute-start(f32[64,512]{1,0:T(8,128)S(1)} %get-tuple-element.26.own_ref), channel_id=1, source_target_pairs={{0,8},{1,9},{2,10},{3,11},{4,12},{5,13},{6,14},{7,15},{8,0},{9,1},... | collective-permute-start | bytes 393224 | tf_op jit(solution)/shard_map/ppermute | solution.py:412
  5.2 0.0 collective-permute-start
  5.2 0.5 %collective-permute-start.2 = (f32[64,121]{1,0:T(8,128)S(1)}, f32[64,121]{1,0:T(8,128)S(1)}, u32[]{:S(2)}, u32[]{:S(2)}) collective-permute-start(f32[64,121]{1,0:T(8,128)S(1)} %get-tuple-element.32), channel_id=1, source_target_pairs={{0,1},{1,0},{2,3},{3,2},{4,5},{5,4},{6,7},{7,6},{8,9},{9,8},{10,11... | collective-permute-start | bytes 92936 | tf_op jit(solution)/shard_map/ppermute | solution.py:383
  5.7 1.3 %counts.1 = (s32[4,8,128]{2,1,0:T(8,128)S(1)}, bf16[1024,256]{1,0:T(8,128)(2,1)S(1)}, f32[256,256]{1,0:T(8,128)S(1)}) custom-call(s32[8,512]{1,0:T(8,128)S(1)} %get-tuple-element.20.list_ref, f32[968,121]{1,0:T(8,128)S(1)} %get-tuple-element.21.operators_ref, s32[32,128]{1,0:T(8,128)S(1)} %get-tuple-element.22.source_ref, ...), custom_call_target="tpu_custom_call" | custom-call | tf_op jit(solution)/shard_map/counts/pallas_call | solution.py:363
  7.0 0.0 collective-permute-done.2.came_ref
  7.0 2.5 %collective-permute-start.3 = (f32[32,121]{1,0:T(8,128)S(1)}, f32[32,121]{1,0:T(8,128)S(1)}, u32[]{:S(2)}, u32[]{:S(2)}) collective-permute-start(f32[32,121]{1,0:T(8,128)S(1)} %get-tuple-element.34), channel_id=1, source_target_pairs={{0,6},{1,7},{2,4},{3,5},{4,2},{5,3},{6,0},{7,1},{8,14},{9,15},{10,... | collective-permute-start | bytes 46472 | tf_op jit(solution)/shard_map/ppermute | solution.py:393
  9.6 0.5 %collective-permute-start.4 = (f32[32,121]{1,0:T(8,128)S(1)}, f32[32,121]{1,0:T(8,128)S(1)}, u32[]{:S(2)}, u32[]{:S(2)}) collective-permute-start(f32[32,121]{1,0:T(8,128)S(1)} %get-tuple-element.35), channel_id=1, source_target_pairs={{0,2},{1,3},{2,0},{3,1},{4,6},{5,7},{6,4},{7,5},{8,10},{9,11},{10,... | collective-permute-start | bytes 46472 | tf_op jit(solution)/shard_map/ppermute | solution.py:393
  10.1 0.5 %collective-permute-start.5 = (f32[32,121]{1,0:T(8,128)S(1)}, f32[32,121]{1,0:T(8,128)S(1)}, u32[]{:S(2)}, u32[]{:S(2)}) collective-permute-start(f32[32,121]{1,0:T(8,128)S(1)} %get-tuple-element.36), channel_id=1, source_target_pairs={{0,4},{1,5},{2,6},{3,7},{4,0},{5,1},{6,2},{7,3},{8,12},{9,13},{10,... | collective-permute-start | bytes 46472 | tf_op jit(solution)/shard_map/ppermute | solution.py:393
  10.6 0.0 collective-permute-done.1.first_ref
  10.6 0.0 collective-permute-done.second_ref
  10.6 4.1 %near.1 = (f32[64,128]{1,0:T(8,128)}, bf16[512,1024]{1,0:T(8,128)(2,1)S(1)}, f32[8,256]{1,0:T(8,128)S(1)}) custom-call(f32[64,512]{1,0:T(8,128)S(1)} %collective-permute-done.second_ref, f32[64,512]{1,0:T(8,128)S(1)} %get-tuple-element.26.own_ref, f32[64,512]{1,0:T(8,128)S(1)} %collective-permute-done.1.first_ref, ...), custom_call_target="tpu_custom_call" | custom-call | tf_op jit(solution)/shard_map/near/pallas_call | solution.py:417
  14.7 0.0 collective-permute-done.3.refs_1_
  14.7 0.0 collective-permute-done.4.refs_2_
  14.7 0.0 collective-permute-done.5.refs_3_
  14.7 1.5 %far.1 = f32[121,512]{1,0:T(8,128)} custom-call(bf16[1024,256]{1,0:T(8,128)(2,1)S(1)} %get-tuple-element.25.parts_ref, bf16[512,1024]{1,0:T(8,128)(2,1)S(1)} %get-tuple-element.29.low_ref, f32[8,256]{1,0:T(8,128)S(1)} %get-tuple-element.30.peak_ref, s32[32,128]{1,0:T(8,128)S(1)} %get-tuple-element.22.source_ref, s32[32,128]{1,0:T(8,128)S(1)} %get-tuple-element.23.target_ref, ...), custom_call_target="tpu_custom_call" | custom-call | tf_op jit(solution)/shard_map/far/pallas_call | solution.py:436
  (1 shorter events, 0.0 us)
Async XLA Ops:
  2.1 8.5 %collective-permute-start.1 = (f32[64,512]{1,0:T(8,128)S(1)}, f32[64,512]{1,0:T(8,128)S(1)}, u32[]{:S(2)}, u32[]{:S(2)}) collective-permute-start(f32[64,512]{1,0:T(8,128)S(1)} %get-tuple-element.26.own_ref), channel_id=1, source_target_pairs={{0,8},{1,9},{2,10},{3,11},{4,12},{5,13},{6,14},{7,15},{8,0},{9,1},... | collective-permute-start | bytes 393224 | tf_op jit(solution)/shard_map/ppermute | solution.py:412
  5.2 5.4 %collective-permute-start = (f32[64,512]{1,0:T(8,128)S(1)}, f32[64,512]{1,0:T(8,128)S(1)}, u32[]{:S(2)}, u32[]{:S(2)}) collective-permute-start(f32[64,512]{1,0:T(8,128)S(1)} %get-tuple-element.26.own_ref), channel_id=1, source_target_pairs={{0,1},{1,0},{2,3},{3,2},{4,5},{5,4},{6,7},{7,6},{8,16},{9,17},{10,... | collective-permute-start | bytes 393224 | tf_op jit(solution)/shard_map/ppermute | solution.py:412
  5.2 1.8 %collective-permute-start.2 = (f32[64,121]{1,0:T(8,128)S(1)}, f32[64,121]{1,0:T(8,128)S(1)}, u32[]{:S(2)}, u32[]{:S(2)}) collective-permute-start(f32[64,121]{1,0:T(8,128)S(1)} %get-tuple-element.32), channel_id=1, source_target_pairs={{0,1},{1,0},{2,3},{3,2},{4,5},{5,4},{6,7},{7,6},{8,9},{9,8},{10,11... | collective-permute-start | bytes 92936 | tf_op jit(solution)/shard_map/ppermute | solution.py:383
  7.0 7.7 %collective-permute-start.3 = (f32[32,121]{1,0:T(8,128)S(1)}, f32[32,121]{1,0:T(8,128)S(1)}, u32[]{:S(2)}, u32[]{:S(2)}) collective-permute-start(f32[32,121]{1,0:T(8,128)S(1)} %get-tuple-element.34), channel_id=1, source_target_pairs={{0,6},{1,7},{2,4},{3,5},{4,2},{5,3},{6,0},{7,1},{8,14},{9,15},{10,... | collective-permute-start | bytes 46472 | tf_op jit(solution)/shard_map/ppermute | solution.py:393
  9.6 5.1 %collective-permute-start.4 = (f32[32,121]{1,0:T(8,128)S(1)}, f32[32,121]{1,0:T(8,128)S(1)}, u32[]{:S(2)}, u32[]{:S(2)}) collective-permute-start(f32[32,121]{1,0:T(8,128)S(1)} %get-tuple-element.35), channel_id=1, source_target_pairs={{0,2},{1,3},{2,0},{3,1},{4,6},{5,7},{6,4},{7,5},{8,10},{9,11},{10,... | collective-permute-start | bytes 46472 | tf_op jit(solution)/shard_map/ppermute | solution.py:393
  10.1 4.6 %collective-permute-start.5 = (f32[32,121]{1,0:T(8,128)S(1)}, f32[32,121]{1,0:T(8,128)S(1)}, u32[]{:S(2)}, u32[]{:S(2)}) collective-permute-start(f32[32,121]{1,0:T(8,128)S(1)} %get-tuple-element.36), channel_id=1, source_target_pairs={{0,4},{1,5},{2,6},{3,7},{4,0},{5,1},{6,2},{7,3},{8,12},{9,13},{10,... | collective-permute-start | bytes 46472 | tf_op jit(solution)/shard_map/ppermute | solution.py:393

commit v15 on v14

--- a/solution.py
+++ b/solution.py
@@ -239,9 +239,11 @@
 
 
 def far_kernel(
-    parts_ref, low_ref, peak_ref, source_ref, target_ref, operator_ref, *refs, ops, cap,
+    parts_ref, low_ref, peak_ref, source_ref, target_ref, operator_ref, near_ref, *refs, ops, cap,
 ):
-    *join_refs, out_hbm, out_ref, received_ref, split_ref, pair_ref, a_ref, b_ref, sems = refs
+    *join_refs, out_hbm, near_hbm, out_ref, received_ref, split_ref, pair_ref, a_ref, b_ref, sems = refs
+    results = [pltpu.make_async_copy(near_ref, near_hbm, sems.at[2])]
+    results[0].start()
     if cap:
         placed(join_refs, received_ref, cap)
     else:
@@ -250,22 +252,23 @@
     sources = received_ref.shape[0]
     f32 = jnp.float32
     hi, lo = split(pad_lanes(received_ref[...]))
-    table = lax.dot_general(
-        parts_ref[...], jnp.concatenate([hi, hi], axis=1), NT, preferred_element_type=f32
-    ) + lax.dot_general(parts_ref[:, :LANES], lo, NT, preferred_element_type=f32)
+    both = jnp.concatenate(
+        [jnp.concatenate([hi, hi], axis=1), jnp.concatenate([lo, jnp.zeros_like(lo)], axis=1)], axis=0
+    )
+    table = lax.dot_general(parts_ref[...], both, NT, preferred_element_type=f32)
+    table = table[:, :sources] + table[:, sources:]
     ones = jnp.where(lax.broadcasted_iota(jnp.int32, (LANES, sources), 0) == LANES - 1, 1.0, 0.0)
     for k in range(ops):
         hi, lo = split(table[LANES * k : LANES * (k + 1), :] + ones)
         split_ref[:LANES, sources * k : sources * (k + 1)] = hi
         split_ref[LANES:, sources * k : sources * (k + 1)] = lo
-    results = []
     total = jnp.zeros((), f32)
     for part in range(2):
         at = pl.ds(leaves // 2 * part, leaves // 2)
         both = lax.dot_general(split_ref[...], low_ref[at, :], NT, preferred_element_type=f32)
         out_ref[:, at] = both[:ncoef, :] + both[LANES : LANES + ncoef, :]
         results.append(pltpu.make_async_copy(out_ref.at[:, at], out_hbm.at[:, at], sems.at[part]))
-        results[part].start()
+        results[-1].start()
         total += jnp.sum(both[LANES - 1 : LANES, :])
 
     used = jnp.sum(jnp.where(target_ref[...] < leaves, 1.0, 0.0))
@@ -418,7 +421,7 @@
         near_kernel,
         name="near",
         out_shape=(
-            jax.ShapeDtypeStruct((tiles, LANES), f32),
+            pltpu.VMEM((tiles, LANES), f32),
             jax.ShapeDtypeStruct((leaves, ops * sources), bf16),
             jax.ShapeDtypeStruct((8, codes), f32),
         ),
@@ -433,12 +436,12 @@
         compiler_params=PARAMS,
     )(second, table, first, places, digits)
 
-    local_exp = pl.pallas_call(
+    local_exp, near_potential = pl.pallas_call(
         functools.partial(far_kernel, ops=ops, cap=cap),
         name="far",
-        out_shape=jax.ShapeDtypeStruct((ncoef, leaves), f32),
-        in_specs=[VMEM] * (6 + len(received)),
-        out_specs=ANY,
+        out_shape=(jax.ShapeDtypeStruct((ncoef, leaves), f32), jax.ShapeDtypeStruct((tiles, LANES), f32)),
+        in_specs=[VMEM] * (7 + len(received)),
+        out_specs=(ANY, ANY),
         scratch_shapes=[
             pltpu.VMEM((ncoef, leaves), f32),
             pltpu.VMEM((sources, ncoef), f32),
@@ -446,10 +449,10 @@
             pltpu.VMEM((leaves, 512), f32),
             pltpu.VMEM((512, 512), bf16),
             pltpu.VMEM((leaves, 512), bf16),
-            pltpu.SemaphoreType.DMA((2,)),
+            pltpu.SemaphoreType.DMA((3,)),
         ],
         compiler_params=PARAMS,
-    )(parts, low, peak, m2l_source, m2l_target, m2l_operator, *received)
+    )(parts, low, peak, m2l_source, m2l_target, m2l_operator, near_potential, *received)
     return (local_exp, near_potential.reshape(npoints))
 
 

time: 16.4 us -> 15.7 us (0.957)
  Pallas kernels: 8.36 us -> 7.63 us
    pallas_call x1, Pallas kernels: 4.09 us -> 3.43 us  [shards(): pl.pallas_call(near_kernel, name='near', out_shape=(pltpu.VMEM((tiles, LA...]
  transfers between devices with their start and end apart: 6 -> 6, of which waited for: 0 -> 0; matrix products, arithmetic and copies ran while one was open for 0% -> 0% of each run, Pallas kernels for 33% -> 31%
where the time goes in v15:
time: 15.7 us; the launch traced here: 15.5 us
  Pallas kernels  7.63 us (49%)
  starting transfers between devices  7.15 us (46%)
  between operations  0.69 us (4%)
    ppermute x3, starting transfers between devices, shards(): lax.ppermute(joins[m], 'grp', [(i, i ^ 2 * m) for i in range(peers)])  3.55 us
    pallas_call x1, Pallas kernels, shards(): pl.pallas_call(near_kernel, name='near', out_shape=(pltpu.VMEM((tiles, LA...  3.43 us
    ppermute x2, starting transfers between devices, exchange(): return lax.ppermute(table, ('slab', 'grp'), sorted(to.items()))  3.09 us
    pallas_call x1, Pallas kernels, shards(): pl.pallas_call(functools.partial(prep_kernel, others=len(others), cap=cap...  1.46 us
    pallas_call x1, Pallas kernels, shards(): pl.pallas_call(functools.partial(far_kernel, ops=ops, cap=cap), name='far...  1.43 us
    pallas_call x1, Pallas kernels, shards(): pl.pallas_call(functools.partial(counts_kernel, ops=ops, sources=sources)...  1.29 us
    ppermute x1, starting transfers between devices, shards(): came = lax.ppermute(other, 'grp', [(i, i ^ 1) for i in range(peers)])  0.51 us
  transfers between devices with their start and end apart: 6, of which 0 were waited for; matrix products, arithmetic and copies ran while one was open for 0% of the time, Pallas kernels for 31%

profile of v15, /device:TPU:0, one launch (start us, length us, event | category | flops | bytes accessed | tf_op | source)
XLA Modules:
  0.0 15.5 jit_solution(12277064232888464992)
XLA Ops:
  0.6 1.5 %prep.1 = (f32[64,512]{1,0:T(8,128)S(1)}, f32[64,121]{1,0:T(8,128)S(1)}, f32[64,121]{1,0:T(8,128)S(1)}, s32[8,512]{1,0:T(8,128)S(1)}, s32[32,128]{1,0:T(8,128)S(...) custom-call(f32[64,3,128]{2,1,0:T(4,128)} %bitcast.13, f32[64,128]{1,0:T(8,128)} %bitcast.14, ...), custom_call_target="tpu_custom_call" | custom-call | tf_op jit(solution)/shard_map/prep/pallas_call | solution.py:341
  2.1 3.1 %collective-permute-start.1 = (f32[64,512]{1,0:T(8,128)S(1)}, f32[64,512]{1,0:T(8,128)S(1)}, u32[]{:S(2)}, u32[]{:S(2)}) collective-permute-start(f32[64,512]{1,0:T(8,128)S(1)} %get-tuple-element.28.own_ref), channel_id=1, source_target_pairs={{0,8},{1,9},{2,10},{3,11},{4,12},{5,13},{6,14},{7,15},{8,0},{9,1},... | collective-permute-start | bytes 393224 | tf_op jit(solution)/shard_map/ppermute | solution.py:415
  5.2 0.0 collective-permute-start
  5.2 0.5 %collective-permute-start.2 = (f32[64,121]{1,0:T(8,128)S(1)}, f32[64,121]{1,0:T(8,128)S(1)}, u32[]{:S(2)}, u32[]{:S(2)}) collective-permute-start(f32[64,121]{1,0:T(8,128)S(1)} %get-tuple-element.35), channel_id=1, source_target_pairs={{0,1},{1,0},{2,3},{3,2},{4,5},{5,4},{6,7},{7,6},{8,9},{9,8},{10,11... | collective-permute-start | bytes 92936 | tf_op jit(solution)/shard_map/ppermute | solution.py:386
  5.7 1.3 %counts.1 = (s32[4,8,128]{2,1,0:T(8,128)S(1)}, bf16[1024,256]{1,0:T(8,128)(2,1)S(1)}, f32[256,256]{1,0:T(8,128)S(1)}) custom-call(s32[8,512]{1,0:T(8,128)S(1)} %get-tuple-element.22.list_ref, f32[968,121]{1,0:T(8,128)S(1)} %get-tuple-element.23.operators_ref, s32[32,128]{1,0:T(8,128)S(1)} %get-tuple-element.24.source_ref, ...), custom_call_target="tpu_custom_call" | custom-call | tf_op jit(solution)/shard_map/counts/pallas_call | solution.py:366
  7.0 0.0 collective-permute-done.2.came_ref
  7.0 2.5 %collective-permute-start.3 = (f32[32,121]{1,0:T(8,128)S(1)}, f32[32,121]{1,0:T(8,128)S(1)}, u32[]{:S(2)}, u32[]{:S(2)}) collective-permute-start(f32[32,121]{1,0:T(8,128)S(1)} %get-tuple-element.37), channel_id=1, source_target_pairs={{0,6},{1,7},{2,4},{3,5},{4,2},{5,3},{6,0},{7,1},{8,14},{9,15},{10,... | collective-permute-start | bytes 46472 | tf_op jit(solution)/shard_map/ppermute | solution.py:396
  9.6 0.5 %collective-permute-start.4 = (f32[32,121]{1,0:T(8,128)S(1)}, f32[32,121]{1,0:T(8,128)S(1)}, u32[]{:S(2)}, u32[]{:S(2)}) collective-permute-start(f32[32,121]{1,0:T(8,128)S(1)} %get-tuple-element.38), channel_id=1, source_target_pairs={{0,2},{1,3},{2,0},{3,1},{4,6},{5,7},{6,4},{7,5},{8,10},{9,11},{10,... | collective-permute-start | bytes 46472 | tf_op jit(solution)/shard_map/ppermute | solution.py:396
  10.1 0.5 %collective-permute-start.5 = (f32[32,121]{1,0:T(8,128)S(1)}, f32[32,121]{1,0:T(8,128)S(1)}, u32[]{:S(2)}, u32[]{:S(2)}) collective-permute-start(f32[32,121]{1,0:T(8,128)S(1)} %get-tuple-element.39), channel_id=1, source_target_pairs={{0,4},{1,5},{2,6},{3,7},{4,0},{5,1},{6,2},{7,3},{8,12},{9,13},{10,... | collective-permute-start | bytes 46472 | tf_op jit(solution)/shard_map/ppermute | solution.py:396
  10.6 0.0 collective-permute-done.1.first_ref
  10.6 0.0 collective-permute-done.second_ref
  10.6 3.4 %near.1 = (f32[64,128]{1,0:T(8,128)S(1)}, bf16[512,1024]{1,0:T(8,128)(2,1)S(1)}, f32[8,256]{1,0:T(8,128)S(1)}) custom-call(f32[64,512]{1,0:T(8,128)S(1)} %collective-permute-done.second_ref, f32[64,512]{1,0:T(8,128)S(1)} %get-tuple-element.28.own_ref, f32[64,512]{1,0:T(8,128)S(1)} %collective-permute-done.1.first_ref, ...), custom_call_target="tpu_custom_call" | custom-call | tf_op jit(solution)/shard_map/near/pallas_call | solution.py:420
  14.0 0.0 collective-permute-done.3.refs_1_
  14.1 0.0 collective-permute-done.4.refs_2_
  14.1 0.0 collective-permute-done.5.refs_3_
  14.1 1.4 %far.1 = (f32[121,512]{1,0:T(8,128)}, f32[64,128]{1,0:T(8,128)}) custom-call(bf16[1024,256]{1,0:T(8,128)(2,1)S(1)} %get-tuple-element.27.parts_ref, bf16[512,1024]{1,0:T(8,128)(2,1)S(1)} %get-tuple-element.31.low_ref, f32[8,256]{1,0:T(8,128)S(1)} %get-tuple-element.32.peak_ref, s32[32,128]{1,0:T(8,128)S(1)} %get-tuple-element.24.source_ref, ...), custom_call_target="tpu_custom_call" | custom-call | tf_op jit(solution)/shard_map/far/pallas_call | solution.py:439
  (1 shorter events, 0.0 us)
Async XLA Ops:
  2.1 8.5 %collective-permute-start.1 = (f32[64,512]{1,0:T(8,128)S(1)}, f32[64,512]{1,0:T(8,128)S(1)}, u32[]{:S(2)}, u32[]{:S(2)}) collective-permute-start(f32[64,512]{1,0:T(8,128)S(1)} %get-tuple-element.28.own_ref), channel_id=1, source_target_pairs={{0,8},{1,9},{2,10},{3,11},{4,12},{5,13},{6,14},{7,15},{8,0},{9,1},... | collective-permute-start | bytes 393224 | tf_op jit(solution)/shard_map/ppermute | solution.py:415
  5.2 5.4 %collective-permute-start = (f32[64,512]{1,0:T(8,128)S(1)}, f32[64,512]{1,0:T(8,128)S(1)}, u32[]{:S(2)}, u32[]{:S(2)}) collective-permute-start(f32[64,512]{1,0:T(8,128)S(1)} %get-tuple-element.28.own_ref), channel_id=1, source_target_pairs={{0,1},{1,0},{2,3},{3,2},{4,5},{5,4},{6,7},{7,6},{8,16},{9,17},{10,... | collective-permute-start | bytes 393224 | tf_op jit(solution)/shard_map/ppermute | solution.py:415
  5.2 1.8 %collective-permute-start.2 = (f32[64,121]{1,0:T(8,128)S(1)}, f32[64,121]{1,0:T(8,128)S(1)}, u32[]{:S(2)}, u32[]{:S(2)}) collective-permute-start(f32[64,121]{1,0:T(8,128)S(1)} %get-tuple-element.35), channel_id=1, source_target_pairs={{0,1},{1,0},{2,3},{3,2},{4,5},{5,4},{6,7},{7,6},{8,9},{9,8},{10,11... | collective-permute-start | bytes 92936 | tf_op jit(solution)/shard_map/ppermute | solution.py:386
  7.0 7.0 %collective-permute-start.3 = (f32[32,121]{1,0:T(8,128)S(1)}, f32[32,121]{1,0:T(8,128)S(1)}, u32[]{:S(2)}, u32[]{:S(2)}) collective-permute-start(f32[32,121]{1,0:T(8,128)S(1)} %get-tuple-element.37), channel_id=1, source_target_pairs={{0,6},{1,7},{2,4},{3,5},{4,2},{5,3},{6,0},{7,1},{8,14},{9,15},{10,... | collective-permute-start | bytes 46472 | tf_op jit(solution)/shard_map/ppermute | solution.py:396
  9.6 4.5 %collective-permute-start.4 = (f32[32,121]{1,0:T(8,128)S(1)}, f32[32,121]{1,0:T(8,128)S(1)}, u32[]{:S(2)}, u32[]{:S(2)}) collective-permute-start(f32[32,121]{1,0:T(8,128)S(1)} %get-tuple-element.38), channel_id=1, source_target_pairs={{0,2},{1,3},{2,0},{3,1},{4,6},{5,7},{6,4},{7,5},{8,10},{9,11},{10,... | collective-permute-start | bytes 46472 | tf_op jit(solution)/shard_map/ppermute | solution.py:396
  10.1 4.0 %collective-permute-start.5 = (f32[32,121]{1,0:T(8,128)S(1)}, f32[32,121]{1,0:T(8,128)S(1)}, u32[]{:S(2)}, u32[]{:S(2)}) collective-permute-start(f32[32,121]{1,0:T(8,128)S(1)} %get-tuple-element.39), channel_id=1, source_target_pairs={{0,4},{1,5},{2,6},{3,7},{4,0},{5,1},{6,2},{7,3},{8,12},{9,13},{10,... | collective-permute-start | bytes 46472 | tf_op jit(solution)/shard_map/ppermute | solution.py:396

commit v16 on v15

--- a/solution.py
+++ b/solution.py
@@ -9,7 +9,6 @@
 
 SOFT2 = 0.0625
 LANES = 128
-CHIPS = (0, 3, 1, 2)
 PTS = 16
 UNITS = 2.0**20
 SCALE = 2.0**31
@@ -80,21 +79,21 @@
         copy.wait()
 
 
-def join_kernel(out_ref, came_ref, digits_ref, *join_refs, cap):
+def join_kernel(out_ref, came_ref, digits_ref, join_ref, *, cap):
     del digits_ref
-    chip = lax.axis_index("grp") // 2
-    for m, ref in enumerate(join_refs):
-        at = pl.ds(pl.multiple_of((chip ^ m) * cap, cap), cap)
-        ref[:cap, :] = out_ref[at, :]
-        ref[cap:, :] = came_ref[at, :]
-
-
-def placed(join_refs, rows_ref, cap):
-    me = lax.axis_index("grp")
-    for m, ref in zip(CHIPS, join_refs):
-        peer = me ^ (2 * m)
-        rows_ref[pl.ds(pl.multiple_of(peer * cap, cap), cap), :] = ref[:cap, :]
-        rows_ref[pl.ds(pl.multiple_of((peer ^ 1) * cap, cap), cap), :] = ref[cap:, :]
+    for chip in range(join_ref.shape[0] // (2 * cap)):
+        join_ref[2 * cap * chip : 2 * cap * chip + cap, :] = out_ref[cap * chip : cap * (chip + 1), :]
+        join_ref[2 * cap * chip + cap : 2 * cap * (chip + 1), :] = came_ref[cap * chip : cap * (chip + 1), :]
+
+
+def placed(joined_ref, rows_ref, cap):
+    side = lax.axis_index("grp") % 2
+    for chip in range(joined_ref.shape[0] // (2 * cap)):
+        for other in range(2):
+            peer = 2 * chip + (side if other == 0 else 1 - side)
+            rows_ref[pl.ds(pl.multiple_of(peer * cap, cap), cap), :] = joined_ref[
+                cap * (2 * chip + other) : cap * (2 * chip + other + 1), :
+            ]
 
 
 def counts_kernel(
@@ -198,14 +197,18 @@
 
     def gather(place):
         idx = place & (LANES - 1)
-        group = place >> 7
+        bits = [(place >> (7 + level)) & 1 == 1 for level in range(4)]
         refs = [packed_ref.at[8 * r : 8 * r + 8] for r in range(2 * PTS // 8)]
         refs += [charge_ref.at[8 * r : 8 * r + 8] for r in range(PTS // 8)]
-        found = [lane_gather(ref[:, :LANES], idx) for ref in refs]
-        for s in range(1, 3 * groups):
-            here = group == s
-            for r, ref in enumerate(refs):
-                found[r] = jnp.where(here, lane_gather(ref[:, LANES * s : LANES * (s + 1)], idx), found[r])
+        found = []
+        for ref in refs:
+            layer = [lane_gather(ref[:, LANES * s : LANES * (s + 1)], idx) for s in range(3 * groups)]
+            for bit in bits:
+                layer = [
+                    jnp.where(bit, layer[i + 1], layer[i]) if i + 1 < len(layer) else layer[i]
+                    for i in range(0, len(layer), 2)
+                ]
+            found.append(layer[0])
         return found
 
     def step(g, carry):
@@ -245,7 +248,7 @@
     results = [pltpu.make_async_copy(near_ref, near_hbm, sems.at[2])]
     results[0].start()
     if cap:
-        placed(join_refs, received_ref, cap)
+        placed(join_refs[0], received_ref, cap)
     else:
         received_ref = join_refs[0]
     ncoef, leaves = out_ref.shape
@@ -384,16 +387,24 @@
     )(near_list, operators, m2l_source, m2l_target, m2l_operator)
     if cap:
         came = lax.ppermute(other, "grp", [(i, i ^ 1) for i in range(peers)])
-        joins = pl.pallas_call(
+        joined = pl.pallas_call(
             functools.partial(join_kernel, cap=cap),
             name="join",
-            out_shape=(jax.ShapeDtypeStruct((2 * cap, ncoef), f32),) * (peers // 2),
+            out_shape=jax.ShapeDtypeStruct((sources, ncoef), f32),
             in_specs=[VMEM, VMEM, ANY],
-            out_specs=(VMEM,) * (peers // 2),
+            out_specs=VMEM,
             compiler_params=PARAMS,
         )(same, came, digits)
-        received = [joins[0]] + [
-            lax.ppermute(joins[m], "grp", [(i, i ^ (2 * m)) for i in range(peers)]) for m in CHIPS[1:]
+        sides = [[2 * chip + side for chip in range(peers // 2)] for side in range(2)]
+        received = [
+            lax.all_to_all(
+                joined.reshape(peers // 2, 2 * cap, ncoef),
+                "grp",
+                split_axis=0,
+                concat_axis=0,
+                axis_index_groups=sides,
+                tiled=True,
+            ).reshape(sources, ncoef)
         ]
     else:
         received = [

time: 15.7 us -> 17.9 us (1.14)
  waiting for transfers between devices: 0.05 us -> 1.45 us
  Pallas kernels: 7.63 us -> 8.18 us
    all_to_all x0 -> x1, starting transfers between devices: none -> 3.72 us  [shards(): lax.all_to_all(joined.reshape(peers // 2, 2 * cap, ncoef), 'grp', split_a...]
    ppermute x3 -> x0, starting transfers between devices: 3.55 us -> none  [shards(): lax.ppermute(joins[m], 'grp', [(i, i ^ 2 * m) for i in range(peers)])]
    all_to_all x0 -> x1, waiting for transfers between devices: none -> 1.44 us  [shards(): lax.all_to_all(joined.reshape(peers // 2, 2 * cap, ncoef), 'grp', split_a...]
    pallas_call x1, Pallas kernels: 0.02 us -> 0.64 us  [shards(): pl.pallas_call(functools.partial(join_kernel, cap=cap), name='join', out_...]
  transfers between devices with their start and end apart: 6 -> 4, of which waited for: 0 -> 1; matrix products, arithmetic and copies ran while one was open for 0% -> 0% of each run, Pallas kernels for 31% -> 30%
where the time goes in v16:
time: 17.9 us; the launch traced here: 17.6 us
  Pallas kernels  8.18 us (46%)
  starting transfers between devices  7.32 us (41%)
  waiting for transfers between devices  1.45 us (8%)
  between operations  0.66 us (4%)
    all_to_all x1, starting transfers between devices, shards(): lax.all_to_all(joined.reshape(peers // 2, 2 * cap, ncoef), 'grp', split_a...  3.72 us
    pallas_call x1, Pallas kernels, shards(): pl.pallas_call(near_kernel, name='near', out_shape=(pltpu.VMEM((tiles, LA...  3.39 us
    ppermute x2, starting transfers between devices, exchange(): return lax.ppermute(table, ('slab', 'grp'), sorted(to.items()))  3.09 us
    pallas_call x1, Pallas kernels, shards(): pl.pallas_call(functools.partial(prep_kernel, others=len(others), cap=cap...  1.46 us
    all_to_all x1, waiting for transfers between devices, shards(): lax.all_to_all(joined.reshape(peers // 2, 2 * cap, ncoef), 'grp', split_a...  1.44 us
    pallas_call x1, Pallas kernels, shards(): pl.pallas_call(functools.partial(far_kernel, ops=ops, cap=cap), name='far...  1.41 us
    pallas_call x1, Pallas kernels, shards(): pl.pallas_call(functools.partial(counts_kernel, ops=ops, sources=sources)...  1.29 us
    pallas_call x1, Pallas kernels, shards(): pl.pallas_call(functools.partial(join_kernel, cap=cap), name='join', out_...  0.64 us
  transfers between devices with their start and end apart: 4, of which 1 were waited for; matrix products, arithmetic and copies ran while one was open for 0% of the time, Pallas kernels for 30%

profile of v16, /device:TPU:0, one launch (start us, length us, event | category | flops | bytes accessed | tf_op | source)
XLA Modules:
  0.0 17.6 jit_solution(3869027367855047328)
XLA Ops:
  0.6 1.5 %prep.1 = (f32[64,512]{1,0:T(8,128)S(1)}, f32[64,121]{1,0:T(8,128)S(1)}, f32[64,121]{1,0:T(8,128)S(1)}, s32[8,512]{1,0:T(8,128)S(1)}, s32[32,128]{1,0:T(8,128)S(...) custom-call(f32[64,3,128]{2,1,0:T(4,128)} %bitcast.16, f32[64,128]{1,0:T(8,128)} %bitcast.17, ...), custom_call_target="tpu_custom_call" | custom-call | tf_op jit(solution)/shard_map/prep/pallas_call | solution.py:344
  2.1 3.1 %collective-permute-start.1 = (f32[64,512]{1,0:T(8,128)S(1)}, f32[64,512]{1,0:T(8,128)S(1)}, u32[]{:S(2)}, u32[]{:S(2)}) collective-permute-start(f32[64,512]{1,0:T(8,128)S(1)} %get-tuple-element.24.own_ref), channel_id=1, source_target_pairs={{0,8},{1,9},{2,10},{3,11},{4,12},{5,13},{6,14},{7,15},{8,0},{9,1},... | collective-permute-start | bytes 393224 | tf_op jit(solution)/shard_map/ppermute | solution.py:426
  5.2 0.0 collective-permute-start
  5.2 0.5 %collective-permute-start.2 = (f32[64,121]{1,0:T(8,128)S(1)}, f32[64,121]{1,0:T(8,128)S(1)}, u32[]{:S(2)}, u32[]{:S(2)}) collective-permute-start(f32[64,121]{1,0:T(8,128)S(1)} %get-tuple-element.31), channel_id=1, source_target_pairs={{0,1},{1,0},{2,3},{3,2},{4,5},{5,4},{6,7},{7,6},{8,9},{9,8},{10,11... | collective-permute-start | bytes 92936 | tf_op jit(solution)/shard_map/ppermute | solution.py:389
  5.7 1.3 %counts.1 = (s32[4,8,128]{2,1,0:T(8,128)S(1)}, bf16[1024,256]{1,0:T(8,128)(2,1)S(1)}, f32[256,256]{1,0:T(8,128)S(1)}) custom-call(s32[8,512]{1,0:T(8,128)S(1)} %get-tuple-element.18.list_ref, f32[968,121]{1,0:T(8,128)S(1)} %get-tuple-element.19.operators_ref, s32[32,128]{1,0:T(8,128)S(1)} %get-tuple-element.20.source_ref, ...), custom_call_target="tpu_custom_call" | custom-call | tf_op jit(solution)/shard_map/counts/pallas_call | solution.py:369
  7.0 0.0 collective-permute-done.2.came_ref
  7.0 0.6 %join.1 = f32[128,121]{1,0:T(8,128)} custom-call(f32[64,121]{1,0:T(8,128)S(1)} %get-tuple-element.30.out_ref, f32[64,121]{1,0:T(8,128)S(1)} %collective-permute-done.2.came_ref, f32[256,256]{1,0:T(8,128)S(1)} %get-tuple-element.26.acc_ref.digits_ref), custom_call_target="tpu_custom_call" | custom-call | tf_op jit(solution)/shard_map/join/pallas_call | solution.py:390
  7.6 3.7 %all-to-all-start = ((f32[4,32,121]{2,1,0:T(8,128)}), f32[4,32,121]{2,1,0:T(8,128)S(1)}, u32[]{:S(2)}, u32[]{:S(2)}) async-start(f32[4,32,121]{2,1,0:T(8,128)} %bitcast.9), calls=%async_computation | async-start | bytes 131072 | tf_op jit(solution)/shard_map/all_to_all | solution.py:400
  11.4 0.0 collective-permute-done.1.first_ref
  11.4 0.0 collective-permute-done.second_ref
  11.4 3.4 %near.1 = (f32[64,128]{1,0:T(8,128)S(1)}, bf16[512,1024]{1,0:T(8,128)(2,1)S(1)}, f32[8,256]{1,0:T(8,128)S(1)}) custom-call(f32[64,512]{1,0:T(8,128)S(1)} %collective-permute-done.second_ref, f32[64,512]{1,0:T(8,128)S(1)} %get-tuple-element.24.own_ref, f32[64,512]{1,0:T(8,128)S(1)} %collective-permute-done.1.first_ref, ...), custom_call_target="tpu_custom_call" | custom-call | tf_op jit(solution)/shard_map/near/pallas_call | solution.py:431
  14.8 1.4 %all-to-all-done = f32[4,32,121]{2,1,0:T(8,128)S(1)} async-done(((f32[4,32,121]{2,1,0:T(8,128)}), f32[4,32,121]{2,1,0:T(8,128)S(1)}, u32[]{:S(2)}, u32[]{:S(2)}) %all-to-all-start) | async-done | bytes 61984 | tf_op jit(solution)/shard_map/all_to_all | solution.py:400
  16.2 1.4 %far.1 = (f32[121,512]{1,0:T(8,128)}, f32[64,128]{1,0:T(8,128)}) custom-call(bf16[1024,256]{1,0:T(8,128)(2,1)S(1)} %get-tuple-element.23.parts_ref, bf16[512,1024]{1,0:T(8,128)(2,1)S(1)} %get-tuple-element.27.low_ref, f32[8,256]{1,0:T(8,128)S(1)} %get-tuple-element.28.peak_ref, s32[32,128]{1,0:T(8,128)S(1)} %get-tuple-element.20.source_ref, ...), custom_call_target="tpu_custom_call" | custom-call | tf_op jit(solution)/shard_map/far/pallas_call | solution.py:450
Async XLA Ops:
  2.1 9.3 %collective-permute-start.1 = (f32[64,512]{1,0:T(8,128)S(1)}, f32[64,512]{1,0:T(8,128)S(1)}, u32[]{:S(2)}, u32[]{:S(2)}) collective-permute-start(f32[64,512]{1,0:T(8,128)S(1)} %get-tuple-element.24.own_ref), channel_id=1, source_target_pairs={{0,8},{1,9},{2,10},{3,11},{4,12},{5,13},{6,14},{7,15},{8,0},{9,1},... | collective-permute-start | bytes 393224 | tf_op jit(solution)/shard_map/ppermute | solution.py:426
  5.2 6.2 %collective-permute-start = (f32[64,512]{1,0:T(8,128)S(1)}, f32[64,512]{1,0:T(8,128)S(1)}, u32[]{:S(2)}, u32[]{:S(2)}) collective-permute-start(f32[64,512]{1,0:T(8,128)S(1)} %get-tuple-element.24.own_ref), channel_id=1, source_target_pairs={{0,1},{1,0},{2,3},{3,2},{4,5},{5,4},{6,7},{7,6},{8,16},{9,17},{10,... | collective-permute-start | bytes 393224 | tf_op jit(solution)/shard_map/ppermute | solution.py:426
  5.2 1.8 %collective-permute-start.2 = (f32[64,121]{1,0:T(8,128)S(1)}, f32[64,121]{1,0:T(8,128)S(1)}, u32[]{:S(2)}, u32[]{:S(2)}) collective-permute-start(f32[64,121]{1,0:T(8,128)S(1)} %get-tuple-element.31), channel_id=1, source_target_pairs={{0,1},{1,0},{2,3},{3,2},{4,5},{5,4},{6,7},{7,6},{8,9},{9,8},{10,11... | collective-permute-start | bytes 92936 | tf_op jit(solution)/shard_map/ppermute | solution.py:389
  7.6 8.6 %all-to-all-start = ((f32[4,32,121]{2,1,0:T(8,128)}), f32[4,32,121]{2,1,0:T(8,128)S(1)}, u32[]{:S(2)}, u32[]{:S(2)}) async-start(f32[4,32,121]{2,1,0:T(8,128)} %bitcast.9), calls=%async_computation | async-start | bytes 131072 | tf_op jit(solution)/shard_map/all_to_all | solution.py:400

commit v17 on v15

--- a/solution.py
+++ b/solution.py
@@ -63,8 +63,8 @@
         lane = send & (LANES - 1)
         group = send >> 7
         idx = jnp.broadcast_to(lane, (ncoef, LANES))
-        picked = jnp.zeros((ncoef, LANES), jnp.float32)
-        for g in range(leaves // LANES):
+        picked = lane_gather(multipoles_ref[:, :LANES], idx)
+        for g in range(1, leaves // LANES):
             got = lane_gather(multipoles_ref[:, LANES * g : LANES * (g + 1)], idx)
             picked = jnp.where(group == g, got, picked)
         rows_ref[LANES * sb : LANES * (sb + 1), :] = picked.T
@@ -198,14 +198,18 @@
 
     def gather(place):
         idx = place & (LANES - 1)
-        group = place >> 7
+        bits = [place & (LANES << level) != 0 for level in range(4)]
         refs = [packed_ref.at[8 * r : 8 * r + 8] for r in range(2 * PTS // 8)]
         refs += [charge_ref.at[8 * r : 8 * r + 8] for r in range(PTS // 8)]
-        found = [lane_gather(ref[:, :LANES], idx) for ref in refs]
-        for s in range(1, 3 * groups):
-            here = group == s
-            for r, ref in enumerate(refs):
-                found[r] = jnp.where(here, lane_gather(ref[:, LANES * s : LANES * (s + 1)], idx), found[r])
+        found = []
+        for ref in refs:
+            layer = [lane_gather(ref[:, LANES * s : LANES * (s + 1)], idx) for s in range(3 * groups)]
+            for bit in bits:
+                layer = [
+                    jnp.where(bit, layer[i + 1], layer[i]) if i + 1 < len(layer) else layer[i]
+                    for i in range(0, len(layer), 2)
+                ]
+            found.append(layer[0])
         return found
 
     def step(g, carry):

time: 15.7 us -> 15.6 us (level)
  transfers between devices with their start and end apart: 6 -> 6, of which waited for: 0 -> 0; matrix products, arithmetic and copies ran while one was open for 0% -> 0% of each run, Pallas kernels for 31% -> 30%
where the time goes in v17:
time: 15.6 us; the launch traced here: 15.5 us
  Pallas kernels  7.59 us (49%)
  starting transfers between devices  7.15 us (46%)
  between operations  0.69 us (4%)
    ppermute x3, starting transfers between devices, shards(): lax.ppermute(joins[m], 'grp', [(i, i ^ 2 * m) for i in range(peers)])  3.55 us
    pallas_call x1, Pallas kernels, shards(): pl.pallas_call(near_kernel, name='near', out_shape=(pltpu.VMEM((tiles, LA...  3.39 us
    ppermute x2, starting transfers between devices, exchange(): return lax.ppermute(table, ('slab', 'grp'), sorted(to.items()))  3.09 us
    pallas_call x1, Pallas kernels, shards(): pl.pallas_call(functools.partial(prep_kernel, others=len(others), cap=cap...  1.46 us
    pallas_call x1, Pallas kernels, shards(): pl.pallas_call(functools.partial(far_kernel, ops=ops, cap=cap), name='far...  1.43 us
    pallas_call x1, Pallas kernels, shards(): pl.pallas_call(functools.partial(counts_kernel, ops=ops, sources=sources)...  1.29 us
    ppermute x1, starting transfers between devices, shards(): came = lax.ppermute(other, 'grp', [(i, i ^ 1) for i in range(peers)])  0.51 us
  transfers between devices with their start and end apart: 6, of which 0 were waited for; matrix products, arithmetic and copies ran while one was open for 0% of the time, Pallas kernels for 30%

profile of v17, /device:TPU:0, one launch (start us, length us, event | category | flops | bytes accessed | tf_op | source)
XLA Modules:
  0.0 15.5 jit_solution(12029939116367662597)
XLA Ops:
  0.6 1.5 %prep.1 = (f32[64,512]{1,0:T(8,128)S(1)}, f32[64,121]{1,0:T(8,128)S(1)}, f32[64,121]{1,0:T(8,128)S(1)}, s32[8,512]{1,0:T(8,128)S(1)}, s32[32,128]{1,0:T(8,128)S(...) custom-call(f32[64,3,128]{2,1,0:T(4,128)} %bitcast.13, f32[64,128]{1,0:T(8,128)} %bitcast.14, ...), custom_call_target="tpu_custom_call" | custom-call | tf_op jit(solution)/shard_map/prep/pallas_call | solution.py:345
  2.1 3.1 %collective-permute-start.1 = (f32[64,512]{1,0:T(8,128)S(1)}, f32[64,512]{1,0:T(8,128)S(1)}, u32[]{:S(2)}, u32[]{:S(2)}) collective-permute-start(f32[64,512]{1,0:T(8,128)S(1)} %get-tuple-element.28.own_ref), channel_id=1, source_target_pairs={{0,8},{1,9},{2,10},{3,11},{4,12},{5,13},{6,14},{7,15},{8,0},{9,1},... | collective-permute-start | bytes 393224 | tf_op jit(solution)/shard_map/ppermute | solution.py:419
  5.2 0.0 collective-permute-start
  5.2 0.5 %collective-permute-start.2 = (f32[64,121]{1,0:T(8,128)S(1)}, f32[64,121]{1,0:T(8,128)S(1)}, u32[]{:S(2)}, u32[]{:S(2)}) collective-permute-start(f32[64,121]{1,0:T(8,128)S(1)} %get-tuple-element.35), channel_id=1, source_target_pairs={{0,1},{1,0},{2,3},{3,2},{4,5},{5,4},{6,7},{7,6},{8,9},{9,8},{10,11... | collective-permute-start | bytes 92936 | tf_op jit(solution)/shard_map/ppermute | solution.py:390
  5.7 1.3 %counts.1 = (s32[4,8,128]{2,1,0:T(8,128)S(1)}, bf16[1024,256]{1,0:T(8,128)(2,1)S(1)}, f32[256,256]{1,0:T(8,128)S(1)}) custom-call(s32[8,512]{1,0:T(8,128)S(1)} %get-tuple-element.22.list_ref, f32[968,121]{1,0:T(8,128)S(1)} %get-tuple-element.23.operators_ref, s32[32,128]{1,0:T(8,128)S(1)} %get-tuple-element.24.source_ref, ...), custom_call_target="tpu_custom_call" | custom-call | tf_op jit(solution)/shard_map/counts/pallas_call | solution.py:370
  7.0 0.0 collective-permute-done.2.came_ref
  7.0 2.5 %collective-permute-start.3 = (f32[32,121]{1,0:T(8,128)S(1)}, f32[32,121]{1,0:T(8,128)S(1)}, u32[]{:S(2)}, u32[]{:S(2)}) collective-permute-start(f32[32,121]{1,0:T(8,128)S(1)} %get-tuple-element.37), channel_id=1, source_target_pairs={{0,6},{1,7},{2,4},{3,5},{4,2},{5,3},{6,0},{7,1},{8,14},{9,15},{10,... | collective-permute-start | bytes 46472 | tf_op jit(solution)/shard_map/ppermute | solution.py:400
  9.6 0.5 %collective-permute-start.4 = (f32[32,121]{1,0:T(8,128)S(1)}, f32[32,121]{1,0:T(8,128)S(1)}, u32[]{:S(2)}, u32[]{:S(2)}) collective-permute-start(f32[32,121]{1,0:T(8,128)S(1)} %get-tuple-element.38), channel_id=1, source_target_pairs={{0,2},{1,3},{2,0},{3,1},{4,6},{5,7},{6,4},{7,5},{8,10},{9,11},{10,... | collective-permute-start | bytes 46472 | tf_op jit(solution)/shard_map/ppermute | solution.py:400
  10.1 0.5 %collective-permute-start.5 = (f32[32,121]{1,0:T(8,128)S(1)}, f32[32,121]{1,0:T(8,128)S(1)}, u32[]{:S(2)}, u32[]{:S(2)}) collective-permute-start(f32[32,121]{1,0:T(8,128)S(1)} %get-tuple-element.39), channel_id=1, source_target_pairs={{0,4},{1,5},{2,6},{3,7},{4,0},{5,1},{6,2},{7,3},{8,12},{9,13},{10,... | collective-permute-start | bytes 46472 | tf_op jit(solution)/shard_map/ppermute | solution.py:400
  10.6 0.0 collective-permute-done.1.first_ref
  10.6 0.0 collective-permute-done.second_ref
  10.6 3.4 %near.1 = (f32[64,128]{1,0:T(8,128)S(1)}, bf16[512,1024]{1,0:T(8,128)(2,1)S(1)}, f32[8,256]{1,0:T(8,128)S(1)}) custom-call(f32[64,512]{1,0:T(8,128)S(1)} %collective-permute-done.second_ref, f32[64,512]{1,0:T(8,128)S(1)} %get-tuple-element.28.own_ref, f32[64,512]{1,0:T(8,128)S(1)} %collective-permute-done.1.first_ref, ...), custom_call_target="tpu_custom_call" | custom-call | tf_op jit(solution)/shard_map/near/pallas_call | solution.py:424
  14.0 0.0 collective-permute-done.3.refs_1_
  14.0 0.0 collective-permute-done.4.refs_2_
  14.0 0.0 collective-permute-done.5.refs_3_
  14.1 1.4 %far.1 = (f32[121,512]{1,0:T(8,128)}, f32[64,128]{1,0:T(8,128)}) custom-call(bf16[1024,256]{1,0:T(8,128)(2,1)S(1)} %get-tuple-element.27.parts_ref, bf16[512,1024]{1,0:T(8,128)(2,1)S(1)} %get-tuple-element.31.low_ref, f32[8,256]{1,0:T(8,128)S(1)} %get-tuple-element.32.peak_ref, s32[32,128]{1,0:T(8,128)S(1)} %get-tuple-element.24.source_ref, ...), custom_call_target="tpu_custom_call" | custom-call | tf_op jit(solution)/shard_map/far/pallas_call | solution.py:443
  (1 shorter events, 0.0 us)
Async XLA Ops:
  2.1 8.5 %collective-permute-start.1 = (f32[64,512]{1,0:T(8,128)S(1)}, f32[64,512]{1,0:T(8,128)S(1)}, u32[]{:S(2)}, u32[]{:S(2)}) collective-permute-start(f32[64,512]{1,0:T(8,128)S(1)} %get-tuple-element.28.own_ref), channel_id=1, source_target_pairs={{0,8},{1,9},{2,10},{3,11},{4,12},{5,13},{6,14},{7,15},{8,0},{9,1},... | collective-permute-start | bytes 393224 | tf_op jit(solution)/shard_map/ppermute | solution.py:419
  5.2 5.4 %collective-permute-start = (f32[64,512]{1,0:T(8,128)S(1)}, f32[64,512]{1,0:T(8,128)S(1)}, u32[]{:S(2)}, u32[]{:S(2)}) collective-permute-start(f32[64,512]{1,0:T(8,128)S(1)} %get-tuple-element.28.own_ref), channel_id=1, source_target_pairs={{0,1},{1,0},{2,3},{3,2},{4,5},{5,4},{6,7},{7,6},{8,16},{9,17},{10,... | collective-permute-start | bytes 393224 | tf_op jit(solution)/shard_map/ppermute | solution.py:419
  5.2 1.8 %collective-permute-start.2 = (f32[64,121]{1,0:T(8,128)S(1)}, f32[64,121]{1,0:T(8,128)S(1)}, u32[]{:S(2)}, u32[]{:S(2)}) collective-permute-start(f32[64,121]{1,0:T(8,128)S(1)} %get-tuple-element.35), channel_id=1, source_target_pairs={{0,1},{1,0},{2,3},{3,2},{4,5},{5,4},{6,7},{7,6},{8,9},{9,8},{10,11... | collective-permute-start | bytes 92936 | tf_op jit(solution)/shard_map/ppermute | solution.py:390
  7.0 7.0 %collective-permute-start.3 = (f32[32,121]{1,0:T(8,128)S(1)}, f32[32,121]{1,0:T(8,128)S(1)}, u32[]{:S(2)}, u32[]{:S(2)}) collective-permute-start(f32[32,121]{1,0:T(8,128)S(1)} %get-tuple-element.37), channel_id=1, source_target_pairs={{0,6},{1,7},{2,4},{3,5},{4,2},{5,3},{6,0},{7,1},{8,14},{9,15},{10,... | collective-permute-start | bytes 46472 | tf_op jit(solution)/shard_map/ppermute | solution.py:400
  9.6 4.5 %collective-permute-start.4 = (f32[32,121]{1,0:T(8,128)S(1)}, f32[32,121]{1,0:T(8,128)S(1)}, u32[]{:S(2)}, u32[]{:S(2)}) collective-permute-start(f32[32,121]{1,0:T(8,128)S(1)} %get-tuple-element.38), channel_id=1, source_target_pairs={{0,2},{1,3},{2,0},{3,1},{4,6},{5,7},{6,4},{7,5},{8,10},{9,11},{10,... | collective-permute-start | bytes 46472 | tf_op jit(solution)/shard_map/ppermute | solution.py:400
  10.1 4.0 %collective-permute-start.5 = (f32[32,121]{1,0:T(8,128)S(1)}, f32[32,121]{1,0:T(8,128)S(1)}, u32[]{:S(2)}, u32[]{:S(2)}) collective-permute-start(f32[32,121]{1,0:T(8,128)S(1)} %get-tuple-element.39), channel_id=1, source_target_pairs={{0,4},{1,5},{2,6},{3,7},{4,0},{5,1},{6,2},{7,3},{8,12},{9,13},{10,... | collective-permute-start | bytes 46472 | tf_op jit(solution)/shard_map/ppermute | solution.py:400

commit v18 on v17

--- a/solution.py
+++ b/solution.py
@@ -98,11 +98,10 @@
 
 
 def counts_kernel(
-    list_ref, operators_ref, source_ref, target_ref, operator_ref, place_ref, parts_ref, acc_ref,
-    wide_ref, code_ref, weight_ref, a_ref, b_ref, *, ops, sources,
+    list_ref, source_ref, target_ref, operator_ref, place_ref, acc_ref,
+    code_ref, weight_ref, a_ref, b_ref, *, sources,
 ):
     near, leaves = list_ref.shape
-    ncoef = operators_ref.shape[1]
     groups = leaves // LANES
     half, codes = acc_ref.shape
     _, block, chunk = a_ref.shape
@@ -141,13 +140,6 @@
             else:
                 acc_ref[:, first : first + block] += product
 
-    wide_ref[...] = pad_lanes(operators_ref[...])
-    for op in range(ops):
-        matrix = wide_ref[pl.ds(op, ncoef, stride=ops), :]
-        matrix = jnp.concatenate([matrix, jnp.zeros((LANES - ncoef, LANES), f32)], axis=0)
-        hi, lo = split(matrix)
-        parts_ref[LANES * spot(op, ops) : LANES * (spot(op, ops) + 1), :] = jnp.concatenate([hi, lo], axis=1)
-
 
 def spot(op, ops):
     return (op % 4) * (ops // 4) + op // 4
@@ -167,8 +159,8 @@
 
 
 def near_kernel(
-    second_ref, own_ref, first_ref, place_ref, acc_ref, near_ref, low_ref, peak_ref,
-    packed_ref, charge_ref, picked_ref, pot_ref,
+    second_ref, own_ref, first_ref, place_ref, acc_ref, operators_ref, near_ref, low_ref, peak_ref, parts_ref,
+    packed_ref, charge_ref, picked_ref, pot_ref, wide_ref, *, ops,
 ):
     groups, near, _ = place_ref.shape
     leaves = own_ref.shape[1]
@@ -212,7 +204,21 @@
             found.append(layer[0])
         return found
 
+    wide_ref[...] = pad_lanes(operators_ref[...])
+    ncoef = operators_ref.shape[1]
+    each = ops // groups
+
+    def cut(g):
+        for j in range(each):
+            place = each * g + j
+            op = 4 * lax.rem(place, ops // 4) + lax.div(place, ops // 4)
+            matrix = wide_ref[pl.ds(op, ncoef, stride=ops), :]
+            matrix = jnp.concatenate([matrix, jnp.zeros((LANES - ncoef, LANES), f32)], axis=0)
+            hi, lo = split(matrix)
+            parts_ref[pl.ds(pl.multiple_of(place * LANES, LANES), LANES), :] = jnp.concatenate([hi, lo], axis=1)
+
     def step(g, carry):
+        cut(g)
         at = pl.ds(pl.multiple_of(g * LANES, LANES), LANES)
         tx, ty, tz = (own_ref[PTS * c : PTS * (c + 1), at] * SCALE for c in range(3))
         square = tx * tx + ty * ty + (tz * tz + SOFT2 * SCALE * SCALE)
@@ -367,25 +373,23 @@
     block = min(codes, 512)
     groups = leaves // LANES
     chunk = entries // 4
-    places, parts, digits = pl.pallas_call(
-        functools.partial(counts_kernel, ops=ops, sources=sources),
+    places, digits = pl.pallas_call(
+        functools.partial(counts_kernel, sources=sources),
         name="counts",
         out_shape=(
             jax.ShapeDtypeStruct((groups, near, LANES), jnp.int32),
-            jax.ShapeDtypeStruct((ops * LANES, 2 * LANES), bf16),
             jax.ShapeDtypeStruct((leaves // 2, codes), f32),
         ),
-        in_specs=[VMEM] * 5,
-        out_specs=(VMEM,) * 3,
+        in_specs=[VMEM] * 4,
+        out_specs=(VMEM,) * 2,
         scratch_shapes=[
-            pltpu.VMEM((ncoef * ops, LANES), f32),
             pltpu.VMEM((2, entries // LANES, LANES), jnp.int32),
             pltpu.VMEM((2, entries // LANES, LANES), f32),
             pltpu.VMEM((2, block, chunk), bf16),
             pltpu.VMEM((2, leaves // 2, chunk), bf16),
         ],
         compiler_params=PARAMS,
-    )(near_list, operators, m2l_source, m2l_target, m2l_operator)
+    )(near_list, m2l_source, m2l_target, m2l_operator)
     if cap:
         came = lax.ppermute(other, "grp", [(i, i ^ 1) for i in range(peers)])
         joins = pl.pallas_call(
@@ -421,24 +425,26 @@
     first = exchange(0)
     second = exchange(1)
 
-    near_potential, low, peak = pl.pallas_call(
-        near_kernel,
+    near_potential, low, peak, parts = pl.pallas_call(
+        functools.partial(near_kernel, ops=ops),
         name="near",
         out_shape=(
             pltpu.VMEM((tiles, LANES), f32),
             jax.ShapeDtypeStruct((leaves, ops * sources), bf16),
             jax.ShapeDtypeStruct((8, codes), f32),
+            jax.ShapeDtypeStruct((ops * LANES, 2 * LANES), bf16),
         ),
-        in_specs=[VMEM] * 5,
-        out_specs=(VMEM,) * 3,
+        in_specs=[VMEM] * 6,
+        out_specs=(VMEM,) * 4,
         scratch_shapes=[
             pltpu.VMEM((2 * PTS, 3 * leaves), jnp.int32),
             pltpu.VMEM((PTS, 3 * leaves), f32),
             pltpu.VMEM((near, 5 * PTS, LANES), f32),
             pltpu.VMEM((groups, PTS, LANES), f32),
+            pltpu.VMEM((ncoef * ops, LANES), f32),
         ],
         compiler_params=PARAMS,
-    )(second, table, first, places, digits)
+    )(second, table, first, places, digits, operators)
 
     local_exp, near_potential = pl.pallas_call(
         functools.partial(far_kernel, ops=ops, cap=cap),

time: 15.6 us -> 15.7 us (level)
  no operation moved by 1% of the time
where the time goes in v18:
time: 15.7 us; the launch traced here: 15.5 us
  Pallas kernels  7.61 us (48%)
  starting transfers between devices  7.15 us (46%)
  between operations  0.69 us (4%)
    ppermute x3, starting transfers between devices, shards(): lax.ppermute(joins[m], 'grp', [(i, i ^ 2 * m) for i in range(peers)])  3.55 us
    pallas_call x1, Pallas kernels, shards(): pl.pallas_call(functools.partial(near_kernel, ops=ops), name='near', out_...  3.46 us
    ppermute x2, starting transfers between devices, exchange(): return lax.ppermute(table, ('slab', 'grp'), sorted(to.items()))  3.09 us
    pallas_call x1, Pallas kernels, shards(): pl.pallas_call(functools.partial(prep_kernel, others=len(others), cap=cap...  1.46 us
    pallas_call x1, Pallas kernels, shards(): pl.pallas_call(functools.partial(far_kernel, ops=ops, cap=cap), name='far...  1.44 us
    pallas_call x1, Pallas kernels, shards(): pl.pallas_call(functools.partial(counts_kernel, sources=sources), name='c...  1.24 us
    ppermute x1, starting transfers between devices, shards(): came = lax.ppermute(other, 'grp', [(i, i ^ 1) for i in range(peers)])  0.51 us
  transfers between devices with their start and end apart: 6, of which 0 were waited for; matrix products, arithmetic and copies ran while one was open for 0% of the time, Pallas kernels for 30%

profile of v18, /device:TPU:0, one launch (start us, length us, event | category | flops | bytes accessed | tf_op | source)
XLA Modules:
  0.0 15.5 jit_solution(16196058099492592152)
XLA Ops:
  0.6 1.5 %prep.1 = (f32[64,512]{1,0:T(8,128)S(1)}, f32[64,121]{1,0:T(8,128)S(1)}, f32[64,121]{1,0:T(8,128)S(1)}, s32[8,512]{1,0:T(8,128)S(1)}, s32[32,128]{1,0:T(8,128)S(...) custom-call(f32[64,3,128]{2,1,0:T(4,128)} %bitcast.13, f32[64,128]{1,0:T(8,128)} %bitcast.14, ...), custom_call_target="tpu_custom_call" | custom-call | tf_op jit(solution)/shard_map/prep/pallas_call | solution.py:351
  2.1 3.1 %collective-permute-start.1 = (f32[64,512]{1,0:T(8,128)S(1)}, f32[64,512]{1,0:T(8,128)S(1)}, u32[]{:S(2)}, u32[]{:S(2)}) collective-permute-start(f32[64,512]{1,0:T(8,128)S(1)} %get-tuple-element.22.own_ref), channel_id=1, source_target_pairs={{0,8},{1,9},{2,10},{3,11},{4,12},{5,13},{6,14},{7,15},{8,0},{9,1},... | collective-permute-start | bytes 393224 | tf_op jit(solution)/shard_map/ppermute | solution.py:423
  5.2 0.0 collective-permute-start
  5.2 0.5 %collective-permute-start.2 = (f32[64,121]{1,0:T(8,128)S(1)}, f32[64,121]{1,0:T(8,128)S(1)}, u32[]{:S(2)}, u32[]{:S(2)}) collective-permute-start(f32[64,121]{1,0:T(8,128)S(1)} %get-tuple-element.35), channel_id=1, source_target_pairs={{0,1},{1,0},{2,3},{3,2},{4,5},{5,4},{6,7},{7,6},{8,9},{9,8},{10,11... | collective-permute-start | bytes 92936 | tf_op jit(solution)/shard_map/ppermute | solution.py:394
  5.7 1.2 %counts.1 = (s32[4,8,128]{2,1,0:T(8,128)S(1)}, f32[256,256]{1,0:T(8,128)S(1)}) custom-call(s32[8,512]{1,0:T(8,128)S(1)} %get-tuple-element.23.list_ref, s32[32,128]{1,0:T(8,128)S(1)} %get-tuple-element.24.source_ref, s32[32,128]{1,0:T(8,128)S(1)} %get-tuple-element.25.target_ref, s32[32,128]{1,0:T(8,128)S(1)} %get-tuple-element.26.operator_ref), custom_call_target="tpu_custom_call" | custom-call | tf_op jit(solution)/shard_map/counts/pallas_call | solution.py:376
  6.9 0.0 collective-permute-done.2.came_ref
  7.0 2.5 %collective-permute-start.3 = (f32[32,121]{1,0:T(8,128)S(1)}, f32[32,121]{1,0:T(8,128)S(1)}, u32[]{:S(2)}, u32[]{:S(2)}) collective-permute-start(f32[32,121]{1,0:T(8,128)S(1)} %get-tuple-element.37), channel_id=1, source_target_pairs={{0,6},{1,7},{2,4},{3,5},{4,2},{5,3},{6,0},{7,1},{8,14},{9,15},{10,... | collective-permute-start | bytes 46472 | tf_op jit(solution)/shard_map/ppermute | solution.py:404
  9.5 0.5 %collective-permute-start.4 = (f32[32,121]{1,0:T(8,128)S(1)}, f32[32,121]{1,0:T(8,128)S(1)}, u32[]{:S(2)}, u32[]{:S(2)}) collective-permute-start(f32[32,121]{1,0:T(8,128)S(1)} %get-tuple-element.38), channel_id=1, source_target_pairs={{0,2},{1,3},{2,0},{3,1},{4,6},{5,7},{6,4},{7,5},{8,10},{9,11},{10,... | collective-permute-start | bytes 46472 | tf_op jit(solution)/shard_map/ppermute | solution.py:404
  10.0 0.5 %collective-permute-start.5 = (f32[32,121]{1,0:T(8,128)S(1)}, f32[32,121]{1,0:T(8,128)S(1)}, u32[]{:S(2)}, u32[]{:S(2)}) collective-permute-start(f32[32,121]{1,0:T(8,128)S(1)} %get-tuple-element.39), channel_id=1, source_target_pairs={{0,4},{1,5},{2,6},{3,7},{4,0},{5,1},{6,2},{7,3},{8,12},{9,13},{10,... | collective-permute-start | bytes 46472 | tf_op jit(solution)/shard_map/ppermute | solution.py:404
  10.5 0.0 collective-permute-done.1.first_ref
  10.5 0.0 collective-permute-done.second_ref
  10.5 3.5 %near.1 = (f32[64,128]{1,0:T(8,128)S(1)}, bf16[512,1024]{1,0:T(8,128)(2,1)S(1)}, f32[8,256]{1,0:T(8,128)S(1)}, bf16[1024,256]{1,0:T(8,128)(2,1)S(1)}) custom-call(f32[64,512]{1,0:T(8,128)S(1)} %collective-permute-done.second_ref, f32[64,512]{1,0:T(8,128)S(1)} %get-tuple-element.22.own_ref, f32[64,512]{1,0:T(8,128)S(1)} %collective-permute-done.1.first_ref, ...), custom_call_target="tpu_custom_call" | custom-call | tf_op jit(solution)/shard_map/near/pallas_call | solution.py:428
  14.0 0.0 collective-permute-done.3.refs_1_
  14.0 0.0 collective-permute-done.4.refs_2_
  14.1 0.0 collective-permute-done.5.refs_3_
  14.1 1.4 %far.1 = (f32[121,512]{1,0:T(8,128)}, f32[64,128]{1,0:T(8,128)}) custom-call(bf16[1024,256]{1,0:T(8,128)(2,1)S(1)} %get-tuple-element.30.parts_ref, bf16[512,1024]{1,0:T(8,128)(2,1)S(1)} %get-tuple-element.31.low_ref, f32[8,256]{1,0:T(8,128)S(1)} %get-tuple-element.32.peak_ref, s32[32,128]{1,0:T(8,128)S(1)} %get-tuple-element.24.source_ref, ...), custom_call_target="tpu_custom_call" | custom-call | tf_op jit(solution)/shard_map/far/pallas_call | solution.py:449
  (1 shorter events, 0.0 us)
Async XLA Ops:
  2.1 8.4 %collective-permute-start.1 = (f32[64,512]{1,0:T(8,128)S(1)}, f32[64,512]{1,0:T(8,128)S(1)}, u32[]{:S(2)}, u32[]{:S(2)}) collective-permute-start(f32[64,512]{1,0:T(8,128)S(1)} %get-tuple-element.22.own_ref), channel_id=1, source_target_pairs={{0,8},{1,9},{2,10},{3,11},{4,12},{5,13},{6,14},{7,15},{8,0},{9,1},... | collective-permute-start | bytes 393224 | tf_op jit(solution)/shard_map/ppermute | solution.py:423
  5.2 5.4 %collective-permute-start = (f32[64,512]{1,0:T(8,128)S(1)}, f32[64,512]{1,0:T(8,128)S(1)}, u32[]{:S(2)}, u32[]{:S(2)}) collective-permute-start(f32[64,512]{1,0:T(8,128)S(1)} %get-tuple-element.22.own_ref), channel_id=1, source_target_pairs={{0,1},{1,0},{2,3},{3,2},{4,5},{5,4},{6,7},{7,6},{8,16},{9,17},{10,... | collective-permute-start | bytes 393224 | tf_op jit(solution)/shard_map/ppermute | solution.py:423
  5.2 1.8 %collective-permute-start.2 = (f32[64,121]{1,0:T(8,128)S(1)}, f32[64,121]{1,0:T(8,128)S(1)}, u32[]{:S(2)}, u32[]{:S(2)}) collective-permute-start(f32[64,121]{1,0:T(8,128)S(1)} %get-tuple-element.35), channel_id=1, source_target_pairs={{0,1},{1,0},{2,3},{3,2},{4,5},{5,4},{6,7},{7,6},{8,9},{9,8},{10,11... | collective-permute-start | bytes 92936 | tf_op jit(solution)/shard_map/ppermute | solution.py:394
  7.0 7.1 %collective-permute-start.3 = (f32[32,121]{1,0:T(8,128)S(1)}, f32[32,121]{1,0:T(8,128)S(1)}, u32[]{:S(2)}, u32[]{:S(2)}) collective-permute-start(f32[32,121]{1,0:T(8,128)S(1)} %get-tuple-element.37), channel_id=1, source_target_pairs={{0,6},{1,7},{2,4},{3,5},{4,2},{5,3},{6,0},{7,1},{8,14},{9,15},{10,... | collective-permute-start | bytes 46472 | tf_op jit(solution)/shard_map/ppermute | solution.py:404
  9.5 4.5 %collective-permute-start.4 = (f32[32,121]{1,0:T(8,128)S(1)}, f32[32,121]{1,0:T(8,128)S(1)}, u32[]{:S(2)}, u32[]{:S(2)}) collective-permute-start(f32[32,121]{1,0:T(8,128)S(1)} %get-tuple-element.38), channel_id=1, source_target_pairs={{0,2},{1,3},{2,0},{3,1},{4,6},{5,7},{6,4},{7,5},{8,10},{9,11},{10,... | collective-permute-start | bytes 46472 | tf_op jit(solution)/shard_map/ppermute | solution.py:404
  10.0 4.0 %collective-permute-start.5 = (f32[32,121]{1,0:T(8,128)S(1)}, f32[32,121]{1,0:T(8,128)S(1)}, u32[]{:S(2)}, u32[]{:S(2)}) collective-permute-start(f32[32,121]{1,0:T(8,128)S(1)} %get-tuple-element.39), channel_id=1, source_target_pairs={{0,4},{1,5},{2,6},{3,7},{4,0},{5,1},{6,2},{7,3},{8,12},{9,13},{10,... | collective-permute-start | bytes 46472 | tf_op jit(solution)/shard_map/ppermute | solution.py:404

commit v19 on v18

--- a/solution.py
+++ b/solution.py
@@ -168,11 +168,14 @@
     f32 = jnp.float32
     value = acc_ref[...]
     peak_ref[...] = jnp.max(value.reshape(-1, 8, codes), axis=0)
-    value = value.astype(jnp.int32)
-    for digit in range(8):
-        h, d = digit // 4, digit % 4
-        here = (value >> (3 * digit)) & 7
-        low_ref[half * h : half * (h + 1), codes * d : codes * (d + 1)] = here.astype(f32).astype(jnp.bfloat16)
+
+    def digits(g):
+        value = acc_ref[...].astype(jnp.int32)
+        for j in range(8 // groups):
+            digit = 8 // groups * g + j
+            rows = pl.ds(pl.multiple_of(half * lax.div(digit, 4), half), half)
+            lanes = pl.ds(pl.multiple_of(codes * lax.rem(digit, 4), codes), codes)
+            low_ref[rows, lanes] = ((value >> (3 * digit)) & 7).astype(f32).astype(jnp.bfloat16)
 
     me = lax.axis_index("slab")
     last = lax.axis_size("slab") - 1
@@ -219,6 +222,7 @@
 
     def step(g, carry):
         cut(g)
+        digits(g)
         at = pl.ds(pl.multiple_of(g * LANES, LANES), LANES)
         tx, ty, tz = (own_ref[PTS * c : PTS * (c + 1), at] * SCALE for c in range(3))
         square = tx * tx + ty * ty + (tz * tz + SOFT2 * SCALE * SCALE)

time: 15.7 us -> 15.7 us (level)
  transfers between devices with their start and end apart: 6 -> 6, of which waited for: 0 -> 0; matrix products, arithmetic and copies ran while one was open for 0% -> 0% of each run, Pallas kernels for 30% -> 31%
where the time goes in v19:
time: 15.7 us; the launch traced here: 15.5 us
  Pallas kernels  7.63 us (49%)
  starting transfers between devices  7.15 us (46%)
  between operations  0.69 us (4%)
    ppermute x3, starting transfers between devices, shards(): lax.ppermute(joins[m], 'grp', [(i, i ^ 2 * m) for i in range(peers)])  3.55 us
    pallas_call x1, Pallas kernels, shards(): pl.pallas_call(functools.partial(near_kernel, ops=ops), name='near', out_...  3.48 us
    ppermute x2, starting transfers between devices, exchange(): return lax.ppermute(table, ('slab', 'grp'), sorted(to.items()))  3.09 us
    pallas_call x1, Pallas kernels, shards(): pl.pallas_call(functools.partial(prep_kernel, others=len(others), cap=cap...  1.46 us
    pallas_call x1, Pallas kernels, shards(): pl.pallas_call(functools.partial(far_kernel, ops=ops, cap=cap), name='far...  1.43 us
    pallas_call x1, Pallas kernels, shards(): pl.pallas_call(functools.partial(counts_kernel, sources=sources), name='c...  1.24 us
    ppermute x1, starting transfers between devices, shards(): came = lax.ppermute(other, 'grp', [(i, i ^ 1) for i in range(peers)])  0.51 us
  transfers between devices with their start and end apart: 6, of which 0 were waited for; matrix products, arithmetic and copies ran while one was open for 0% of the time, Pallas kernels for 31%

profile of v19, /device:TPU:0, one launch (start us, length us, event | category | flops | bytes accessed | tf_op | source)
XLA Modules:
  0.0 15.5 jit_solution(11467732553458121308)
XLA Ops:
  0.6 1.5 %prep.1 = (f32[64,512]{1,0:T(8,128)S(1)}, f32[64,121]{1,0:T(8,128)S(1)}, f32[64,121]{1,0:T(8,128)S(1)}, s32[8,512]{1,0:T(8,128)S(1)}, s32[32,128]{1,0:T(8,128)S(...) custom-call(f32[64,3,128]{2,1,0:T(4,128)} %bitcast.13, f32[64,128]{1,0:T(8,128)} %bitcast.14, ...), custom_call_target="tpu_custom_call" | custom-call | tf_op jit(solution)/shard_map/prep/pallas_call | solution.py:355
  2.1 3.1 %collective-permute-start.1 = (f32[64,512]{1,0:T(8,128)S(1)}, f32[64,512]{1,0:T(8,128)S(1)}, u32[]{:S(2)}, u32[]{:S(2)}) collective-permute-start(f32[64,512]{1,0:T(8,128)S(1)} %get-tuple-element.22.own_ref), channel_id=1, source_target_pairs={{0,8},{1,9},{2,10},{3,11},{4,12},{5,13},{6,14},{7,15},{8,0},{9,1},... | collective-permute-start | bytes 393224 | tf_op jit(solution)/shard_map/ppermute | solution.py:427
  5.2 0.0 collective-permute-start
  5.2 0.5 %collective-permute-start.2 = (f32[64,121]{1,0:T(8,128)S(1)}, f32[64,121]{1,0:T(8,128)S(1)}, u32[]{:S(2)}, u32[]{:S(2)}) collective-permute-start(f32[64,121]{1,0:T(8,128)S(1)} %get-tuple-element.35), channel_id=1, source_target_pairs={{0,1},{1,0},{2,3},{3,2},{4,5},{5,4},{6,7},{7,6},{8,9},{9,8},{10,11... | collective-permute-start | bytes 92936 | tf_op jit(solution)/shard_map/ppermute | solution.py:398
  5.7 1.2 %counts.1 = (s32[4,8,128]{2,1,0:T(8,128)S(1)}, f32[256,256]{1,0:T(8,128)S(1)}) custom-call(s32[8,512]{1,0:T(8,128)S(1)} %get-tuple-element.23.list_ref, s32[32,128]{1,0:T(8,128)S(1)} %get-tuple-element.24.source_ref, s32[32,128]{1,0:T(8,128)S(1)} %get-tuple-element.25.target_ref, s32[32,128]{1,0:T(8,128)S(1)} %get-tuple-element.26.operator_ref), custom_call_target="tpu_custom_call" | custom-call | tf_op jit(solution)/shard_map/counts/pallas_call | solution.py:380
  6.9 0.0 collective-permute-done.2.came_ref
  7.0 2.5 %collective-permute-start.3 = (f32[32,121]{1,0:T(8,128)S(1)}, f32[32,121]{1,0:T(8,128)S(1)}, u32[]{:S(2)}, u32[]{:S(2)}) collective-permute-start(f32[32,121]{1,0:T(8,128)S(1)} %get-tuple-element.37), channel_id=1, source_target_pairs={{0,6},{1,7},{2,4},{3,5},{4,2},{5,3},{6,0},{7,1},{8,14},{9,15},{10,... | collective-permute-start | bytes 46472 | tf_op jit(solution)/shard_map/ppermute | solution.py:408
  9.5 0.5 %collective-permute-start.4 = (f32[32,121]{1,0:T(8,128)S(1)}, f32[32,121]{1,0:T(8,128)S(1)}, u32[]{:S(2)}, u32[]{:S(2)}) collective-permute-start(f32[32,121]{1,0:T(8,128)S(1)} %get-tuple-element.38), channel_id=1, source_target_pairs={{0,2},{1,3},{2,0},{3,1},{4,6},{5,7},{6,4},{7,5},{8,10},{9,11},{10,... | collective-permute-start | bytes 46472 | tf_op jit(solution)/shard_map/ppermute | solution.py:408
  10.0 0.5 %collective-permute-start.5 = (f32[32,121]{1,0:T(8,128)S(1)}, f32[32,121]{1,0:T(8,128)S(1)}, u32[]{:S(2)}, u32[]{:S(2)}) collective-permute-start(f32[32,121]{1,0:T(8,128)S(1)} %get-tuple-element.39), channel_id=1, source_target_pairs={{0,4},{1,5},{2,6},{3,7},{4,0},{5,1},{6,2},{7,3},{8,12},{9,13},{10,... | collective-permute-start | bytes 46472 | tf_op jit(solution)/shard_map/ppermute | solution.py:408
  10.5 0.0 collective-permute-done.1.first_ref
  10.5 0.0 collective-permute-done.second_ref
  10.5 3.5 %near.1 = (f32[64,128]{1,0:T(8,128)S(1)}, bf16[512,1024]{1,0:T(8,128)(2,1)S(1)}, f32[8,256]{1,0:T(8,128)S(1)}, bf16[1024,256]{1,0:T(8,128)(2,1)S(1)}) custom-call(f32[64,512]{1,0:T(8,128)S(1)} %collective-permute-done.second_ref, f32[64,512]{1,0:T(8,128)S(1)} %get-tuple-element.22.own_ref, f32[64,512]{1,0:T(8,128)S(1)} %collective-permute-done.1.first_ref, ...), custom_call_target="tpu_custom_call" | custom-call | tf_op jit(solution)/shard_map/near/pallas_call | solution.py:432
  14.0 0.0 collective-permute-done.3.refs_1_
  14.1 0.0 collective-permute-done.4.refs_2_
  14.1 0.0 collective-permute-done.5.refs_3_
  14.1 1.4 %far.1 = (f32[121,512]{1,0:T(8,128)}, f32[64,128]{1,0:T(8,128)}) custom-call(bf16[1024,256]{1,0:T(8,128)(2,1)S(1)} %get-tuple-element.30.parts_ref, bf16[512,1024]{1,0:T(8,128)(2,1)S(1)} %get-tuple-element.31.low_ref, f32[8,256]{1,0:T(8,128)S(1)} %get-tuple-element.32.peak_ref, s32[32,128]{1,0:T(8,128)S(1)} %get-tuple-element.24.source_ref, ...), custom_call_target="tpu_custom_call" | custom-call | tf_op jit(solution)/shard_map/far/pallas_call | solution.py:453
  (1 shorter events, 0.0 us)
Async XLA Ops:
  2.1 8.4 %collective-permute-start.1 = (f32[64,512]{1,0:T(8,128)S(1)}, f32[64,512]{1,0:T(8,128)S(1)}, u32[]{:S(2)}, u32[]{:S(2)}) collective-permute-start(f32[64,512]{1,0:T(8,128)S(1)} %get-tuple-element.22.own_ref), channel_id=1, source_target_pairs={{0,8},{1,9},{2,10},{3,11},{4,12},{5,13},{6,14},{7,15},{8,0},{9,1},... | collective-permute-start | bytes 393224 | tf_op jit(solution)/shard_map/ppermute | solution.py:427
  5.2 5.4 %collective-permute-start = (f32[64,512]{1,0:T(8,128)S(1)}, f32[64,512]{1,0:T(8,128)S(1)}, u32[]{:S(2)}, u32[]{:S(2)}) collective-permute-start(f32[64,512]{1,0:T(8,128)S(1)} %get-tuple-element.22.own_ref), channel_id=1, source_target_pairs={{0,1},{1,0},{2,3},{3,2},{4,5},{5,4},{6,7},{7,6},{8,16},{9,17},{10,... | collective-permute-start | bytes 393224 | tf_op jit(solution)/shard_map/ppermute | solution.py:427
  5.2 1.8 %collective-permute-start.2 = (f32[64,121]{1,0:T(8,128)S(1)}, f32[64,121]{1,0:T(8,128)S(1)}, u32[]{:S(2)}, u32[]{:S(2)}) collective-permute-start(f32[64,121]{1,0:T(8,128)S(1)} %get-tuple-element.35), channel_id=1, source_target_pairs={{0,1},{1,0},{2,3},{3,2},{4,5},{5,4},{6,7},{7,6},{8,9},{9,8},{10,11... | collective-permute-start | bytes 92936 | tf_op jit(solution)/shard_map/ppermute | solution.py:398
  7.0 7.1 %collective-permute-start.3 = (f32[32,121]{1,0:T(8,128)S(1)}, f32[32,121]{1,0:T(8,128)S(1)}, u32[]{:S(2)}, u32[]{:S(2)}) collective-permute-start(f32[32,121]{1,0:T(8,128)S(1)} %get-tuple-element.37), channel_id=1, source_target_pairs={{0,6},{1,7},{2,4},{3,5},{4,2},{5,3},{6,0},{7,1},{8,14},{9,15},{10,... | collective-permute-start | bytes 46472 | tf_op jit(solution)/shard_map/ppermute | solution.py:408
  9.5 4.6 %collective-permute-start.4 = (f32[32,121]{1,0:T(8,128)S(1)}, f32[32,121]{1,0:T(8,128)S(1)}, u32[]{:S(2)}, u32[]{:S(2)}) collective-permute-start(f32[32,121]{1,0:T(8,128)S(1)} %get-tuple-element.38), channel_id=1, source_target_pairs={{0,2},{1,3},{2,0},{3,1},{4,6},{5,7},{6,4},{7,5},{8,10},{9,11},{10,... | collective-permute-start | bytes 46472 | tf_op jit(solution)/shard_map/ppermute | solution.py:408
  10.0 4.0 %collective-permute-start.5 = (f32[32,121]{1,0:T(8,128)S(1)}, f32[32,121]{1,0:T(8,128)S(1)}, u32[]{:S(2)}, u32[]{:S(2)}) collective-permute-start(f32[32,121]{1,0:T(8,128)S(1)} %get-tuple-element.39), channel_id=1, source_target_pairs={{0,4},{1,5},{2,6},{3,7},{4,0},{5,1},{6,2},{7,3},{8,12},{9,13},{10,... | collective-permute-start | bytes 46472 | tf_op jit(solution)/shard_map/ppermute | solution.py:408
